TPU v7x, 128 devices: a whole 4x4x4 slice. The times are simulated.
128 devices in a mesh: seq: 4 (over y), ctx: 32 (over z, x, core).
Axes of the slice: x: 4, y: 4, z: 4, core: 2. Of those that a mesh axis runs over, the one named last changes fastest.
Arguments:
- tokens: bfloat16 [4, 4096, 768], P('seq', 'ctx'), may hold values from -6 to 6
- cotangent: bfloat16 [4, 4096, 768], P('seq', 'ctx'), may hold values from -6 to 6
- block_map: int32 [32, 2], replicated, may hold values from 0 to 63, as said below
- ln1_gain: bfloat16 [768], P(('seq', 'ctx')), may hold values from 0.5 to 1.5
- ln1_bias: bfloat16 [768], P(('seq', 'ctx')), may hold values from -1.5 to 1.5
- w_qkv: bfloat16 [768, 2304], P(('seq', 'ctx')), may hold values from -0.3125 to 0.3125
- b_query: bfloat16 [768], P(('seq', 'ctx')), may hold values from -2.5 to 2.5
- b_value: bfloat16 [768], P(('seq', 'ctx')), may hold values from -2.5 to 2.5
- w_out: bfloat16 [768, 768], P(('seq', 'ctx')), may hold values from -0.875 to 0.875
- b_out: bfloat16 [768], P(('seq', 'ctx')), may hold values from -1.5 to 1.5
- ln2_gain: bfloat16 [768], P(('seq', 'ctx')), may hold values from 0.5 to 1.5
- ln2_bias: bfloat16 [768], P(('seq', 'ctx')), may hold values from -1.5 to 1.5
- w_fc1: bfloat16 [768, 3072], P(('seq', 'ctx')), may hold values from -0.21875 to 0.21875
- b_fc1: bfloat16 [3072], P(('seq', 'ctx')), may hold values from -2.5 to 2.5
- w_fc2: bfloat16 [3072, 768], P(('seq', 'ctx')), may hold values from -0.109375 to 0.109375
- b_fc2: bfloat16 [768], P(('seq', 'ctx')), may hold values from -1.5 to 1.5
Outputs:
- mixed: bfloat16 [4, 4096, 768], P('seq', 'ctx')
- grad_tokens: bfloat16 [4, 4096, 768], P('seq', 'ctx')
- grad_ln1_gain: float32 [768], P(('seq', 'ctx'))
- grad_ln1_bias: float32 [768], P(('seq', 'ctx'))
- grad_w_qkv: float32 [768, 2304], P(('seq', 'ctx'))
- grad_b_query: float32 [768], P(('seq', 'ctx'))
- grad_b_value: float32 [768], P(('seq', 'ctx'))
- grad_w_out: float32 [768, 768], P(('seq', 'ctx'))
- grad_b_out: float32 [768], P(('seq', 'ctx'))
- grad_ln2_gain: float32 [768], P(('seq', 'ctx'))
- grad_ln2_bias: float32 [768], P(('seq', 'ctx'))
- grad_w_fc1: float32 [768, 3072], P(('seq', 'ctx'))
- grad_b_fc1: float32 [3072], P(('seq', 'ctx'))
- grad_w_fc2: float32 [3072, 768], P(('seq', 'ctx'))
- grad_b_fc2: float32 [768], P(('seq', 'ctx'))
Inputs may be any that keep to these rules, and one draw needn't show every extreme that they name: `block_map`: row c names blocks p and 63 - p for some p; every p of 0 to 31 stands in exactly one row.
All inputs are finite; a program needn't handle non-finite values.
Results may differ from a plain program's by a relative error of at most 0.038.
Values may be sent and summed in bfloat16 or wider, within the bound.
No kernel may reach another device: no remote copies, remote signals or barrier semaphores. Data moves between devices by JAX's collectives and lax.ppermute only.
A program may use at most 128 MiB of HBM per device.

v0:
```python
import jax
import jax.numpy as jnp
from jax import lax
from jax.sharding import PartitionSpec as P

H = 12


norm_eps = 1e-05
masked_fill = -1e30


def layer_norm(values, gain, offset):
    row_mean = jnp.mean(values, -1, keepdims=True)
    centered = values - row_mean
    variance = jnp.mean(centered * centered, -1, keepdims=True)
    return centered * lax.rsqrt(variance + norm_eps) * gain + offset


def gelu_tanh(values):
    return jax.nn.gelu(values, approximate=True)


def positions(rows, block_span):
    rows = rows.reshape(-1)
    offsets = jnp.tile(jnp.arange(block_span, dtype=jnp.int32), rows.shape[0])
    return jnp.repeat(rows, block_span) * block_span + offsets


def masked_scores(query_block, key_block, query_pos, key_pos, score_scale):
    scores = (
        jnp.einsum("bqhd,bkhd->bhqk", query_block, key_block, preferred_element_type=jnp.float32)
        * score_scale
    )
    allowed = (query_pos[:, None] >= key_pos[None, :])[None, None]
    return (scores, allowed)


def grad_terms(
    query_block,
    key_block,
    value_block,
    dout_block,
    log_mass,
    row_delta,
    query_pos,
    key_pos,
    score_scale,
):
    scores, allowed = masked_scores(query_block, key_block, query_pos, key_pos, score_scale)
    probs = jnp.where(allowed, jnp.exp(scores - log_mass[..., None]), 0.0)
    weights = probs.astype(jnp.bfloat16)
    dprobs = jnp.einsum(
        "bqhd,bkhd->bhqk", dout_block, value_block, preferred_element_type=jnp.float32
    )
    dscore = (probs * (dprobs - row_delta[..., None])).astype(jnp.bfloat16)
    return (weights, dscore)


def per_device(
    tokens,
    cotangent,
    block_map,
    ln1_gain,
    ln1_bias,
    w_qkv,
    b_query,
    b_value,
    w_out,
    b_out,
    ln2_gain,
    ln2_bias,
    w_fc1,
    b_fc1,
    w_fc2,
    b_fc2,
):
    gathered = (
        lax.all_gather(ln1_gain, ("seq", "ctx"), axis=0, tiled=True),
        lax.all_gather(ln1_bias, ("seq", "ctx"), axis=0, tiled=True),
        lax.all_gather(w_qkv, ("seq", "ctx"), axis=0, tiled=True),
        lax.all_gather(b_query, ("seq", "ctx"), axis=0, tiled=True),
        lax.all_gather(b_value, ("seq", "ctx"), axis=0, tiled=True),
        lax.all_gather(w_out, ("seq", "ctx"), axis=0, tiled=True),
        lax.all_gather(b_out, ("seq", "ctx"), axis=0, tiled=True),
        lax.all_gather(ln2_gain, ("seq", "ctx"), axis=0, tiled=True),
        lax.all_gather(ln2_bias, ("seq", "ctx"), axis=0, tiled=True),
        lax.all_gather(w_fc1, ("seq", "ctx"), axis=0, tiled=True),
        lax.all_gather(b_fc1, ("seq", "ctx"), axis=0, tiled=True),
        lax.all_gather(w_fc2, ("seq", "ctx"), axis=0, tiled=True),
        lax.all_gather(b_fc2, ("seq", "ctx"), axis=0, tiled=True),
    )
    (
        gain_one,
        offset_one,
        full_qkv,
        query_bias,
        value_bias,
        full_out,
        out_bias,
        gain_two,
        offset_two,
        full_fc1,
        fc1_bias,
        full_fc2,
        fc2_bias,
    ) = gathered
    seq_count, rows_local, model_width = tokens.shape
    head_count = H
    head_size = model_width // head_count
    score_scale = head_size ** (-0.5)
    block_span = rows_local // 2
    ctx_index = lax.axis_index("ctx")
    own_rows = lax.dynamic_slice_in_dim(block_map, ctx_index, 1, 0)
    query_pos = positions(own_rows, block_span)
    key_pos = positions(block_map, block_span)
    shape_four = (seq_count, rows_local, head_count, head_size)
    token_rows = tokens.reshape(-1, model_width).astype(jnp.float32)
    normed, norm_one_back = jax.vjp(
        layer_norm, token_rows, gain_one.astype(jnp.float32), offset_one.astype(jnp.float32)
    )
    normed_low = normed.astype(jnp.bfloat16)
    qkv_bias = jnp.concatenate([query_bias, jnp.zeros_like(query_bias), value_bias]).astype(
        jnp.float32
    )
    qkv = (jnp.dot(normed_low, full_qkv, preferred_element_type=jnp.float32) + qkv_bias).astype(
        jnp.bfloat16
    )
    queries = qkv[:, :model_width].reshape(shape_four)
    key_rows = qkv[:, model_width : 2 * model_width].reshape(shape_four)
    values = qkv[:, 2 * model_width :].reshape(shape_four)
    keys_all, values_all = (
        lax.all_gather(key_rows, "ctx", axis=1, tiled=True),
        lax.all_gather(values, "ctx", axis=1, tiled=True),
    )
    total = keys_all.shape[1]
    key_span = min(512, total)
    block_starts = jnp.arange(total // key_span, dtype=jnp.int32) * key_span

    def max_step(carry, start):
        row_top, row_mass = carry
        key_block = lax.dynamic_slice_in_dim(keys_all, start, key_span, 1)
        block_pos = lax.dynamic_slice_in_dim(key_pos, start, key_span, 0)
        scores, allowed = masked_scores(queries, key_block, query_pos, block_pos, score_scale)
        scores = jnp.where(allowed, scores, masked_fill)
        new_top = jnp.maximum(row_top, jnp.max(scores, -1))
        row_mass = row_mass * jnp.exp(row_top - new_top) + jnp.sum(
            jnp.where(allowed, jnp.exp(scores - new_top[..., None]), 0.0), -1
        )
        return ((new_top, row_mass), None)

    start_top = jnp.full((seq_count, head_count, rows_local), masked_fill, jnp.float32)
    start_mass = jnp.zeros((seq_count, head_count, rows_local), jnp.float32)
    (row_top, row_mass), _ = lax.scan(max_step, (start_top, start_mass), block_starts)
    log_mass = row_top + jnp.log(row_mass)

    def out_step(acc, start):
        key_block = lax.dynamic_slice_in_dim(keys_all, start, key_span, 1)
        value_block = lax.dynamic_slice_in_dim(values_all, start, key_span, 1)
        block_pos = lax.dynamic_slice_in_dim(key_pos, start, key_span, 0)
        scores, allowed = masked_scores(queries, key_block, query_pos, block_pos, score_scale)
        weights = jnp.where(allowed, jnp.exp(scores - log_mass[..., None]), 0.0).astype(
            jnp.bfloat16
        )
        return (
            acc
            + jnp.einsum(
                "bhqk,bkhd->bqhd", weights, value_block, preferred_element_type=jnp.float32
            ),
            None,
        )

    attended, _ = lax.scan(out_step, jnp.zeros(shape_four, jnp.float32), block_starts)
    attended_low = attended.reshape(-1, model_width).astype(jnp.bfloat16)
    branch = jnp.dot(attended_low, full_out, preferred_element_type=jnp.float32) + out_bias.astype(
        jnp.float32
    )
    residual = token_rows + branch
    normed_two, norm_two_back = jax.vjp(
        layer_norm, residual, gain_two.astype(jnp.float32), offset_two.astype(jnp.float32)
    )
    normed_two_low = normed_two.astype(jnp.bfloat16)
    hidden_pre = jnp.dot(
        normed_two_low, full_fc1, preferred_element_type=jnp.float32
    ) + fc1_bias.astype(jnp.float32)
    hidden_act, gelu_back = jax.vjp(gelu_tanh, hidden_pre)
    hidden_low = hidden_act.astype(jnp.bfloat16)
    result = (
        residual
        + jnp.dot(hidden_low, full_fc2, preferred_element_type=jnp.float32)
        + fc2_bias.astype(jnp.float32)
    )
    mixed = result.astype(jnp.bfloat16).reshape(tokens.shape)
    grad_out_rows = cotangent.reshape(-1, model_width)
    grad_out_float = grad_out_rows.astype(jnp.float32)
    grad_fc2 = jnp.dot(hidden_low.T, grad_out_rows, preferred_element_type=jnp.float32)
    grad_fc2_bias = jnp.sum(grad_out_float, 0)
    grad_hidden = gelu_back(jnp.dot(grad_out_rows, full_fc2.T, preferred_element_type=jnp.float32))[
        0
    ].astype(jnp.bfloat16)
    grad_fc1 = jnp.dot(normed_two_low.T, grad_hidden, preferred_element_type=jnp.float32)
    grad_fc1_bias = jnp.sum(grad_hidden.astype(jnp.float32), 0)
    grad_resid_norm, grad_gain_two, grad_offset_two = norm_two_back(
        jnp.dot(grad_hidden, full_fc1.T, preferred_element_type=jnp.float32)
    )
    grad_resid = grad_out_float + grad_resid_norm
    grad_branch = grad_resid.astype(jnp.bfloat16)
    grad_out_proj = jnp.dot(attended_low.T, grad_branch, preferred_element_type=jnp.float32)
    grad_out_bias = jnp.sum(grad_branch.astype(jnp.float32), 0)
    grad_attended = (
        jnp.dot(grad_branch, full_out.T, preferred_element_type=jnp.float32)
        .astype(jnp.bfloat16)
        .reshape(shape_four)
    )
    row_delta = jnp.einsum("bqhd,bqhd->bhq", grad_attended.astype(jnp.float32), attended)

    def query_step(grad_queries, start):
        key_block = lax.dynamic_slice_in_dim(keys_all, start, key_span, 1)
        value_block = lax.dynamic_slice_in_dim(values_all, start, key_span, 1)
        block_pos = lax.dynamic_slice_in_dim(key_pos, start, key_span, 0)
        weights, dscore = grad_terms(
            queries,
            key_block,
            value_block,
            grad_attended,
            log_mass,
            row_delta,
            query_pos,
            block_pos,
            score_scale,
        )
        grad_queries = (
            grad_queries
            + jnp.einsum("bhqk,bkhd->bqhd", dscore, key_block, preferred_element_type=jnp.float32)
            * score_scale
        )
        return (grad_queries, (weights, dscore, key_block))

    def both_step(carry, start):
        grad_queries, grad_keys_all, grad_values_all = carry
        grad_queries, (weights, dscore, key_block) = query_step(grad_queries, start)
        key_part = (
            jnp.einsum("bhqk,bqhd->bkhd", dscore, queries, preferred_element_type=jnp.float32)
            * score_scale
        )
        value_part = jnp.einsum(
            "bhqk,bqhd->bkhd", weights, grad_attended, preferred_element_type=jnp.float32
        )
        grad_keys_all = lax.dynamic_update_slice_in_dim(grad_keys_all, key_part, start, 1)
        grad_values_all = lax.dynamic_update_slice_in_dim(grad_values_all, value_part, start, 1)
        return ((grad_queries, grad_keys_all, grad_values_all), None)

    whole_shape = (seq_count, total, head_count, head_size)
    (grad_queries, grad_keys_all, grad_values_all), _ = lax.scan(
        both_step,
        (
            jnp.zeros(shape_four, jnp.float32),
            jnp.zeros(whole_shape, jnp.float32),
            jnp.zeros(whole_shape, jnp.float32),
        ),
        block_starts,
    )
    grad_keys, grad_values = (
        lax.psum_scatter(
            grad_keys_all.astype(jnp.bfloat16), "ctx", scatter_dimension=1, tiled=True
        ).astype(jnp.float32),
        lax.psum_scatter(
            grad_values_all.astype(jnp.bfloat16), "ctx", scatter_dimension=1, tiled=True
        ).astype(jnp.float32),
    )
    grad_qkv = jnp.concatenate(
        [
            grad_queries.reshape(-1, model_width),
            grad_keys.reshape(-1, model_width),
            grad_values.reshape(-1, model_width),
        ],
        axis=1,
    ).astype(jnp.bfloat16)
    grad_qkv_proj = jnp.dot(normed_low.T, grad_qkv, preferred_element_type=jnp.float32)
    grad_qkv_float = grad_qkv.astype(jnp.float32)
    grad_query_bias = jnp.sum(grad_qkv_float[:, :model_width], 0)
    grad_value_bias = jnp.sum(grad_qkv_float[:, 2 * model_width :], 0)
    grad_rows_norm, grad_gain_one, grad_offset_one = norm_one_back(
        jnp.dot(grad_qkv, full_qkv.T, preferred_element_type=jnp.float32)
    )
    grad_tokens = (grad_resid + grad_rows_norm).astype(jnp.bfloat16).reshape(tokens.shape)
    summed = (
        lax.psum_scatter(grad_gain_one, ("seq", "ctx"), scatter_dimension=0, tiled=True),
        lax.psum_scatter(grad_offset_one, ("seq", "ctx"), scatter_dimension=0, tiled=True),
        lax.psum_scatter(grad_qkv_proj, ("seq", "ctx"), scatter_dimension=0, tiled=True),
        lax.psum_scatter(grad_query_bias, ("seq", "ctx"), scatter_dimension=0, tiled=True),
        lax.psum_scatter(grad_value_bias, ("seq", "ctx"), scatter_dimension=0, tiled=True),
        lax.psum_scatter(grad_out_proj, ("seq", "ctx"), scatter_dimension=0, tiled=True),
        lax.psum_scatter(grad_out_bias, ("seq", "ctx"), scatter_dimension=0, tiled=True),
        lax.psum_scatter(grad_gain_two, ("seq", "ctx"), scatter_dimension=0, tiled=True),
        lax.psum_scatter(grad_offset_two, ("seq", "ctx"), scatter_dimension=0, tiled=True),
        lax.psum_scatter(grad_fc1, ("seq", "ctx"), scatter_dimension=0, tiled=True),
        lax.psum_scatter(grad_fc1_bias, ("seq", "ctx"), scatter_dimension=0, tiled=True),
        lax.psum_scatter(grad_fc2, ("seq", "ctx"), scatter_dimension=0, tiled=True),
        lax.psum_scatter(grad_fc2_bias, ("seq", "ctx"), scatter_dimension=0, tiled=True),
    )
    return (
        mixed,
        grad_tokens,
        summed[0],
        summed[1],
        summed[2],
        summed[3],
        summed[4],
        summed[5],
        summed[6],
        summed[7],
        summed[8],
        summed[9],
        summed[10],
        summed[11],
        summed[12],
    )


def solution(mesh):
    in_specs = (
        P("seq", "ctx", None),
        P("seq", "ctx", None),
        P(),
        P(("seq", "ctx")),
        P(("seq", "ctx")),
        P(("seq", "ctx"), None),
        P(("seq", "ctx")),
        P(("seq", "ctx")),
        P(("seq", "ctx"), None),
        P(("seq", "ctx")),
        P(("seq", "ctx")),
        P(("seq", "ctx")),
        P(("seq", "ctx"), None),
        P(("seq", "ctx")),
        P(("seq", "ctx"), None),
        P(("seq", "ctx")),
    )
    out_specs = (
        P("seq", "ctx", None),
        P("seq", "ctx", None),
        P(("seq", "ctx")),
        P(("seq", "ctx")),
        P(("seq", "ctx"), None),
        P(("seq", "ctx")),
        P(("seq", "ctx")),
        P(("seq", "ctx"), None),
        P(("seq", "ctx")),
        P(("seq", "ctx")),
        P(("seq", "ctx")),
        P(("seq", "ctx"), None),
        P(("seq", "ctx")),
        P(("seq", "ctx"), None),
        P(("seq", "ctx")),
    )
    return jax.shard_map(
        per_device, mesh=mesh, in_specs=in_specs, out_specs=out_specs, check_vma=False
    )
```

profile of v0, /device:TPU:0, one launch (start us, length us, event | category | flops | bytes accessed | tf_op | source)
XLA Modules:
  0.0 1700.6 jit_solution(16672452959664277250)
XLA Ops:
  17.0 69.7 %all-reduce.25 = (bf16[768]{0:T(1024)(128)(2,1)S(1)}, bf16[768]{0:T(1024)(128)(2,1)S(1)}, bf16[768]{0:T(1024)(128)(2,1)S(1)}, bf16[768]{0:T(1024)(128)(2,1)S(1)}...) all-reduce(bf16[768]{0:T(1024)(128)(2,1)S(1)} %dynamic-update-slice, ...), channel_id=1, replica_groups=mesh['seq'=4,'ctx'=32] {'seq','ctx'}, use_global_device_ids=true, to_apply=%add.3 | all-reduce | flops 9216 | bytes 36864
  108.1 37.1 %all-gather.18.cloned.1.call-done = bf16[128,6,768]{2,1,0:T(8,128)(2,1)} async-done(((bf16[1,6,768]{2,1,0:T(8,128)(2,1)}), bf16[128,6,768]{2,1,0:T(8,128)(2,1)}) %all-gather.18.cloned.1.call-update) | async-done | bytes 1179664 | tf_op jit(solution)/shard_map/all_gather | solution.py:84
  148.6 65.4 %all-gather.20.cloned.1.call-done = bf16[128,6,3072]{2,1,0:T(8,128)(2,1)} async-done(((bf16[1,6,3072]{2,1,0:T(8,128)(2,1)}), bf16[128,6,3072]{2,1,0:T(8,128)(2,1)}) %all-gather.20.cloned.1.call-update) | async-done | bytes 4718608 | tf_op jit(solution)/shard_map/all_gather | solution.py:88
  221.7 46.4 %all-gather.12.cloned.1.call-done = bf16[1,4096,12,64]{1,3,2,0:T(8,128)(2,1)} async-done(((bf16[1,128,12,64]{1,3,2,0:T(8,128)(2,1)}), bf16[1,4096,12,64]{1,3,2,0:T(8,128)(2,1)}) %all-gather.12.cloned.1.call-update) | async-done | bytes 6291472 | tf_op jit(solution)/shard_map/all_gather | solution.py:133
  268.2 49.1 %while.39 = (s32[]{:T(128)}, f32[1,12,128]{2,1,0:T(8,128)S(1)}, f32[1,12,128]{2,1,0:T(8,128)S(1)}, s32[8]{0:T(128)S(1)}, s32[4096]{0:T(1024)S(1)}, /*index=5*/bf...) while((s32[]{:T(128)}, f32[1,12,128]{2,1,0:T(8,128)S(1)}, ...), condition=%wide.region_5.6_spmd.clone, body=%wide.region_2.5_spmd.clone.sunk | while | flops 107028096 | bytes 7559358 | solution.py:154
  324.8 71.5 %while.40 = (s32[]{:T(128)}, f32[1,128,12,64]{1,3,2,0:T(8,128)}, s32[8]{0:T(128)}, bf16[1,4096,12,64]{1,3,2,0:T(8,128)(2,1)}, s32[4096]{0:T(1024)}, /*index=5*/b...) while((s32[]{:T(128)}, f32[1,128,12,64]{1,3,2,0:T(8,128)}, ...), condition=%wide.region_7.8_spmd.clone, body=%wide.region_6.7_spmd.clone.sunk | while | flops 204734592 | bytes 2703040 | solution.py:173
  421.7 256.9 %while.41 = (s32[]{:T(128)}, f32[1,128,12,64]{1,3,2,0:T(8,128)S(1)}, bf16[1,4096,12,64]{1,3,2,0:T(8,128)(2,1)}, bf16[1,4096,12,64]{1,3,2,0:T(8,128)(2,1)}, s32[8...) while((s32[]{:T(128)}, ...), condition=%wide.region_13.14_spmd.clone, body=%wide.region_12.13_spmd.clone.sunk | while | flops 512327808 | bytes 24939148 | solution.py:254
  435.6 7.9 dynamic_update_slice.10
  446.2 7.9 dynamic_update_slice.11
  467.9 7.9 dynamic_update_slice.10
  478.5 7.9 dynamic_update_slice.11
  500.2 7.9 dynamic_update_slice.10
  510.8 7.9 dynamic_update_slice.11
  532.5 7.9 dynamic_update_slice.10
  543.2 7.9 dynamic_update_slice.11
  575.5 7.9 dynamic_update_slice.11
  597.1 7.9 dynamic_update_slice.10
  607.8 7.9 dynamic_update_slice.11
  629.4 7.9 dynamic_update_slice.10
  640.1 7.9 dynamic_update_slice.11
  678.5 19.3 %copy.76 = bf16[1,4096,12,64]{3,2,0,1:T(8,128)(2,1)} copy(bf16[1,4096,12,64]{1,3,2,0:T(8,128)(2,1)} %get-tuple-element.977) | data formatting | bytes 12582912
  697.8 20.7 %reshape.394 = bf16[4096,768]{1,0:T(8,128)(2,1)} reshape(bf16[4096,1,12,64]{3,2,1,0:T(8,128)(2,1)} %bitcast.267) | data formatting | bytes 12582912
  718.6 19.4 %copy.74 = bf16[1,4096,12,64]{3,2,0,1:T(8,128)(2,1)} copy(bf16[1,4096,12,64]{1,3,2,0:T(8,128)(2,1)} %get-tuple-element.976) | data formatting | bytes 12582912
  738.0 21.0 %reshape.392 = bf16[4096,768]{1,0:T(8,128)(2,1)} reshape(bf16[4096,1,12,64]{3,2,1,0:T(8,128)(2,1)} %bitcast.268) | data formatting | bytes 12582912
  773.2 31.4 %reduce-scatter.18.cloned.1.call-done = bf16[128,768]{1,0:T(8,128)(2,1)} async-done(((bf16[4096,768]{1,0:T(8,128)(2,1)}), bf16[128,768]{1,0:T(8,128)(2,1)}) %reduce-scatter.18.cloned.1.call-update) | async-done | bytes 196624
  806.9 87.4 %reduce-scatter.16.cloned.1.call-done = bf16[128,768]{1,0:T(8,128)(2,1)} async-done(((bf16[4096,768]{1,0:T(8,128)(2,1)}), bf16[128,768]{1,0:T(8,128)(2,1)}) %reduce-scatter.16.cloned.1.call-update) | async-done | bytes 196624
  901.9 369.3 %fusion.103 = (f32[8,2304]{1,0:T(8,128)}, f32[8,768]{1,0:T(8,128)S(1)}, f32[8,3072]{1,0:T(8,128)}) fusion(f32[768,2304]{1,0:T(8,128)} %fusion.95, f32[768,768]{1,0:T(8,128)S(1)} %fusion.108, f32[768,3072]{1,0:T(8,128)} %fusion.101), kind=kCustom, calls=%all-reduce-scatter.3 | all-reduce-scatter fusion | flops 6291457 | bytes 19070976
  1282.9 14.3 collective-permute-start.54
  1499.9 8.4 collective-permute-start.78
  1517.9 65.6 %all-reduce.24 = (f32[768]{0:T(1024)S(1)}, f32[768]{0:T(1024)S(1)}, f32[768]{0:T(1024)S(1)}, f32[768]{0:T(1024)S(1)}, f32[768]{0:T(1024)S(1)}, /*index=5*/f32[76...) all-reduce(f32[768]{0:T(1024)S(1)} %get-tuple-element.331, ...), channel_id=4, replica_groups=mesh['seq'=4,'ctx'=32] {'seq','ctx'}, use_global_device_ids=true, to_apply=%region_19.20.clone | all-reduce | flops 9216 | bytes 73728
  1611.7 33.5 %concatenate.13 = f32[262,2304]{1,0:T(8,128)S(1)} concatenate(f32[6,2304]{1,0:T(8,128)} %copy-done.60, f32[8,2304]{1,0:T(8,128)} %copy-done.57, f32[8,2304]{1,0:T(8,128)} %copy-done.58, f32[8,2304]{1,0:T(8,128)} %copy-done.59, f32[8,2304]{1,0:T(8,128)} %copy-done.61, f32[8,2304]{1,0:T(8,128)} %copy-done.62, f32[8,2304]{1,0:T(8,128)} %copy-done.63, ...), dimensions={0} | concatenate | bytes 4829184
  1661.8 31.5 %concatenate.15 = f32[262,3072]{1,0:T(8,128)S(1)} concatenate(f32[6,3072]{1,0:T(8,128)} %copy-done.30, f32[8,3072]{1,0:T(8,128)} %copy-done.29, f32[8,3072]{1,0:T(8,128)} %copy-done.31, f32[8,3072]{1,0:T(8,128)} %copy-done.32, f32[8,3072]{1,0:T(8,128)} %copy-done.33, f32[8,3072]{1,0:T(8,128)} %copy-done.34, f32[8,3072]{1,0:T(8,128)} %copy-done.35, f32[8,3072]{1,0:T(8,128)S(1)} %copy-done.37, ...), dimensions={0} | concatenate | bytes 6438912
  (868 shorter events, 592.3 us)
Async XLA Ops:
  7.2 82.9 %all-gather.16.cloned.1.call-start = ((), (), s32[]{:S(2)}) async-start(), calls=%async_computation.7 | async-start | bytes 4755456 | tf_op jit(solution)/shard_map/all_gather | solution.py:81
  7.9 137.3 %all-gather.18.cloned.1.call-start = ((), (), s32[]{:S(2)}) async-start(), calls=%async_computation.8 | async-start | bytes 1585152 | tf_op jit(solution)/shard_map/all_gather | solution.py:84
  8.7 205.3 %all-gather.20.cloned.1.call-start = ((), (), s32[]{:S(2)}) async-start(), calls=%async_computation.9 | async-start | bytes 6340608 | tf_op jit(solution)/shard_map/all_gather | solution.py:88
  9.4 258.8 %all-gather.12.cloned.1.call-start = ((), (), s32[]{:S(2)}) async-start(), calls=%async_computation.4 | async-start | bytes 6488064 | tf_op jit(solution)/shard_map/all_gather | solution.py:133
  99.6 225.2 %all-gather.10.cloned.1.call-start = ((), (), s32[]{:S(2)}) async-start(), calls=%async_computation.3 | async-start | bytes 6488064 | tf_op jit(solution)/shard_map/all_gather | solution.py:134
  101.4 301.2 %all-gather.14.cloned.1.call-start = ((), (), s32[]{:S(2)}) async-start(), calls=%async_computation.5 | async-start | bytes 4755456 | tf_op jit(solution)/shard_map/all_gather | solution.py:90
  102.0 702.6 %reduce-scatter.18.cloned.1.call-start = ((), (), s32[]{:S(2)}) async-start(), calls=%async_computation.11 | async-start | bytes 6488064
  718.6 175.7 %reduce-scatter.16.cloned.1.call-start = ((), (), s32[]{:S(2)}) async-start(), calls=%async_computation.10 | async-start | bytes 6488064
  759.1 934.8 %reduce-scatter.14.cloned.1.call-start = ((), (), s32[]{:S(2)}) async-start(), calls=%async_computation.6 | async-start | bytes 9510912 | tf_op jit(solution)/shard_map/reduce_scatter | solution.py:299
  1277.7 19.5 %collective-permute-start.58 = (f32[8,768]{1,0:T(8,128)S(1)}, f32[8,768]{1,0:T(8,128)S(1)}, u32[]{:S(2)}, u32[]{:S(2)}) collective-permute-start(f32[8,768]{1,0:T(8,128)S(1)} %get-tuple-element.418), channel_id=1, source_target_pairs={{0,27},{1,28},{2,29},{3,30},{4,31},{5,32},{6,33},{7,34},{8,35},{9,... | collective-permute-start | bytes 73736
  1279.0 21.0 %collective-permute-start.57 = (f32[8,768]{1,0:T(8,128)S(1)}, f32[8,768]{1,0:T(8,128)S(1)}, u32[]{:S(2)}, u32[]{:S(2)}) collective-permute-start(f32[8,768]{1,0:T(8,128)S(1)} %get-tuple-element.418), channel_id=1, source_target_pairs={{0,26},{1,27},{2,28},{3,29},{4,30},{5,31},{6,32},{7,33},{8,34},{9,... | collective-permute-start | bytes 73736
  1280.3 21.0 %collective-permute-start.56 = (f32[8,768]{1,0:T(8,128)S(1)}, f32[8,768]{1,0:T(8,128)S(1)}, u32[]{:S(2)}, u32[]{:S(2)}) collective-permute-start(f32[8,768]{1,0:T(8,128)S(1)} %get-tuple-element.418), channel_id=1, source_target_pairs={{0,25},{1,26},{2,27},{3,28},{4,29},{5,30},{6,31},{7,32},{8,33},{9,... | collective-permute-start | bytes 73736
  1281.6 22.9 %collective-permute-start.55 = (f32[8,768]{1,0:T(8,128)S(1)}, f32[8,768]{1,0:T(8,128)S(1)}, u32[]{:S(2)}, u32[]{:S(2)}) collective-permute-start(f32[8,768]{1,0:T(8,128)S(1)} %get-tuple-element.418), channel_id=1, source_target_pairs={{0,24},{1,25},{2,26},{3,27},{4,28},{5,29},{6,30},{7,31},{8,32},{9,... | collective-permute-start | bytes 73736
  1282.9 22.9 %collective-permute-start.54 = (f32[8,768]{1,0:T(8,128)S(1)}, f32[8,768]{1,0:T(8,128)S(1)}, u32[]{:S(2)}, u32[]{:S(2)}) collective-permute-start(f32[8,768]{1,0:T(8,128)S(1)} %get-tuple-element.418), channel_id=1, source_target_pairs={{0,23},{1,24},{2,25},{3,26},{4,27},{5,28},{6,29},{7,30},{8,31},{9,... | collective-permute-start | bytes 73736
  1349.2 21.0 %collective-permute-start.30 = (f32[8,2304]{1,0:T(8,128)}, f32[8,2304]{1,0:T(8,128)S(1)}, u32[]{:S(2)}, u32[]{:S(2)}) collective-permute-start(f32[8,2304]{1,0:T(8,128)} %get-tuple-element.417), channel_id=1, source_target_pairs={{0,31},{1,32},{2,33},{3,34},{4,35},{5,36},{6,37},{7,38},{8,39},{9,... | collective-permute-start | bytes 221192
  1350.5 21.1 %collective-permute-start.29 = (f32[8,2304]{1,0:T(8,128)}, f32[8,2304]{1,0:T(8,128)S(1)}, u32[]{:S(2)}, u32[]{:S(2)}) collective-permute-start(f32[8,2304]{1,0:T(8,128)} %get-tuple-element.417), channel_id=1, source_target_pairs={{0,30},{1,31},{2,32},{3,33},{4,34},{5,35},{6,36},{7,37},{8,38},{9,... | collective-permute-start | bytes 221192
  1352.2 21.4 %collective-permute-start.28 = (f32[8,2304]{1,0:T(8,128)}, f32[8,2304]{1,0:T(8,128)S(1)}, u32[]{:S(2)}, u32[]{:S(2)}) collective-permute-start(f32[8,2304]{1,0:T(8,128)} %get-tuple-element.417), channel_id=1, source_target_pairs={{0,29},{1,30},{2,31},{3,32},{4,33},{5,34},{6,35},{7,36},{8,37},{9,... | collective-permute-start | bytes 221192
  1399.3 19.2 %collective-permute-start.15 = (f32[8,2304]{1,0:T(8,128)}, f32[8,2304]{1,0:T(8,128)S(1)}, u32[]{:S(2)}, u32[]{:S(2)}) collective-permute-start(f32[8,2304]{1,0:T(8,128)} %get-tuple-element.417), channel_id=1, source_target_pairs={{0,16},{1,17},{2,18},{3,19},{4,20},{5,21},{6,22},{7,23},{8,24},{9,... | collective-permute-start | bytes 221192
  1400.6 19.2 %collective-permute-start.14 = (f32[8,2304]{1,0:T(8,128)}, f32[8,2304]{1,0:T(8,128)S(1)}, u32[]{:S(2)}, u32[]{:S(2)}) collective-permute-start(f32[8,2304]{1,0:T(8,128)} %get-tuple-element.417), channel_id=1, source_target_pairs={{0,15},{1,16},{2,17},{3,18},{4,19},{5,20},{6,21},{7,22},{8,23},{9,... | collective-permute-start | bytes 221192
  1485.0 23.3 %collective-permute-start.82 = (f32[8,3072]{1,0:T(8,128)S(1)}, f32[8,3072]{1,0:T(8,128)S(1)}, u32[]{:S(2)}, u32[]{:S(2)}) collective-permute-start(f32[8,3072]{1,0:T(8,128)S(1)} %copy-done.21), channel_id=1, source_target_pairs={{0,19},{1,20},{2,21},{3,22},{4,23},{5,24},{6,25},{7,26},{8,27},{9,... | collective-permute-start | bytes 294920
  1486.9 22.7 %collective-permute-start.81 = (f32[8,3072]{1,0:T(8,128)S(1)}, f32[8,3072]{1,0:T(8,128)S(1)}, u32[]{:S(2)}, u32[]{:S(2)}) collective-permute-start(f32[8,3072]{1,0:T(8,128)S(1)} %copy-done.21), channel_id=1, source_target_pairs={{0,18},{1,19},{2,20},{3,21},{4,22},{5,23},{6,24},{7,25},{8,26},{9,... | collective-permute-start | bytes 294920
  1490.6 20.3 %collective-permute-start.80 = (f32[8,3072]{1,0:T(8,128)S(1)}, f32[8,3072]{1,0:T(8,128)S(1)}, u32[]{:S(2)}, u32[]{:S(2)}) collective-permute-start(f32[8,3072]{1,0:T(8,128)S(1)} %copy-done.21), channel_id=1, source_target_pairs={{0,17},{1,18},{2,19},{3,20},{4,21},{5,22},{6,23},{7,24},{8,25},{9,... | collective-permute-start | bytes 294920
  1499.9 92.3 %collective-permute-start.78 = (f32[8,3072]{1,0:T(8,128)S(1)}, f32[8,3072]{1,0:T(8,128)S(1)}, u32[]{:S(2)}, u32[]{:S(2)}) collective-permute-start(f32[8,3072]{1,0:T(8,128)S(1)} %copy-done.21), channel_id=1, source_target_pairs={{0,15},{1,16},{2,17},{3,18},{4,19},{5,20},{6,21},{7,22},{8,23},{9,... | collective-permute-start | bytes 294920
  1508.3 87.1 %collective-permute-start.77 = (f32[8,3072]{1,0:T(8,128)S(1)}, f32[8,3072]{1,0:T(8,128)S(1)}, u32[]{:S(2)}, u32[]{:S(2)}) collective-permute-start(f32[8,3072]{1,0:T(8,128)S(1)} %copy-done.21), channel_id=1, source_target_pairs={{0,14},{1,15},{2,16},{3,17},{4,18},{5,19},{6,20},{7,21},{8,22},{9,... | collective-permute-start | bytes 294920
  1509.6 88.9 %collective-permute-start.76 = (f32[8,3072]{1,0:T(8,128)S(1)}, f32[8,3072]{1,0:T(8,128)S(1)}, u32[]{:S(2)}, u32[]{:S(2)}) collective-permute-start(f32[8,3072]{1,0:T(8,128)S(1)} %copy-done.21), channel_id=1, source_target_pairs={{0,13},{1,14},{2,15},{3,16},{4,17},{5,18},{6,19},{7,20},{8,21},{9,... | collective-permute-start | bytes 294920
  1511.0 90.3 %collective-permute-start.75 = (f32[8,3072]{1,0:T(8,128)S(1)}, f32[8,3072]{1,0:T(8,128)S(1)}, u32[]{:S(2)}, u32[]{:S(2)}) collective-permute-start(f32[8,3072]{1,0:T(8,128)S(1)} %copy-done.21), channel_id=1, source_target_pairs={{0,12},{1,13},{2,14},{3,15},{4,16},{5,17},{6,18},{7,19},{8,20},{9,... | collective-permute-start | bytes 294920
  1512.5 94.5 %collective-permute-start.74 = (f32[8,3072]{1,0:T(8,128)S(1)}, f32[8,3072]{1,0:T(8,128)S(1)}, u32[]{:S(2)}, u32[]{:S(2)}) collective-permute-start(f32[8,3072]{1,0:T(8,128)S(1)} %copy-done.21), channel_id=1, source_target_pairs={{0,11},{1,12},{2,13},{3,14},{4,15},{5,16},{6,17},{7,18},{8,19},{9,... | collective-permute-start | bytes 294920
  1592.2 53.2 %collective-permute-start.73 = (f32[8,3072]{1,0:T(8,128)S(1)}, f32[8,3072]{1,0:T(8,128)}, u32[]{:S(2)}, u32[]{:S(2)}) collective-permute-start(f32[8,3072]{1,0:T(8,128)S(1)} %copy-done.21), channel_id=1, source_target_pairs={{0,10},{1,11},{2,12},{3,13},{4,14},{5,15},{6,16},{7,17},{8,18},{9,... | collective-permute-start | bytes 294920
  1595.4 51.2 %collective-permute-start.72 = (f32[8,3072]{1,0:T(8,128)S(1)}, f32[8,3072]{1,0:T(8,128)}, u32[]{:S(2)}, u32[]{:S(2)}) collective-permute-start(f32[8,3072]{1,0:T(8,128)S(1)} %copy-done.21), channel_id=1, source_target_pairs={{0,9},{1,10},{2,11},{3,12},{4,13},{5,14},{6,15},{7,16},{8,17},{9,1... | collective-permute-start | bytes 294920
  1598.5 52.6 %collective-permute-start.71 = (f32[8,3072]{1,0:T(8,128)S(1)}, f32[8,3072]{1,0:T(8,128)}, u32[]{:S(2)}, u32[]{:S(2)}) collective-permute-start(f32[8,3072]{1,0:T(8,128)S(1)} %copy-done.21), channel_id=1, source_target_pairs={{0,8},{1,9},{2,10},{3,11},{4,12},{5,13},{6,14},{7,15},{8,16},{9,17... | collective-permute-start | bytes 294920
  1601.3 51.2 %collective-permute-start.70 = (f32[8,3072]{1,0:T(8,128)S(1)}, f32[8,3072]{1,0:T(8,128)}, u32[]{:S(2)}, u32[]{:S(2)}) collective-permute-start(f32[8,3072]{1,0:T(8,128)S(1)} %copy-done.21), channel_id=1, source_target_pairs={{0,7},{1,8},{2,9},{3,10},{4,11},{5,12},{6,13},{7,14},{8,15},{9,16}... | collective-permute-start | bytes 294920
  1607.0 49.1 %collective-permute-start.69 = (f32[8,3072]{1,0:T(8,128)S(1)}, f32[8,3072]{1,0:T(8,128)}, u32[]{:S(2)}, u32[]{:S(2)}) collective-permute-start(f32[8,3072]{1,0:T(8,128)S(1)} %copy-done.21), channel_id=1, source_target_pairs={{0,6},{1,7},{2,8},{3,9},{4,10},{5,11},{6,12},{7,13},{8,14},{9,15},... | collective-permute-start | bytes 294920
  (245 other events, 6489.5 us)
Sparse Core Ops, SparseCore 0:
  11.0 69.5 all-gather.15
  83.5 61.6 all-gather.17
  148.3 65.6 all-gather.19
  216.0 52.1 all-gather.11
  270.8 54.0 all-gather.9
  327.7 66.6 all-gather.13
  718.7 85.8 reduce-scatter.17
  808.8 85.4 reduce-scatter.15
  899.9 222.8 reduce-scatter.13
where the time goes:
time: 1720 us; the launch traced here: 1700 us
  blocking collectives  505 us (29%)
  local copies, waits for them, and re-layouts  360 us (21%)
  waiting for transfers between devices  286 us (17%)
  starting transfers between devices  262 us (15%)
  matrix products  194 us (11%)
  loops' own time  48.5 us (3%)
  other arithmetic  29.3 us (2%)
    unnamed x3, blocking collectives  505 us
    unnamed x98, starting transfers between devices  261 us
    unnamed x264, local copies, waits for them, and re-layouts  189 us
    unnamed x107, waiting for transfers between devices  129 us
    all_gather x1, waiting for transfers between devices, per_device(): lax.all_gather(w_fc1, ('seq', 'ctx'), axis=0, tiled=True)  65.4 us
    dynamic_update_slice x8, local copies, waits for them, and re-layouts, both_step(): lax.dynamic_update_slice_in_dim(grad_values_all, value_part, start, 1)  62.4 us
    dynamic_update_slice x8, local copies, waits for them, and re-layouts, both_step(): lax.dynamic_update_slice_in_dim(grad_keys_all, key_part, start, 1)  62.2 us
    dot_general x16, matrix products, masked_scores(): jnp.einsum('bqhd,bkhd->bhqk', query_block, key_block, preferred_element_t...  51.7 us
  transfers between devices with their start and end apart: 105, of which 9 were waited for; matrix products, arithmetic and copies ran while one was open for 38% of the time, Pallas kernels for 0%

commit v1 on v0

v1 whole, which is shorter than its diff:
```python
import jax
import jax.numpy as jnp
import numpy as np
from jax import lax
from jax.experimental import pallas as pl
from jax.experimental.pallas import tpu as pltpu
from jax.sharding import Mesh, PartitionSpec as P

D = 768
H = 12
HD = 64
FF = 3072
BLK = 64
TP = 4
HL = H // TP
HW = HL * HD
TOK = 128
ROWS = TOK * TP
KEYS = 4096
CHUNK = 512
EPS = 1e-05
MASKED = -1e30
LOG2E = 1.4426950408889634
SCALE = HD**-0.5
BF = jnp.bfloat16
F32 = jnp.float32
G = ("c", "y", "z")


def natural_feature(i):
    c, y, z, x, r = i // 384, (i // 96) % 4, (i // 24) % 4, (i // 6) % 4, i % 6
    return y * 192 + z * 48 + x * 12 + c * 6 + r


def feature_matrix():
    out = np.zeros((D, D), np.float32)
    i = np.arange(D)
    out[natural_feature(i), i] = 1
    return out.astype(jnp.bfloat16)


def head_matrix():
    out = np.zeros((3 * HW, 6 * 2 * HD), np.float32)
    for h in range(HL):
        for d in range(HD):
            out[HW + h * HD + d, h * 128 + d] = 1
            out[2 * HW + h * HD + d, h * 128 + HD + d] = 1
            out[h * HD + d, 384 + h * 128 + d] = 1
    return out.astype(jnp.bfloat16)


def dot(a, b):
    return lax.dot_general(a, b, (((1,), (0,)), ((), ())), preferred_element_type=F32)


def dot_nt(a, b):
    return lax.dot_general(a, b, (((1,), (1,)), ((), ())), preferred_element_type=F32)


def dot_tn(a, b):
    return lax.dot_general(a, b, (((0,), (0,)), ((), ())), preferred_element_type=F32)


def standardized(v):
    mean = jnp.mean(v, -1, keepdims=True)
    centered = v - mean
    rstd = lax.rsqrt(jnp.mean(centered * centered, -1, keepdims=True) + EPS)
    return centered * rstd, rstd


def norm_back(g, xhat, rstd):
    return rstd * (
        g - jnp.mean(g, -1, keepdims=True) - xhat * jnp.mean(g * xhat, -1, keepdims=True)
    )


def gelu_pair(u):
    k = 0.7978845608028654
    t = jnp.tanh(k * (u + 0.044715 * u * u * u))
    value = 0.5 * u * (1 + t)
    slope = 0.5 * (1 + t) + 0.5 * u * (1 - t * t) * k * (1 + 3 * 0.044715 * u * u)
    return value, slope


TILES = ((0, KEYS // 2), (ROWS // 2, KEYS))


def scores_t(kv, q, qpos, start, masked):
    s = dot_nt(kv, q)
    if masked:
        key = lax.broadcasted_iota(jnp.int32, s.shape, 0) + start
        s = jnp.where(key <= qpos, s, MASKED)
    return s


def attend_kernel(kpos, rank, qpos_ref, q_ref, kv_ref, o_ref, lse_ref, kvs_ref, kvt_ref, qs_ref):
    for b in range(KEYS // BLK):
        at = pl.multiple_of(kpos[b] * BLK, BLK)
        kvs_ref[pl.ds(at, BLK), :] = kv_ref[b * BLK : (b + 1) * BLK, :]
    for b in range(ROWS // BLK):
        at = pl.multiple_of(rank[b] * BLK, BLK)
        qs_ref[pl.ds(at, BLK), :] = q_ref[b * BLK : (b + 1) * BLK, :] * SCALE
    for i in range(KEYS // CHUNK):
        kvt_ref[:, i * CHUNK : (i + 1) * CHUNK] = kvs_ref[i * CHUNK : (i + 1) * CHUNK, :].T
    for first, span in TILES:
        q = qs_ref[first : first + 256, :]
        qpos = qpos_ref[0:1, first : first + 256]
        top = jnp.full((1, 256), MASKED, F32)
        mass = jnp.zeros((1, 256), F32)
        acc = jnp.zeros((128, 256), F32)
        for start in range(0, span, CHUNK):
            s = scores_t(
                kvs_ref[start : start + CHUNK, :], q, qpos, start, start + CHUNK > span - KEYS // 2
            )
            new = jnp.maximum(top, jnp.max(s, 0, keepdims=True))
            p = jnp.exp2((s - new) * LOG2E)
            alpha = jnp.exp2((top - new) * LOG2E)
            mass = mass * alpha + jnp.sum(p, 0, keepdims=True)
            acc = acc * alpha + dot(kvt_ref[:, start : start + CHUNK], p.astype(BF))
            top = new
        o_ref[:, first : first + 256] = acc[HD:, :] * (1.0 / mass)
        lse_ref[0, :, first : first + 256] = jnp.broadcast_to(
            top * LOG2E + jnp.log2(mass), (8, 256)
        )


def attend_back_kernel(
    kpos, rank, qpos_ref, qs_ref, kvs_ref, kvt_ref, do_ref, o_ref, lse_ref, dkv_ref, dq_ref, dos, acc
):
    for b in range(ROWS // BLK):
        at = pl.multiple_of(rank[b] * BLK, BLK)
        dos[pl.ds(at, BLK), :] = do_ref[b * BLK : (b + 1) * BLK, :]
    dot_t = dos[...].astype(F32).T
    delta = jnp.sum(dot_t[HD:, :] * o_ref[...], 0, keepdims=True)
    dq = [jnp.zeros((128, 256), F32), jnp.zeros((128, 256), F32)]
    for start in range(0, KEYS, CHUNK):
        kv = kvs_ref[start : start + CHUNK, :]
        kvt = kvt_ref[:, start : start + CHUNK]
        total = None
        for n, (first, span) in enumerate(TILES):
            if start >= span:
                continue
            cols = slice(first, first + 256)
            q = qs_ref[cols, :]
            do = dos[cols, :]
            s = scores_t(kv, q, qpos_ref[0:1, cols], start, start + CHUNK > span - KEYS // 2)
            p = jnp.exp2(s * LOG2E - lse_ref[0, 0:1, cols])
            dp = dot_nt(kv, do)
            ds = (p * (dp - delta[:, cols])).astype(BF)
            part = dot(ds, q) + dot(p.astype(BF), do)
            total = part if total is None else total + part
            dq[n] = dq[n] + dot(kvt, ds)
        acc[start : start + CHUNK, :] = total.astype(BF)
    for b in range(KEYS // BLK):
        at = pl.multiple_of(kpos[b] * BLK, BLK)
        dkv_ref[b * BLK : (b + 1) * BLK, :] = acc[pl.ds(at, BLK), :]
    dos[0:256, :] = (dq[0] * SCALE).T.astype(BF)
    dos[256:512, :] = (dq[1] * SCALE).T.astype(BF)
    for b in range(ROWS // BLK):
        at = pl.multiple_of(rank[b] * BLK, BLK)
        dq_ref[b * BLK : (b + 1) * BLK, :] = dos[pl.ds(at, BLK), :]


PARAMS = dict(compiler_params=pltpu.CompilerParams(vmem_limit_bytes=48 * 1024 * 1024))


def attend(kpos, rank, qpos, q, kv):
    grid_spec = pltpu.PrefetchScalarGridSpec(
        num_scalar_prefetch=2,
        grid=(HL,),
        in_specs=[
            pl.BlockSpec((8, ROWS), lambda h, *_: (0, 0)),
            pl.BlockSpec((ROWS, 128), lambda h, *_: (0, h)),
            pl.BlockSpec((KEYS, 128), lambda h, *_: (0, h)),
        ],
        out_specs=[
            pl.BlockSpec((HD, ROWS), lambda h, *_: (h, 0)),
            pl.BlockSpec((1, 8, ROWS), lambda h, *_: (h, 0, 0)),
            pl.BlockSpec((KEYS, 128), lambda h, *_: (0, h)),
            pl.BlockSpec((128, KEYS), lambda h, *_: (h, 0)),
            pl.BlockSpec((ROWS, 128), lambda h, *_: (0, h)),
        ],
    )
    return pl.pallas_call(
        attend_kernel,
        grid_spec=grid_spec,
        out_shape=[
            jax.ShapeDtypeStruct((HW, ROWS), F32),
            jax.ShapeDtypeStruct((HL, 8, ROWS), F32),
            jax.ShapeDtypeStruct((KEYS, 384), BF),
            jax.ShapeDtypeStruct((384, KEYS), BF),
            jax.ShapeDtypeStruct((ROWS, 384), BF),
        ],
        name="attend",
        **PARAMS,
    )(kpos, rank, qpos, q, kv)


def attend_back(kpos, rank, qpos, qs, kvs, kvt, do, o, lse):
    grid_spec = pltpu.PrefetchScalarGridSpec(
        num_scalar_prefetch=2,
        grid=(HL,),
        in_specs=[
            pl.BlockSpec((8, ROWS), lambda h, *_: (0, 0)),
            pl.BlockSpec((ROWS, 128), lambda h, *_: (0, h)),
            pl.BlockSpec((KEYS, 128), lambda h, *_: (0, h)),
            pl.BlockSpec((128, KEYS), lambda h, *_: (h, 0)),
            pl.BlockSpec((ROWS, 128), lambda h, *_: (0, h)),
            pl.BlockSpec((HD, ROWS), lambda h, *_: (h, 0)),
            pl.BlockSpec((1, 8, ROWS), lambda h, *_: (h, 0, 0)),
        ],
        out_specs=[
            pl.BlockSpec((KEYS, 128), lambda h, *_: (0, h)),
            pl.BlockSpec((ROWS, 128), lambda h, *_: (0, h)),
        ],
        scratch_shapes=[pltpu.VMEM((ROWS, 128), BF), pltpu.VMEM((KEYS, 128), BF)],
    )
    return pl.pallas_call(
        attend_back_kernel,
        grid_spec=grid_spec,
        out_shape=[
            jax.ShapeDtypeStruct((KEYS, 384), BF),
            jax.ShapeDtypeStruct((ROWS, 384), BF),
        ],
        name="attend_back",
        **PARAMS,
    )(kpos, rank, qpos, qs, kvs, kvt, do, o, lse)


def exchange(v, axes):
    return lax.all_to_all(v, axes, 0, 0, tiled=True)


def spread(v, axes, n):
    return exchange(jnp.broadcast_to(v[None], (n,) + v.shape), axes)


def per_device(
    tokens,
    cotangent,
    block_map,
    ln1_gain,
    ln1_bias,
    w_qkv,
    b_query,
    b_value,
    w_out,
    b_out,
    ln2_gain,
    ln2_bias,
    w_fc1,
    b_fc1,
    w_fc2,
    b_fc2,
):
    perm = jnp.asarray(feature_matrix())
    heads = jnp.asarray(head_matrix())
    z, x, c = lax.axis_index("z"), lax.axis_index("x"), lax.axis_index("c")
    perm_t = lax.dynamic_slice_in_dim(perm, x * HW, HW, 0)

    maps = block_map.reshape(4, 4, 2, 2).transpose(2, 0, 1, 3)
    kpos = maps.reshape(-1)
    own = lax.dynamic_slice(maps, (c, z, 0, 0), (1, 1, 4, 2)).reshape(-1)
    before = own[None, :] < own[:, None]
    rank = jnp.sum(before.astype(jnp.int32), 1)
    ordered = jnp.sum(jnp.where(rank[:, None] == jnp.arange(8)[None, :], own[:, None], 0), 0)
    qpos = (ordered[:, None] * BLK + jnp.arange(BLK, dtype=jnp.int32)[None, :]).reshape(1, -1)
    qpos = jnp.broadcast_to(qpos, (8, ROWS))

    own_rows = dot(jnp.concatenate([tokens[0], cotangent[0]], 0), perm).astype(BF)
    all_rows = lax.all_gather(own_rows, "x", axis=0)
    tok = all_rows[:, :TOK].reshape(ROWS, D)
    dy = all_rows[:, TOK:].reshape(ROWS, D)
    own_tok = own_rows[:TOK].astype(F32)
    own_dy = own_rows[TOK:].astype(F32)

    out_cols = dot(jnp.concatenate([w_out, w_fc2], 0), perm).astype(BF)
    vectors = jnp.stack([ln1_gain, ln1_bias, b_query, b_value, b_out, ln2_gain, ln2_bias, b_fc2], 1)
    vectors = jnp.pad(vectors, ((0, 0), (0, 120)))
    qkv_cols = w_qkv.reshape(6, 3, TP, HW).transpose(2, 0, 1, 3).reshape(TP, 6, 3 * HW)
    fc1_cols = w_fc1.reshape(6, 16, TP, 2, 24).transpose(2, 0, 3, 1, 4).reshape(TP, 6, D)
    everyone = jnp.concatenate([vectors, out_cols[:6]], 1)
    sent = jnp.concatenate(
        [qkv_cols, fc1_cols, jnp.broadcast_to(everyone[None], (TP,) + everyone.shape)], 2
    )
    got = exchange(sent, "x").reshape(24, -1)
    extras = jnp.where(
        jnp.arange(128)[None, :] == 8, b_fc1[:, None], got[:, 1344:1472]
    )
    first = spread(jnp.concatenate([got[:, :576], extras], 1), G, 32).reshape(D, 704)
    second = lax.all_gather(
        jnp.concatenate([got[:, 576:1344], got[:, 1472:], out_cols[6:]], 1), G, axis=0, tiled=True
    )
    vec = first[:, 576:592].astype(F32).T
    gain1, bias1, bout, gain2, bias2, bfc2, bfc1 = (
        vec[i : i + 1] for i in (0, 1, 4, 5, 6, 7, 8)
    )
    bqv = dot_nt(first[:, 578:580].T, perm_t)
    bias_t = jnp.concatenate([bqv[0:1], jnp.zeros((1, HW), F32), bqv[1:2]], 1)
    bias_pad = dot(bias_t.astype(BF), heads)
    w_heads = dot(first[:, :576], heads).astype(BF)

    hat1, _ = standardized(tok.astype(F32))
    a1 = (hat1 * gain1 + bias1).astype(BF)
    qkv = (dot(a1, w_heads) + bias_pad).astype(BF)
    kv = spread(qkv[:, :384], "z", 4).reshape(4 * ROWS, 384)
    kv = lax.all_gather(kv, "c", axis=0, tiled=True)
    o_t, lse, kvs, kvt, qs = attend(kpos, rank, qpos, qkv[:, 384:], kv)

    place = jnp.repeat(rank, BLK) * BLK + jnp.tile(jnp.arange(BLK, dtype=jnp.int32), 8)
    unsort = (place[:, None] == jnp.arange(ROWS, dtype=jnp.int32)[None, :]).astype(BF)
    o = dot_nt(unsort, o_t.astype(BF)).astype(BF)
    o_all = spread(o, "x", 4)
    o_perm = sum(dot(o_all[i], perm[i * HW : (i + 1) * HW]) for i in range(TP)).astype(BF)

    w1, wo, w2 = second[:, :D], second[:, D : 2 * D], second[:, 2 * D :]
    resid = tok.astype(F32) + dot(o_perm, wo) + bout
    hat2, _ = standardized(resid)
    a2 = (hat2 * gain2 + bias2).astype(BF)
    u = dot(a2, w1) + bfc1
    act, slope = gelu_pair(u)
    gb = act.astype(BF)
    du = (dot_nt(dy, w2) * slope).astype(BF)
    mixed_part = dot(gb, w2).astype(BF)
    da2_part = dot_nt(du, w1).astype(BF)
    g_fc2 = dot_tn(gb, dy).astype(BF)
    g_fc1 = dot_tn(a2, du).astype(BF)
    g_bfc1 = jnp.sum(du.astype(F32), 0)

    parts = jnp.concatenate(
        [mixed_part.reshape(TP, TOK, D), da2_part.reshape(TP, TOK, D)], 1
    )
    sums = jnp.sum(exchange(parts, "x").astype(F32), 0)
    own_resid = lax.dynamic_slice_in_dim(resid, x * TOK, TOK, 0)
    mixed = (own_resid + sums[:TOK] + bfc2).astype(BF)
    da2 = sums[TOK:]
    hat2o, rstd2 = standardized(own_resid)
    g_gain2 = jnp.sum(da2 * hat2o, 0)
    g_bias2 = jnp.sum(da2, 0)
    dresid = own_dy + norm_back(da2 * gain2, hat2o, rstd2)
    dbranch = dresid.astype(BF)
    g_bout = jnp.sum(dbranch.astype(F32), 0)
    g_bfc2 = jnp.sum(own_dy, 0)
    dbr = spread(dbranch, "x", 4).reshape(ROWS, D)

    wo_t = dot(perm_t, wo).astype(BF)
    wo_pad = dot_tn(heads[2 * HW :, :384], wo_t).astype(BF)
    do = dot_nt(dbr, wo_pad).astype(BF)
    dkv_part, dq = attend_back(kpos, rank, qpos, qs, kvs, kvt, do, o_t, lse)
    dkv_c = exchange(dkv_part, "c").reshape(2, KEYS // 2, 384)
    dkv_c = (dkv_c[0].astype(F32) + dkv_c[1].astype(F32)).astype(BF)
    dkv_z = exchange(dkv_c, "z").reshape(4, ROWS, 384)
    dkv = jnp.sum(dkv_z.astype(F32), 0).astype(BF)
    dqkv = dot_nt(jnp.concatenate([dkv, dq], 1), heads).astype(BF)
    da1_part = dot_nt(dqkv, first[:, :576])
    g_gain1 = jnp.sum(da1_part * hat1, 0)
    g_bias1 = jnp.sum(da1_part, 0)
    g_qkv = dot_tn(a1, dqkv).astype(BF)
    dqkv_sum = jnp.sum(dqkv.astype(F32), 0)
    g_bqv = dot(jnp.stack([dqkv_sum[:HW], dqkv_sum[2 * HW :]], 0).astype(BF), perm_t)
    dbr_t = lax.dynamic_slice_in_dim(dbr, x * HW, HW, 1)
    g_out = dot_tn(o_perm, dbr_t).astype(BF)

    da1 = jnp.sum(exchange(da1_part.astype(BF).reshape(TP, TOK, D), "x").astype(F32), 0)
    hat1o, rstd1 = standardized(own_tok)
    dtok = (dresid + norm_back(da1 * gain1, hat1o, rstd1)).astype(BF)
    back = dot_nt(jnp.concatenate([mixed, dtok], 0), perm).astype(BF)
    mixed, dtok = back[:TOK], back[TOK:]

    rows = jnp.stack(
        [g_gain1, g_bias1, g_bqv[0], g_bqv[1], g_bout, g_gain2, g_bias2, g_bfc2, g_bfc1], 0
    )
    columns = jnp.pad(rows, ((0, 119), (0, 0))).T.astype(BF)
    grads = jnp.concatenate([g_qkv, g_fc1, g_out, columns, g_fc2], 1)
    half = exchange(grads, "c").reshape(2, D // 2, -1)
    half = (half[0].astype(F32) + half[1].astype(F32)).astype(BF)
    mine = jnp.sum(exchange(half, ("y", "z")).reshape(16, 24, -1).astype(F32), 0)
    last = exchange(mine[:, :1664].reshape(TP, 6, 1664), "x")
    r_qkv = last[:, :, :576].reshape(TP, 6, 3, HW).transpose(1, 2, 0, 3).reshape(6, 3 * D)
    r_fc1 = (
        last[:, :, 576:1344].reshape(TP, 6, 2, 16, 24).transpose(1, 3, 0, 2, 4).reshape(6, FF)
    )
    r_out = last[:, :, 1344:1536].transpose(1, 0, 2).reshape(6, D)
    r_vec = jnp.sum(last[:, :, 1536:1544], 0)
    r_cols = lax.dot_general(
        jnp.concatenate([r_out, mine[:, 1664:]], 0),
        perm.astype(F32),
        (((1,), (1,)), ((), ())),
        precision=lax.Precision.HIGHEST,
    )
    return (
        mixed[None],
        dtok[None],
        r_vec[:, 0],
        r_vec[:, 1],
        r_qkv,
        r_vec[:, 2],
        r_vec[:, 3],
        r_cols[:6],
        r_vec[:, 4],
        r_vec[:, 5],
        r_vec[:, 6],
        r_fc1,
        mine[:, 1544],
        r_cols[6:],
        r_vec[:, 7],
    )


def solution(mesh):
    fine = Mesh(mesh.devices.reshape(4, 4, 4, 2), ("y", "z", "x", "c"))
    rows = P("y", ("z", "x", "c"), None)
    every = ("y", "z", "x", "c")
    vec, mat = P(every), P(every, None)
    in_specs = (rows, rows, P(), vec, vec, mat, vec, vec, mat, vec, vec, vec, mat, vec, mat, vec)
    out_specs = (rows, rows, vec, vec, mat, vec, vec, mat, vec, vec, vec, mat, vec, mat, vec)
    return jax.shard_map(
        per_device, mesh=fine, in_specs=in_specs, out_specs=out_specs, check_vma=False
    )
```

time: 1720 us -> 373 us (0.22)
  blocking collectives: 505 us -> 41.1 us
  local copies, waits for them, and re-layouts: 360 us -> 40.9 us
  starting transfers between devices: 262 us -> 41.3 us
  matrix products: 194 us -> 38.3 us
  waiting for transfers between devices: 286 us -> 136 us
  loops' own time: 48.5 us -> 0 us
  Pallas kernels: 0 us -> 36.6 us
    unnamed x3 -> x0, blocking collectives: 505 us -> none
    unnamed x98 -> x0, starting transfers between devices: 261 us -> none
    unnamed x264 -> x99, local copies, waits for them, and re-layouts: 189 us -> 9.37 us
    dot_general x68 -> x27, matrix products: 194 us -> 38.3 us  [the longest x13 18.5 us: dot(): lax.dot_general(a, b, (((1,), (0,)), ((), ())), preferred_element_type=F32)]
    all_gather x6 -> x3, waiting for transfers between devices: 156 us -> 15.3 us  [the longest x1 8.63 us: per_device(): kv = lax.all_gather(kv, 'c', axis=0, tiled=True)]
    unnamed x107 -> x3, waiting for transfers between devices: 129 us -> 0.05 us
    dynamic_update_slice x16 -> x0, local copies, waits for them, and re-layouts: 125 us -> none  [the longest x8 62.4 us: both_step(): lax.dynamic_update_slice_in_dim(grad_values_all, value_part, start, 1)]
    all_to_all x0 -> x9, waiting for transfers between devices: none -> 121 us  [exchange(): return lax.all_to_all(v, axes, 0, 0, tiled=True)]
  transfers between devices with their start and end apart: 105 -> 12, of which waited for: 9 -> 11; matrix products, arithmetic and copies ran while one was open for 38% -> 8% of each run, Pallas kernels for 0% -> 5%
where the time goes in v1:
time: 373 us; the launch traced here: 371 us
  waiting for transfers between devices  136 us (36%)
  starting transfers between devices  41.3 us (11%)
  blocking collectives  41.1 us (11%)
  local copies, waits for them, and re-layouts  40.9 us (11%)
  matrix products  38.3 us (10%)
  Pallas kernels  36.6 us (10%)
  other arithmetic  21.7 us (6%)
  between operations  14.6 us (4%)
    all_to_all x9, waiting for transfers between devices, exchange(): return lax.all_to_all(v, axes, 0, 0, tiled=True)  121 us
    all_to_all x9, starting transfers between devices, exchange(): return lax.all_to_all(v, axes, 0, 0, tiled=True)  41.2 us
    all_to_all x3, blocking collectives, exchange(): return lax.all_to_all(v, axes, 0, 0, tiled=True)  41.1 us
    pallas_call x1, Pallas kernels, attend(): pl.pallas_call(attend_kernel, grid_spec=grid_spec, out_shape=[jax.ShapeDt...  19.3 us
    dot_general x13, matrix products, dot(): lax.dot_general(a, b, (((1,), (0,)), ((), ())), preferred_element_type=F32)  18.5 us
    pallas_call x1, Pallas kernels, attend_back(): pl.pallas_call(attend_back_kernel, grid_spec=grid_spec, out_shape=[jax.Sh...  17.3 us
    unnamed x99, local copies, waits for them, and re-layouts  9.37 us
    dot_general x4, matrix products, dot_tn(): lax.dot_general(a, b, (((0,), (0,)), ((), ())), preferred_element_type=F32)  9.37 us
  transfers between devices with their start and end apart: 12, of which 11 were waited for; matrix products, arithmetic and copies ran while one was open for 8% of the time, Pallas kernels for 5%

profile of v1, /device:TPU:0, one launch (start us, length us, event | category | flops | bytes accessed | tf_op | source)
XLA Modules:
  0.0 370.6 jit_solution(5838730262773762854)
XLA Ops:
  18.1 4.5 %all-to-all-start = ((bf16[4,6,2240]{2,1,0:T(8,128)(2,1)}), bf16[4,6,2240]{2,1,0:T(8,128)(2,1)S(1)}, u32[]{:S(2)}, u32[]{:S(2)}) async-start(bf16[4,6,2240]{2,1,0:T(8,128)(2,1)} %concatenate.47), calls=%async_computation | async-start | bytes 294912 | tf_op jit(solution)/shard_map/all_to_all | solution.py:231
  23.9 4.8 %all-to-all-done = bf16[4,6,2240]{2,1,0:T(8,128)(2,1)S(1)} async-done(((bf16[4,6,2240]{2,1,0:T(8,128)(2,1)}), bf16[4,6,2240]{2,1,0:T(8,128)(2,1)S(1)}, u32[]{:S(2)}, u32[]{:S(2)}) %all-to-all-start) | async-done | bytes 107552 | tf_op jit(solution)/shard_map/all_to_all | solution.py:231
  30.1 8.3 %all-to-all-start.1 = ((bf16[32,24,704]{2,1,0:T(8,128)(2,1)}), bf16[32,24,704]{2,1,0:T(8,128)(2,1)S(1)}, u32[]{:S(2)}, u32[]{:S(2)}) async-start(bf16[32,24,704]{2,1,0:T(8,128)(2,1)} %broadcast_in_dim.52), calls=%async_computation.1 | async-start | bytes 2359296 | tf_op jit(solution)/shard_map/all_to_all | solution.py:231
  38.5 18.8 %all-to-all-done.1 = bf16[32,24,704]{2,1,0:T(8,128)(2,1)S(1)} async-done(((bf16[32,24,704]{2,1,0:T(8,128)(2,1)}), bf16[32,24,704]{2,1,0:T(8,128)(2,1)S(1)}, u32[]{:S(2)}, u32[]{:S(2)}) %all-to-all-start.1) | async-done | bytes 1081376 | tf_op jit(solution)/shard_map/all_to_all | solution.py:231
  65.5 3.7 %add_convert_fusion.4 = bf16[512,768]{1,0:T(8,128)(2,1)} fusion(bf16[512,768]{1,0:T(8,128)(2,1)S(1)} %fusion.13, bf16[576,768]{1,0:T(8,128)(2,1)} %constant.71.clone, bf16[768,704]{1,0:T(8,128)(2,1)S(1)} %bitcast.128, f32[768]{0:T(1024)} %convolution_reduce_fusion), kind=kOutput, calls=%fused_computation.32 | convolution fusion | flops 1284833280 | bytes 3443712 | tf_op jit(solution)/shard_map/dot_general | solution.py:53
  70.6 23.5 %all_to_all.70 = bf16[4,512,384]{2,1,0:T(8,128)(2,1)} all-to-all(bf16[4,512,384]{2,1,0:T(8,128)(2,1)S(1)} %broadcast_in_dim.54), channel_id=1, replica_groups=mesh['y'=4,'z'=4,'x'=4,'c'=2] {'z'}, dimensions={0} | all-to-all | bytes 3145728 | tf_op jit(solution)/shard_map/all_to_all | solution.py:231
  97.1 8.6 %all-gather.5.cloned.1.call-done.kv_ref = bf16[4096,384]{1,0:T(8,128)(2,1)} async-done(((bf16[2048,384]{1,0:T(8,128)(2,1)}), bf16[4096,384]{1,0:T(8,128)(2,1)}) %all-gather.5.cloned.1.call-update) | async-done | bytes 3145744 | tf_op jit(solution)/shard_map/all_gather | solution.py:307
  105.8 19.3 %attend.1 = (f32[192,512]{1,0:T(8,128)S(1)}, f32[3,8,512]{2,1,0:T(8,128)S(1)}, bf16[4096,384]{1,0:T(8,128)(2,1)S(1)}, bf16[384,4096]{1,0:T(8,128)(2,1)}, bf16[512,384]{1,0:T(8,128)(2,1)S(1)}) custom-call(s32[64]{0:T(128)S(1)} %reshape.289.kpos, s32[8]{0:T(128)S(1)} %convert_reduce_fusion.5.rank, s32[8,512]{1,0:T(8,128)S(1)} %broadcast_in_dim.48.qpos_ref, ...), custom_call_target="tpu_custom_call" | custom-call | tf_op jit(solution)/shard_map/attend/pallas_call | solution.py:184
  128.2 4.3 %all-to-all-start.3 = ((bf16[4,512,192]{1,2,0:T(8,128)(2,1)}), bf16[4,512,192]{1,2,0:T(8,128)(2,1)S(1)}, u32[]{:S(2)}, u32[]{:S(2)}) async-start(bf16[4,512,192]{1,2,0:T(8,128)(2,1)} %broadcast_in_dim.55), calls=%async_computation.3 | async-start | bytes 1572864 | tf_op jit(solution)/shard_map/all_to_all | solution.py:231
  133.8 11.4 %all-to-all-done.3 = bf16[4,512,192]{1,2,0:T(8,128)(2,1)S(1)} async-done(((bf16[4,512,192]{1,2,0:T(8,128)(2,1)}), bf16[4,512,192]{1,2,0:T(8,128)(2,1)S(1)}, u32[]{:S(2)}, u32[]{:S(2)}) %all-to-all-start.3) | async-done | bytes 786464 | tf_op jit(solution)/shard_map/all_to_all | solution.py:231
  149.3 6.7 %all-gather.7.cloned.1.call-done = bf16[768,2304]{1,0:T(8,128)(2,1)} async-done(((bf16[24,2304]{1,0:T(8,128)(2,1)}), bf16[768,2304]{1,0:T(8,128)(2,1)}) %all-gather.7.cloned.1.call-update) | async-done | bytes 3538960 | tf_op jit(solution)/shard_map/all_gather | solution.py:291
  155.9 2.5 fusion.85
  165.5 4.4 %all-to-all-start.4 = ((bf16[4,256,768]{2,1,0:T(8,128)(2,1)}), bf16[4,256,768]{2,1,0:T(8,128)(2,1)}, u32[]{:S(2)}, u32[]{:S(2)}) async-start(bf16[4,256,768]{2,1,0:T(8,128)(2,1)} %pad_maximum_fusion), calls=%async_computation.4 | async-start | bytes 3145728 | tf_op jit(solution)/shard_map/all_to_all | solution.py:231
  172.3 19.1 %all-to-all-done.4 = bf16[4,256,768]{2,1,0:T(8,128)(2,1)} async-done(((bf16[4,256,768]{2,1,0:T(8,128)(2,1)}), bf16[4,256,768]{2,1,0:T(8,128)(2,1)}, u32[]{:S(2)}, u32[]{:S(2)}) %all-to-all-start.4) | async-done | bytes 1572896 | tf_op jit(solution)/shard_map/all_to_all | solution.py:231
  196.1 3.8 %all-to-all-start.5 = ((bf16[4,128,768]{2,1,0:T(8,128)(2,1)}), bf16[4,128,768]{2,1,0:T(8,128)(2,1)S(1)}, u32[]{:S(2)}, u32[]{:S(2)}) async-start(bf16[4,128,768]{2,1,0:T(8,128)(2,1)} %broadcast_in_dim.56), calls=%async_computation.5 | async-start | bytes 1572864 | tf_op jit(solution)/shard_map/all_to_all | solution.py:231
  200.0 2.5 convolution_convert_fusion.9
  202.5 9.4 %all-to-all-done.5 = bf16[4,128,768]{2,1,0:T(8,128)(2,1)S(1)} async-done(((bf16[4,128,768]{2,1,0:T(8,128)(2,1)}), bf16[4,128,768]{2,1,0:T(8,128)(2,1)S(1)}, u32[]{:S(2)}, u32[]{:S(2)}) %all-to-all-start.5) | async-done | bytes 786464 | tf_op jit(solution)/shard_map/all_to_all | solution.py:231
  214.9 17.3 %attend_back.1 = (bf16[4096,384]{1,0:T(8,128)(2,1)S(1)}, bf16[512,384]{1,0:T(8,128)(2,1)S(1)}) custom-call(s32[64]{0:T(128)S(1)} %reshape.289.kpos, s32[8]{0:T(128)S(1)} %convert_reduce_fusion.5.rank, s32[8,512]{1,0:T(8,128)S(1)} %broadcast_in_dim.48.qpos_ref, bf16[512,384]{1,0:T(8,128)(2,1)S(1)} %get-tuple-element.23.qs_ref, bf16[4096,384]{1,0:T(8,128)(2,1)} %copy-done, ...), custom_call_target="tpu_custom_call" | custom-call | tf_op jit(solution)/shard_map/attend_back/pallas_call | solution.py:218
  232.2 6.3 %all_to_all.71 = bf16[2,2048,384]{2,1,0:T(8,128)(2,1)S(1)} all-to-all(bf16[2,2048,384]{2,1,0:T(8,128)(2,1)S(1)} %bitcast.116), channel_id=1, replica_groups=mesh['y'=4,'z'=4,'x'=4,'c'=2] {'c'}, dimensions={0} | all-to-all | bytes 6291456 | tf_op jit(solution)/shard_map/all_to_all | solution.py:231
  240.0 4.5 %all-to-all-start.7 = ((bf16[4,512,384]{2,1,0:T(8,128)(2,1)}), bf16[4,512,384]{2,1,0:T(8,128)(2,1)}, u32[]{:S(2)}, u32[]{:S(2)}) async-start(bf16[4,512,384]{2,1,0:T(8,128)(2,1)} %bitcast.125), calls=%async_computation.7 | async-start | bytes 3145728 | tf_op jit(solution)/shard_map/all_to_all | solution.py:231
  244.6 21.2 %all-to-all-done.7 = bf16[4,512,384]{2,1,0:T(8,128)(2,1)} async-done(((bf16[4,512,384]{2,1,0:T(8,128)(2,1)}), bf16[4,512,384]{2,1,0:T(8,128)(2,1)}, u32[]{:S(2)}, u32[]{:S(2)}) %all-to-all-start.7) | async-done | bytes 1572896 | tf_op jit(solution)/shard_map/all_to_all | solution.py:231
  275.1 2.3 fusion.22
  278.3 3.5 fusion.16
  281.8 6.1 %copy.150 = bf16[768,2432]{1,0:T(8,128)(2,1)} copy(bf16[768,2432]{0,1:T(8,128)(2,1)} %fusion.16) | data formatting | bytes 7471104 | tf_op jit(solution)/shard_map/all_to_all | solution.py:231
  287.8 11.3 %all_to_all.72 = bf16[2,384,2432]{2,1,0:T(8,128)(2,1)} all-to-all(bf16[2,384,2432]{2,1,0:T(8,128)(2,1)} %bitcast.117), channel_id=1, replica_groups=mesh['y'=4,'z'=4,'x'=4,'c'=2] {'c'}, dimensions={0} | all-to-all | bytes 7471104 | tf_op jit(solution)/shard_map/all_to_all | solution.py:231
  299.2 3.8 %all-to-all-start.8 = ((bf16[4,128,768]{2,1,0:T(8,128)(2,1)}), bf16[4,128,768]{2,1,0:T(8,128)(2,1)S(1)}, u32[]{:S(2)}, u32[]{:S(2)}) async-start(bf16[4,128,768]{2,1,0:T(8,128)(2,1)} %bitcast.30), calls=%async_computation.8 | async-start | bytes 1572864 | tf_op jit(solution)/shard_map/all_to_all | solution.py:231
  302.9 3.8 %add_convert_fusion = bf16[1,384,2432]{2,1,0:T(8,128)(2,1)} fusion(bf16[2,384,2432]{2,1,0:T(8,128)(2,1)} %all_to_all.72), kind=kLoop, calls=%fused_computation.1 | loop fusion | flops 3735552 | bytes 5603328 | tf_op jit(solution)/shard_map/convert_element_type | solution.py:376
  306.7 8.8 %all-to-all-done.8 = bf16[4,128,768]{2,1,0:T(8,128)(2,1)S(1)} async-done(((bf16[4,128,768]{2,1,0:T(8,128)(2,1)}), bf16[4,128,768]{2,1,0:T(8,128)(2,1)S(1)}, u32[]{:S(2)}, u32[]{:S(2)}) %all-to-all-start.8) | async-done | bytes 786464 | tf_op jit(solution)/shard_map/all_to_all | solution.py:231
  316.4 4.2 %all-to-all-start.10 = ((bf16[16,24,2432]{2,1,0:T(8,128)(2,1)}), bf16[16,24,2432]{2,1,0:T(8,128)(2,1)S(1)}, u32[]{:S(2)}, u32[]{:S(2)}) async-start(bf16[16,24,2432]{2,1,0:T(8,128)(2,1)} %bitcast.123), calls=%async_computation.10 | async-start | bytes 3735552 | tf_op jit(solution)/shard_map/all_to_all | solution.py:231
  323.8 23.4 %all-to-all-done.10 = bf16[16,24,2432]{2,1,0:T(8,128)(2,1)S(1)} async-done(((bf16[16,24,2432]{2,1,0:T(8,128)(2,1)}), bf16[16,24,2432]{2,1,0:T(8,128)(2,1)S(1)}, u32[]{:S(2)}, u32[]{:S(2)}) %all-to-all-start.10) | async-done | bytes 1867808 | tf_op jit(solution)/shard_map/all_to_all | solution.py:231
  348.2 3.4 all-to-all-start.11
  354.1 3.9 %all-to-all-done.11 = f32[4,6,1664]{2,1,0:T(8,128)S(1)} async-done(((f32[4,6,1664]{2,1,0:T(8,128)}), f32[4,6,1664]{2,1,0:T(8,128)S(1)}, u32[]{:S(2)}, u32[]{:S(2)}) %all-to-all-start.11) | async-done | bytes 159776 | tf_op jit(solution)/shard_map/all_to_all | solution.py:231
  (246 shorter events, 76.7 us)
Async XLA Ops:
  7.2 9.5 %copy-start.32 = (bf16[6,3072]{1,0:T(8,128)(2,1)S(1)}, bf16[6,3072]{1,0:T(8,128)(2,1)}, u32[]{:S(2)}) copy-start(bf16[6,3072]{1,0:T(8,128)(2,1)} %param.30) | copy-start | bytes 110596
  14.1 8.5 %copy-start.2 = (bf16[768,768]{1,0:T(8,128)(2,1)S(1)}, bf16[768,768]{1,0:T(8,128)(2,1)}, u32[]{:S(2)}) copy-start(bf16[768,768]{1,0:T(8,128)(2,1)} %constant.70.clone) | copy-start | bytes 3538948
  14.2 8.5 %copy-start.43 = (bf16[1,128,768]{2,1,0:T(8,128)(2,1)S(1)}, bf16[1,128,768]{2,1,0:T(8,128)(2,1)}, u32[]{:S(2)}) copy-start(bf16[1,128,768]{2,1,0:T(8,128)(2,1)} %param.19) | copy-start | bytes 589828
  14.2 8.5 %copy-start.44 = (bf16[1,128,768]{2,1,0:T(8,128)(2,1)S(1)}, bf16[1,128,768]{2,1,0:T(8,128)(2,1)}, u32[]{:S(2)}) copy-start(bf16[1,128,768]{2,1,0:T(8,128)(2,1)} %param.18) | copy-start | bytes 589828
  18.1 10.7 %copy-start.41 = (bf16[24]{0:T(256)(128)(2,1)S(1)}, bf16[24]{0:T(256)(128)(2,1)}, u32[]{:S(2)}) copy-start(bf16[24]{0:T(256)(128)(2,1)} %param.31) | copy-start | bytes 148
  18.1 10.6 %all-to-all-start = ((bf16[4,6,2240]{2,1,0:T(8,128)(2,1)}), bf16[4,6,2240]{2,1,0:T(8,128)(2,1)S(1)}, u32[]{:S(2)}, u32[]{:S(2)}) async-start(bf16[4,6,2240]{2,1,0:T(8,128)(2,1)} %concatenate.47), calls=%async_computation | async-start | bytes 294912 | tf_op jit(solution)/shard_map/all_to_all | solution.py:231
  22.7 38.0 %all-gather.9.cloned.1.call-start = ((), (), s32[]{:S(2)}) async-start(), calls=%async_computation.14 | async-start | bytes 1966080 | tf_op jit(solution)/shard_map/all_gather | solution.py:271
  30.1 27.2 %all-to-all-start.1 = ((bf16[32,24,704]{2,1,0:T(8,128)(2,1)}), bf16[32,24,704]{2,1,0:T(8,128)(2,1)S(1)}, u32[]{:S(2)}, u32[]{:S(2)}) async-start(bf16[32,24,704]{2,1,0:T(8,128)(2,1)} %broadcast_in_dim.52), calls=%async_computation.1 | async-start | bytes 2359296 | tf_op jit(solution)/shard_map/all_to_all | solution.py:231
  38.4 67.3 %all-gather.5.cloned.1.call-start = ((), (), s32[]{:S(2)}) async-start(), calls=%async_computation.12 | async-start | bytes 4718592 | tf_op jit(solution)/shard_map/all_gather | solution.py:307
  57.3 7.3 %copy-start.13 = (bf16[32,24,704]{2,1,0:T(8,128)(2,1)}, bf16[32,24,704]{2,1,0:T(8,128)(2,1)S(1)}, u32[]{:S(2)}) copy-start(bf16[32,24,704]{2,1,0:T(8,128)(2,1)S(1)} %all-to-all-done.1) | copy-start | bytes 3244036
  57.8 2.0 copy-start.17
  60.7 3.5 copy-start.1
  94.2 61.8 %all-gather.7.cloned.1.call-start = ((), (), s32[]{:S(2)}) async-start(), calls=%async_computation.13 | async-start | bytes 3649536 | tf_op jit(solution)/shard_map/all_gather | solution.py:291
  128.2 17.1 %all-to-all-start.3 = ((bf16[4,512,192]{1,2,0:T(8,128)(2,1)}), bf16[4,512,192]{1,2,0:T(8,128)(2,1)S(1)}, u32[]{:S(2)}, u32[]{:S(2)}) async-start(bf16[4,512,192]{1,2,0:T(8,128)(2,1)} %broadcast_in_dim.55), calls=%async_computation.3 | async-start | bytes 1572864 | tf_op jit(solution)/shard_map/all_to_all | solution.py:231
  133.8 13.5 %copy-start.27 = (bf16[192,768]{1,0:T(8,128)(2,1)S(1)}, bf16[192,768]{1,0:T(8,128)(2,1)}, u32[]{:S(2)}) copy-start(bf16[192,768]{1,0:T(8,128)(2,1)} %constant.91) | copy-start | bytes 884740
  145.3 2.1 copy-start.12
  147.9 8.0 %copy-start.39 = (f32[768]{0:T(1024)S(1)}, f32[768]{0:T(1024)}, u32[]{:S(2)}) copy-start(f32[768]{0:T(1024)} %get-tuple-element.41) | copy-start | bytes 9220
  149.3 9.2 %copy-start.10 = (bf16[512,768]{1,0:T(8,128)(2,1)}, bf16[512,768]{1,0:T(8,128)(2,1)S(1)}, u32[]{:S(2)}) copy-start(bf16[512,768]{1,0:T(8,128)(2,1)S(1)} %add_convert_fusion.3) | copy-start | bytes 2359300
  155.9 2.9 copy-start.42
  165.5 25.9 %all-to-all-start.4 = ((bf16[4,256,768]{2,1,0:T(8,128)(2,1)}), bf16[4,256,768]{2,1,0:T(8,128)(2,1)}, u32[]{:S(2)}, u32[]{:S(2)}) async-start(bf16[4,256,768]{2,1,0:T(8,128)(2,1)} %pad_maximum_fusion), calls=%async_computation.4 | async-start | bytes 3145728 | tf_op jit(solution)/shard_map/all_to_all | solution.py:231
  172.3 21.9 %copy-start.7 = (bf16[256,768]{1,0:T(8,128)(2,1)S(1)}, bf16[256,768]{1,0:T(8,128)(2,1)}, u32[]{:S(2)}) copy-start(bf16[256,768]{1,0:T(8,128)(2,1)} %convolution_convert_fusion.8) | copy-start | bytes 1179652
  196.1 16.7 %copy-start.45 = (bf16[192,384]{1,0:T(8,128)(2,1)S(1)}, bf16[192,384]{1,0:T(8,128)(2,1)}, u32[]{:S(2)}) copy-start(bf16[192,384]{1,0:T(8,128)(2,1)} %constant.95) | copy-start | bytes 442372
  196.1 15.8 %all-to-all-start.5 = ((bf16[4,128,768]{2,1,0:T(8,128)(2,1)}), bf16[4,128,768]{2,1,0:T(8,128)(2,1)S(1)}, u32[]{:S(2)}, u32[]{:S(2)}) async-start(bf16[4,128,768]{2,1,0:T(8,128)(2,1)} %broadcast_in_dim.56), calls=%async_computation.5 | async-start | bytes 1572864 | tf_op jit(solution)/shard_map/all_to_all | solution.py:231
  240.0 4.5 %copy-start.8 = (bf16[256,768]{1,0:T(8,128)(2,1)S(1)}, bf16[256,768]{1,0:T(8,128)(2,1)}, u32[]{:S(2)}) copy-start(bf16[256,768]{1,0:T(8,128)(2,1)} %convolution_convert_fusion.8) | copy-start | bytes 1179652
  240.0 25.8 %all-to-all-start.7 = ((bf16[4,512,384]{2,1,0:T(8,128)(2,1)}), bf16[4,512,384]{2,1,0:T(8,128)(2,1)}, u32[]{:S(2)}, u32[]{:S(2)}) async-start(bf16[4,512,384]{2,1,0:T(8,128)(2,1)} %bitcast.125), calls=%async_computation.7 | async-start | bytes 3145728 | tf_op jit(solution)/shard_map/all_to_all | solution.py:231
  244.5 23.2 %copy-start.24 = (bf16[576,384]{1,0:T(8,128)(2,1)S(1)}, bf16[576,384]{1,0:T(8,128)(2,1)}, u32[]{:S(2)}) copy-start(bf16[576,384]{1,0:T(8,128)(2,1)} %constant.96) | copy-start | bytes 1327108
  273.0 2.1 copy-start.11
  273.0 4.4 %copy-start.3 = (bf16[768,768]{1,0:T(8,128)(2,1)S(1)}, bf16[768,768]{1,0:T(8,128)(2,1)}, u32[]{:S(2)}) copy-start(bf16[768,768]{1,0:T(8,128)(2,1)} %constant.70.clone) | copy-start | bytes 3538948
  275.1 3.2 copy-start.21
  299.2 16.3 %all-to-all-start.8 = ((bf16[4,128,768]{2,1,0:T(8,128)(2,1)}), bf16[4,128,768]{2,1,0:T(8,128)(2,1)S(1)}, u32[]{:S(2)}, u32[]{:S(2)}) async-start(bf16[4,128,768]{2,1,0:T(8,128)(2,1)} %bitcast.30), calls=%async_computation.8 | async-start | bytes 1572864 | tf_op jit(solution)/shard_map/all_to_all | solution.py:231
  316.4 30.8 %all-to-all-start.10 = ((bf16[16,24,2432]{2,1,0:T(8,128)(2,1)}), bf16[16,24,2432]{2,1,0:T(8,128)(2,1)S(1)}, u32[]{:S(2)}, u32[]{:S(2)}) async-start(bf16[16,24,2432]{2,1,0:T(8,128)(2,1)} %bitcast.123), calls=%async_computation.10 | async-start | bytes 3735552 | tf_op jit(solution)/shard_map/all_to_all | solution.py:231
  348.2 9.8 %all-to-all-start.11 = ((f32[4,6,1664]{2,1,0:T(8,128)}), f32[4,6,1664]{2,1,0:T(8,128)S(1)}, u32[]{:S(2)}, u32[]{:S(2)}) async-start(f32[4,6,1664]{2,1,0:T(8,128)} %reshape.302), calls=%async_computation.11 | async-start | bytes 425984 | tf_op jit(solution)/shard_map/all_to_all | solution.py:231
  (29 other events, 37.2 us)
Sparse Core Ops, SparseCore 0:
  25.1 29.3 all-gather.8
  94.3 11.4 all-gather.4
  108.7 47.2 all-gather.6

commit v2 on v1

v2 whole, which is shorter than its diff:
```python
import jax
import jax.numpy as jnp
import numpy as np
from jax import lax
from jax.experimental import pallas as pl
from jax.experimental.pallas import tpu as pltpu
from jax.sharding import Mesh, PartitionSpec as P

D = 768
H = 12
HD = 64
FF = 3072
BLK = 64
TP = 4
HL = H // TP
HW = HL * HD
COLS = 640
TOK = 128
ROWS = TOK * TP
KEYS = 4096
CHUNK = 1024
BACK = 2048
EPS = 1e-05
MASKED = -1e30
LOG2E = 1.4426950408889634
SCALE = HD**-0.5
BF = jnp.bfloat16
F32 = jnp.float32
G = ("c", "y", "z")
SWAP = ((0, 1), (1, 0))


def natural_feature(i):
    c, y, z, x, r = i // 384, (i // 96) % 4, (i // 24) % 4, (i // 6) % 4, i % 6
    return y * 192 + z * 48 + x * 12 + c * 6 + r


def feature_matrix():
    out = np.zeros((D, D), np.float32)
    i = np.arange(D)
    out[natural_feature(i), i] = 1
    return out.astype(jnp.bfloat16)


def head_matrix():
    out = np.zeros((COLS, 6 * 2 * HD), np.float32)
    for h in range(HL):
        for d in range(HD):
            out[HW + h * HD + d, h * 128 + d] = 1
            out[2 * HW + h * HD + d, h * 128 + HD + d] = 1
            out[h * HD + d, 384 + h * 128 + d] = 1
    return out.astype(jnp.bfloat16)


def dot(a, b):
    return lax.dot_general(a, b, (((1,), (0,)), ((), ())), preferred_element_type=F32)


def dot_nt(a, b):
    return lax.dot_general(a, b, (((1,), (1,)), ((), ())), preferred_element_type=F32)


def dot_tn(a, b):
    return lax.dot_general(a, b, (((0,), (0,)), ((), ())), preferred_element_type=F32)


def standardized(v):
    mean = jnp.mean(v, -1, keepdims=True)
    centered = v - mean
    rstd = lax.rsqrt(jnp.mean(centered * centered, -1, keepdims=True) + EPS)
    return centered * rstd, rstd


def norm_back(g, xhat, rstd):
    return rstd * (
        g - jnp.mean(g, -1, keepdims=True) - xhat * jnp.mean(g * xhat, -1, keepdims=True)
    )


def gelu_pair(u):
    k = 0.7978845608028654
    t = jnp.tanh(k * (u + 0.044715 * u * u * u))
    value = 0.5 * u * (1 + t)
    slope = 0.5 * (1 + t) + 0.5 * u * (1 - t * t) * k * (1 + 3 * 0.044715 * u * u)
    return value, slope


TILES = ((0, KEYS // 2), (ROWS // 2, KEYS))


def scores_t(kv, q, qpos, start, masked):
    s = dot_nt(kv, q)
    if masked:
        key = lax.broadcasted_iota(jnp.int32, s.shape, 0) + start
        s = jnp.where(key <= qpos, s, MASKED)
    return s


def attend_kernel(
    kpos, rank, qpos_ref, q_ref, own_ref, other_ref, o_ref, ot_ref, lse_ref, kvs_ref, kvt_ref, qs_ref, o_s, o_r
):
    head = pl.program_id(0)
    for b in range(KEYS // BLK):
        at = pl.multiple_of(kpos[b] * BLK, BLK)
        part = own_ref if b < KEYS // BLK // 2 else other_ref
        row = b % (KEYS // BLK // 2) * BLK
        kvs_ref[pl.ds(at, BLK), :] = part[row : row + BLK, :]
    for b in range(ROWS // BLK):
        at = pl.multiple_of(rank[b] * BLK, BLK)
        qs_ref[pl.ds(at, BLK), :] = q_ref[b * BLK : (b + 1) * BLK, :] * SCALE
    for i in range(KEYS // CHUNK):
        kvt_ref[:, i * CHUNK : (i + 1) * CHUNK] = kvs_ref[i * CHUNK : (i + 1) * CHUNK, :].T
    for first, span in TILES:
        q = qs_ref[first : first + 256, :]
        qpos = qpos_ref[0:1, first : first + 256]
        top = jnp.full((8, 256), MASKED, F32)
        for start in range(0, span, CHUNK):
            masked = start + CHUNK > span - KEYS // 2
            s = scores_t(kvs_ref[start : start + CHUNK, :], q, qpos, start, masked)
            top = jnp.maximum(top, jnp.max(s.reshape(-1, 8, 256), 0))
        top = jnp.max(top, 0, keepdims=True) * LOG2E
        mass = jnp.zeros((8, 256), F32)
        acc = jnp.zeros((128, 256), F32)
        for start in range(0, span, CHUNK):
            masked = start + CHUNK > span - KEYS // 2
            s = scores_t(kvs_ref[start : start + CHUNK, :], q, qpos, start, masked)
            p = jnp.exp2(s * LOG2E - top)
            mass = mass + jnp.sum(p.reshape(-1, 8, 256), 0)
            acc = acc + dot(kvt_ref[:, start : start + CHUNK], p.astype(BF))
        mass = jnp.sum(mass, 0, keepdims=True)
        o = acc[HD:, :] * (1.0 / mass)
        ot_ref[:, first : first + 256] = o
        o_s[pl.ds(pl.multiple_of(head * HD, HD), HD), first : first + 256] = o
        lse_ref[0, :, first : first + 256] = jnp.broadcast_to(top + jnp.log2(mass), (8, 256))

    @pl.when(head == HL - 1)
    def _():
        o_r[...] = o_s[...].T.astype(BF)
        for b in range(ROWS // BLK):
            at = pl.multiple_of(rank[b] * BLK, BLK)
            row, col = b * BLK % TOK, b * BLK // TOK * HW
            o_ref[row : row + BLK, col : col + HW] = o_r[pl.ds(at, BLK), :]


def attend_back_kernel(
    kpos,
    rank,
    qpos_ref,
    qs_ref,
    kvs_ref,
    kvt_ref,
    dbr_ref,
    wo_ref,
    o_ref,
    lse_ref,
    own_ref,
    other_ref,
    dq_ref,
    dos,
    acc,
):
    do_all = dot_nt(dbr_ref[...], wo_ref[...]).astype(BF)
    for b in range(ROWS // BLK):
        at = pl.multiple_of(rank[b] * BLK, BLK)
        dos[pl.ds(at, BLK), :] = do_all[b * BLK : (b + 1) * BLK, :]
    dot_t = dos[...].astype(F32).T
    delta = jnp.sum(dot_t[HD:, :] * o_ref[...], 0, keepdims=True)
    dq = [jnp.zeros((128, 256), F32), jnp.zeros((128, 256), F32)]
    for start in range(0, KEYS, BACK):
        kv = kvs_ref[start : start + BACK, :]
        kvt = kvt_ref[:, start : start + BACK]
        total = None
        for n, (first, span) in enumerate(TILES):
            if start >= span:
                continue
            cols = slice(first, first + 256)
            q = qs_ref[cols, :]
            do = dos[cols, :]
            s = scores_t(kv, q, qpos_ref[0:1, cols], start, start + BACK > span - KEYS // 2)
            p = jnp.exp2(s * LOG2E - lse_ref[0, 0:1, cols])
            dp = dot_nt(kv, do)
            ds = (p * (dp - delta[:, cols])).astype(BF)
            part = dot(ds, q) + dot(p.astype(BF), do)
            total = part if total is None else total + part
            dq[n] = dq[n] + dot(kvt, ds)
        acc[start : start + BACK, :] = total.astype(BF)
    for b in range(KEYS // BLK):
        at = pl.multiple_of(kpos[b] * BLK, BLK)
        part = own_ref if b < KEYS // BLK // 2 else other_ref
        row = b % (KEYS // BLK // 2) * BLK
        part[row : row + BLK, :] = acc[pl.ds(at, BLK), :]
    dos[0:256, :] = (dq[0] * SCALE).T.astype(BF)
    dos[256:512, :] = (dq[1] * SCALE).T.astype(BF)
    for b in range(ROWS // BLK):
        at = pl.multiple_of(rank[b] * BLK, BLK)
        dq_ref[b * BLK : (b + 1) * BLK, :] = dos[pl.ds(at, BLK), :]


def settings(flops):
    return dict(
        compiler_params=pltpu.CompilerParams(vmem_limit_bytes=56 * 1024 * 1024),
        cost_estimate=pl.CostEstimate(flops=flops, bytes_accessed=8_000_000, transcendentals=0),
    )


def shape(dims, kind=BF):
    return jax.ShapeDtypeStruct(dims, kind)


def attend(kpos, rank, qpos, q, own, other):
    grid_spec = pltpu.PrefetchScalarGridSpec(
        num_scalar_prefetch=2,
        grid=(HL,),
        in_specs=[
            pl.BlockSpec((8, ROWS), lambda h, *_: (0, 0)),
            pl.BlockSpec((ROWS, 128), lambda h, *_: (0, h)),
            pl.BlockSpec((KEYS // 2, 128), lambda h, *_: (0, h)),
            pl.BlockSpec((KEYS // 2, 128), lambda h, *_: (0, h)),
        ],
        out_specs=[
            pl.BlockSpec((TOK, D), lambda h, *_: (0, 0)),
            pl.BlockSpec((HD, ROWS), lambda h, *_: (h, 0)),
            pl.BlockSpec((1, 8, ROWS), lambda h, *_: (h, 0, 0)),
            pl.BlockSpec((KEYS, 128), lambda h, *_: (0, h)),
            pl.BlockSpec((128, KEYS), lambda h, *_: (h, 0)),
            pl.BlockSpec((ROWS, 128), lambda h, *_: (0, h)),
        ],
        scratch_shapes=[pltpu.VMEM((HW, ROWS), F32), pltpu.VMEM((ROWS, HW), BF)],
    )
    return pl.pallas_call(
        attend_kernel,
        grid_spec=grid_spec,
        out_shape=[
            shape((TOK, D)),
            shape((HW, ROWS), F32),
            shape((HL, 8, ROWS), F32),
            shape((KEYS, 384)),
            shape((384, KEYS)),
            shape((ROWS, 384)),
        ],
        name="attend",
        **settings(5_000_000_000),
    )(kpos, rank, qpos, q, own, other)


def attend_back(kpos, rank, qpos, qs, kvs, kvt, dbr, wo, o, lse):
    grid_spec = pltpu.PrefetchScalarGridSpec(
        num_scalar_prefetch=2,
        grid=(HL,),
        in_specs=[
            pl.BlockSpec((8, ROWS), lambda h, *_: (0, 0)),
            pl.BlockSpec((ROWS, 128), lambda h, *_: (0, h)),
            pl.BlockSpec((KEYS, 128), lambda h, *_: (0, h)),
            pl.BlockSpec((128, KEYS), lambda h, *_: (h, 0)),
            pl.BlockSpec((ROWS, D), lambda h, *_: (0, 0)),
            pl.BlockSpec((128, D), lambda h, *_: (h, 0)),
            pl.BlockSpec((HD, ROWS), lambda h, *_: (h, 0)),
            pl.BlockSpec((1, 8, ROWS), lambda h, *_: (h, 0, 0)),
        ],
        out_specs=[
            pl.BlockSpec((KEYS // 2, 128), lambda h, *_: (0, h)),
            pl.BlockSpec((KEYS // 2, 128), lambda h, *_: (0, h)),
            pl.BlockSpec((ROWS, 128), lambda h, *_: (0, h)),
        ],
        scratch_shapes=[pltpu.VMEM((ROWS, 128), BF), pltpu.VMEM((KEYS, 128), BF)],
    )
    return pl.pallas_call(
        attend_back_kernel,
        grid_spec=grid_spec,
        out_shape=[shape((KEYS // 2, 384)), shape((KEYS // 2, 384)), shape((ROWS, 384))],
        name="attend_back",
        **settings(15_000_000_000),
    )(kpos, rank, qpos, qs, kvs, kvt, dbr, wo, o, lse)


GAIN1, BIAS1, BQ, BV, BOUT, GAIN2, BIAS2, BFC2, BFC1 = range(9)


def project_kernel(
    c_ref, rows_ref, own_ref, other_ref, heads_ref, perm_t_ref, a1_ref, kv_ref, q_ref, vec_ref, w_ref
):
    c = c_ref[0]
    w_ref[pl.ds(pl.multiple_of(c * (D // 2), D // 2), D // 2), :] = own_ref[...]
    w_ref[pl.ds(pl.multiple_of((1 - c) * (D // 2), D // 2), D // 2), :] = other_ref[...]
    vec = w_ref[:, 512:].astype(F32).T[64:80]
    vec_ref[...] = vec
    bqv = dot_nt(vec[0:8].astype(BF), perm_t_ref[...]).astype(BF)
    bias = (
        dot(bqv, heads_ref[0:HW, :])[BQ : BQ + 1]
        + dot(bqv, heads_ref[2 * HW : 3 * HW, :])[BV : BV + 1]
    )
    w = dot(w_ref[...], heads_ref[...]).astype(BF)
    for i in range(TP):
        at = slice(i * TOK, (i + 1) * TOK)
        hat, _ = standardized(rows_ref[i, 0:TOK, :].astype(F32))
        a1_ref[at, :] = (hat * vec[GAIN1 : GAIN1 + 1] + vec[BIAS1 : BIAS1 + 1]).astype(BF)
    for i in range(2):
        at = slice(i * 256, (i + 1) * 256)
        qkv = (dot(a1_ref[at, :], w) + bias).astype(BF)
        q_ref[at, :] = qkv[:, 384:]
        for j in range(4):
            kv_ref[j, at, :] = qkv[:, :384]


def project(c, rows, own, other, heads, perm_t):
    half = pl.BlockSpec((D // 2, COLS), lambda i: (0, 0))
    return pl.pallas_call(
        project_kernel,
        grid=(1,),
        in_specs=[
            pl.BlockSpec(memory_space=pltpu.SMEM),
            pl.BlockSpec((TP, TOK, D), lambda i: (0, 0, 0)),
            half,
            half,
            pl.BlockSpec((COLS, D), lambda i: (0, 0)),
            pl.BlockSpec((HW, D), lambda i: (0, 0)),
        ],
        out_specs=[
            pl.BlockSpec((ROWS, D), lambda i: (0, 0)),
            pl.BlockSpec((4, ROWS, 384), lambda i: (0, 0, 0)),
            pl.BlockSpec((ROWS, 384), lambda i: (0, 0)),
            pl.BlockSpec((16, D), lambda i: (0, 0)),
            pl.BlockSpec((D, COLS), lambda i: (0, 0)),
        ],
        out_shape=[
            shape((ROWS, D)),
            shape((4, ROWS, 384)),
            shape((ROWS, 384)),
            shape((16, D), F32),
            shape((D, COLS)),
        ],
        name="project",
        **settings(2_000_000_000),
    )(c, rows, own, other, heads, perm_t)


def feed_kernel(
    x_ref,
    o_ref,
    rows_ref,
    perm_ref,
    w_ref,
    vec_ref,
    da2_ref,
    act_ref,
    a2_ref,
    du_ref,
    resid_ref,
    op_ref,
    resid_s,
):
    vec = vec_ref[...]
    for i in range(2):
        at = slice(i * 256, (i + 1) * 256)
        op = None
        for j in range(TP):
            first = o_ref[j, :, 2 * i * HW : (2 * i + 1) * HW]
            later = o_ref[j, :, (2 * i + 1) * HW : (2 * i + 2) * HW]
            part = dot(jnp.concatenate([first, later], 0), perm_ref[j * HW : (j + 1) * HW, :])
            op = part if op is None else op + part
        op = op.astype(BF)
        op_ref[at, :] = op
        tok = jnp.concatenate([rows_ref[2 * i, 0:TOK, :], rows_ref[2 * i + 1, 0:TOK, :]], 0)
        dy = jnp.concatenate([rows_ref[2 * i, TOK:, :], rows_ref[2 * i + 1, TOK:, :]], 0)
        resid = tok.astype(F32) + dot(op, w_ref[:, D : 2 * D]) + vec[BOUT : BOUT + 1]
        resid_s[at, :] = resid
        hat, _ = standardized(resid)
        a2 = (hat * vec[GAIN2 : GAIN2 + 1] + vec[BIAS2 : BIAS2 + 1]).astype(BF)
        a2_ref[at, :] = a2
        act, slope = gelu_pair(dot(a2, w_ref[:, 0:D]) + vec[BFC1 : BFC1 + 1])
        du = (dot_nt(dy, w_ref[:, 2 * D :]) * slope).astype(BF)
        du_ref[at, :] = du
        act_ref[at, :] = act.astype(BF)
        da2 = dot_nt(du, w_ref[:, 0:D]).astype(BF)
        da2_ref[2 * i] = da2[:TOK]
        da2_ref[2 * i + 1] = da2[TOK:]
    resid_ref[...] = resid_s[pl.ds(pl.multiple_of(x_ref[0] * TOK, TOK), TOK), :]


def feed(x, o, rows, perm, w, vec):
    whole = pl.BlockSpec(memory_space=pltpu.VMEM)
    return pl.pallas_call(
        feed_kernel,
        in_specs=[pl.BlockSpec(memory_space=pltpu.SMEM)] + [whole] * 5,
        out_specs=[whole] * 6,
        out_shape=[
            shape((TP, TOK, D)),
            shape((ROWS, D)),
            shape((ROWS, D)),
            shape((ROWS, D)),
            shape((TOK, D), F32),
            shape((ROWS, D)),
        ],
        scratch_shapes=[pltpu.VMEM((ROWS, D), F32)],
        name="feed",
        **settings(4_000_000_000),
    )(x, o, rows, perm, w, vec)


def feed_grads_kernel(
    rows_ref,
    perm_ref,
    perm_t_ref,
    heads_ref,
    wo_ref,
    w2_ref,
    act_ref,
    a2_ref,
    du_ref,
    gw_ref,
    mixed_ref,
    gb_ref,
    wo_pad_ref,
    dy_s,
):
    wo_t = dot(perm_t_ref[...], wo_ref[...]).astype(BF)
    wo_pad_ref[...] = dot_tn(heads_ref[...], wo_t).astype(BF)
    for i in range(TP):
        at = slice(i * TOK, (i + 1) * TOK)
        dy_s[at, :] = dot_nt(rows_ref[i, TOK:, :], perm_ref[...]).astype(BF)
    for i in range(3):
        at = slice(i * 256, (i + 1) * 256)
        gw_ref[at, 0:D] = dot_tn(a2_ref[:, at], du_ref[...])
        gw_ref[at, D:] = dot_tn(act_ref[:, at], dy_s[...])
    for i in range(2):
        at = slice(i * 256, (i + 1) * 256)
        mixed_ref[at, :] = dot(act_ref[at, :], w2_ref[...]).astype(BF)
    gb_ref[...] = jnp.broadcast_to(jnp.sum(du_ref[...].astype(F32), 0, keepdims=True), (8, D))


def feed_grads(rows, perm, perm_t, heads, w, act, a2, du):
    whole = pl.BlockSpec((ROWS, D), lambda i: (0, 0))
    return pl.pallas_call(
        feed_grads_kernel,
        grid=(1,),
        in_specs=[
            pl.BlockSpec((TP, 2 * TOK, D), lambda i: (0, 0, 0)),
            pl.BlockSpec((D, D), lambda i: (0, 0)),
            pl.BlockSpec((HW, D), lambda i: (0, 0)),
            pl.BlockSpec((HW, 384), lambda i: (2, 0)),
            pl.BlockSpec((D, D), lambda i: (0, 1)),
            pl.BlockSpec((D, D), lambda i: (0, 2)),
            whole,
            whole,
            whole,
        ],
        out_specs=[
            pl.BlockSpec((D, 2 * D), lambda i: (0, 0)),
            whole,
            pl.BlockSpec((8, D), lambda i: (0, 0)),
            pl.BlockSpec((384, D), lambda i: (0, 0)),
        ],
        out_shape=[shape((D, 2 * D), F32), shape((ROWS, D)), shape((8, D), F32), shape((384, D))],
        scratch_shapes=[pltpu.VMEM((ROWS, D), BF)],
        name="feed_grads",
        **settings(3_000_000_000),
    )(rows, perm, perm_t, heads, w, w, act, a2, du)


def norm2_kernel(da2_ref, resid_ref, dy_ref, vec_ref, dbr_ref, dresid_ref, sums_ref):
    da2 = da2_ref[0].astype(F32)
    for i in range(1, TP):
        da2 = da2 + da2_ref[i].astype(F32)
    hat, rstd = standardized(resid_ref[...])
    dy = dy_ref[...].astype(F32)
    dresid = dy + norm_back(da2 * vec_ref[GAIN2 : GAIN2 + 1, :], hat, rstd)
    dresid_ref[...] = dresid
    dbr = dresid.astype(BF)
    dbr_ref[...] = dbr
    sums_ref[0:1, :] = jnp.sum(dbr.astype(F32), 0, keepdims=True)
    sums_ref[1:2, :] = jnp.sum(da2 * hat, 0, keepdims=True)
    sums_ref[2:3, :] = jnp.sum(da2, 0, keepdims=True)
    sums_ref[3:4, :] = jnp.sum(dy, 0, keepdims=True)
    sums_ref[4:8, :] = jnp.zeros((4, D), F32)


def norm2(da2, resid, dy, vec):
    return pl.pallas_call(
        norm2_kernel,
        out_shape=[shape((TOK, D)), shape((TOK, D), F32), shape((8, D), F32)],
        name="norm2",
        **settings(100_000_000),
    )(da2, resid, dy, vec)


def early_kernel(dq_ref, heads_ref, a1_ref, perm_t_ref, op_ref, dbr_ref, dqn_ref, pack_ref):
    dq = dot_nt(dq_ref[...], heads_ref[0:256, 384:]).astype(BF)
    dqn_ref[...] = dq
    dbr_t = [dot_nt(dbr_ref[i], perm_t_ref[...]).astype(BF) for i in range(TP)]
    dbr_t = jnp.concatenate(dbr_t, 0)
    for i in range(3):
        at = slice(i * 256, (i + 1) * 256)
        pack_ref[at, 0:256] = dot_tn(a1_ref[:, at], dq).astype(BF)
        pack_ref[at, 256 : 256 + HW] = dot_tn(op_ref[:, at], dbr_t).astype(BF)
        pack_ref[at, 256 + HW :] = jnp.zeros((256, 64), BF)


def early(dq, heads, a1, perm_t, op, dbr):
    return pl.pallas_call(
        early_kernel,
        out_shape=[shape((ROWS, 256)), shape((D, 512))],
        name="early",
        **settings(1_000_000_000),
    )(dq, heads, a1, perm_t, op, dbr)


def grads_kernel(
    c_ref,
    dkv_ref,
    dqn_ref,
    early_ref,
    heads_ref,
    w_ref,
    a1_ref,
    rows_ref,
    perm_t_ref,
    gb_ref,
    sums_ref,
    da1_ref,
    own_ref,
    other_ref,
    g_s,
    dqkv_s,
    pack_ref,
):
    ones = jnp.zeros((1, D), F32)
    gain, bias = ones, ones
    for i in range(2):
        at = slice(i * 256, (i + 1) * 256)
        dkv = dkv_ref[0, at, :].astype(F32)
        for j in range(1, 4):
            dkv = dkv + dkv_ref[j, at, :].astype(F32)
        dqkv = dot_nt(dkv.astype(BF), heads_ref[:, :384]).astype(BF)
        dqkv_s[at, :] = dqkv
        dqkv_s[at, 0:128] = dqn_ref[at, 0:128]
        dqkv_s[at, 128:256] = dqkv[:, 128:256] + dqn_ref[at, 128:256]
        da1 = dot_nt(dqkv_s[at, :], w_ref[...])
        da1_ref[at, :] = da1.astype(BF)
        tok = jnp.concatenate([rows_ref[2 * i], rows_ref[2 * i + 1]], 0)
        hat, _ = standardized(tok.astype(F32))
        gain = gain + jnp.sum(da1 * hat, 0, keepdims=True)
        bias = bias + jnp.sum(da1, 0, keepdims=True)
    dsum = jnp.sum(dqkv_s[...].astype(F32), 0, keepdims=True).astype(BF)
    dsum = jnp.broadcast_to(dsum, (8, COLS))
    lanes = lax.broadcasted_iota(jnp.int32, (COLS, HW), 0)
    head = lax.broadcasted_iota(jnp.int32, (COLS, HW), 1)
    g_bq = dot(dot(dsum, (lanes == head).astype(BF)).astype(BF), perm_t_ref[...])
    g_bv = dot(dot(dsum, (lanes == head + 2 * HW).astype(BF)).astype(BF), perm_t_ref[...])
    g_s[...] = jnp.zeros((128, D), F32)
    g_s[64 + GAIN1 : 65 + GAIN1, :] = gain
    g_s[64 + BIAS1 : 65 + BIAS1, :] = bias
    g_s[64 + BQ : 65 + BQ, :] = g_bq[0:1]
    g_s[64 + BV : 65 + BV, :] = g_bv[0:1]
    g_s[64 + BOUT : 64 + BOUT + 4, :] = sums_ref[0:4, :]
    g_s[64 + BFC1 : 65 + BFC1, :] = gb_ref[0:1, :]
    pack_ref[:, 0:128] = early_ref[:, 0:128]
    pack_ref[:, COLS:] = early_ref[:, 256:]
    for i in range(3):
        at = slice(i * 256, (i + 1) * 256)
        g = dot_tn(a1_ref[:, at], dqkv_s[:, 128:])
        pack_ref[at, 128:512] = g[:, :384].astype(BF)
        pack_ref[at, 512:COLS] = (g[:, 384:] + g_s[:, at].T).astype(BF)
    c = c_ref[0]
    own_ref[...] = pack_ref[pl.ds(pl.multiple_of(c * (D // 2), D // 2), D // 2), :]
    other_ref[...] = pack_ref[pl.ds(pl.multiple_of((1 - c) * (D // 2), D // 2), D // 2), :]


def grads(c, dkv, dqn, pack, heads, w, a1, rows, perm_t, gb, sums):
    def whole(*dims):
        return pl.BlockSpec(dims, lambda i: (0,) * len(dims))

    return pl.pallas_call(
        grads_kernel,
        grid=(1,),
        in_specs=[
            pl.BlockSpec(memory_space=pltpu.SMEM),
            whole(4, ROWS, 384),
            whole(ROWS, 256),
            whole(D, 512),
            whole(COLS, 384),
            whole(D, COLS),
            whole(ROWS, D),
            whole(TP, TOK, D),
            whole(HW, D),
            whole(8, D),
            whole(8, D),
        ],
        out_specs=[whole(ROWS, D), whole(D // 2, 896), whole(D // 2, 896)],
        out_shape=[shape((ROWS, D)), shape((D // 2, 896)), shape((D // 2, 896))],
        scratch_shapes=[
            pltpu.VMEM((128, D), F32),
            pltpu.VMEM((ROWS, COLS), BF),
            pltpu.VMEM((D, 896), BF),
        ],
        name="grads",
        **settings(2_000_000_000),
    )(c, dkv, dqn, pack, heads, w, a1, rows, perm_t, gb, sums)


def exchange(v, axes):
    return lax.all_to_all(v, axes, 0, 0, tiled=True)


def spread(v, axes, n):
    return exchange(jnp.broadcast_to(v[None], (n,) + v.shape), axes)


def per_device(
    tokens,
    cotangent,
    block_map,
    ln1_gain,
    ln1_bias,
    w_qkv,
    b_query,
    b_value,
    w_out,
    b_out,
    ln2_gain,
    ln2_bias,
    w_fc1,
    b_fc1,
    w_fc2,
    b_fc2,
):
    perm = jnp.asarray(feature_matrix())
    heads = jnp.asarray(head_matrix())
    z, x, c = lax.axis_index("z"), lax.axis_index("x"), lax.axis_index("c")
    perm_t = lax.dynamic_slice_in_dim(perm, x * HW, HW, 0)

    maps = block_map.reshape(4, 4, 2, 2).transpose(2, 0, 1, 3)
    maps = jnp.where(c == 0, maps, maps[::-1])
    kpos = maps.reshape(-1)
    own = lax.dynamic_slice(maps[0], (z, 0, 0), (1, 4, 2)).reshape(-1)
    before = own[None, :] < own[:, None]
    rank = jnp.sum(before.astype(jnp.int32), 1)
    ordered = jnp.sum(jnp.where(rank[:, None] == jnp.arange(8)[None, :], own[:, None], 0), 0)
    qpos = (ordered[:, None] * BLK + jnp.arange(BLK, dtype=jnp.int32)[None, :]).reshape(1, -1)
    qpos = jnp.broadcast_to(qpos, (8, ROWS))

    own_rows = dot(jnp.concatenate([tokens[0], cotangent[0]], 0), perm).astype(BF)
    all_rows = lax.all_gather(own_rows, "x", axis=0)

    out_cols = dot(jnp.concatenate([w_out, w_fc2], 0), perm).astype(BF)
    vectors = (ln1_gain, ln1_bias, b_query, b_value, b_out, ln2_gain, ln2_bias, b_fc2)
    vectors = sum(jnp.pad(v, (6 * i, 42 - 6 * i)) for i, v in enumerate(vectors))
    vectors = jnp.pad(vectors.reshape(8, 6).T, ((0, 0), (0, 56)))
    qkv_cols = w_qkv.reshape(6, 3, TP, HW).transpose(2, 0, 1, 3).reshape(TP, 6, 3 * HW)
    fc1_cols = w_fc1.reshape(6, 16, TP, 2, 24).transpose(2, 0, 3, 1, 4).reshape(TP, 6, D)
    sent = jnp.concatenate(
        [
            qkv_cols,
            jnp.broadcast_to(vectors[None], (TP, 6, 64)),
            fc1_cols,
            jnp.broadcast_to(out_cols[None, :6], (TP, 6, D)),
        ],
        2,
    )
    got = exchange(sent, "x").reshape(24, -1)
    first = jnp.where(
        jnp.arange(COLS)[None, :] == 3 * HW + BFC1, b_fc1[:, None], got[:, :COLS]
    )
    first = spread(first, ("y", "z"), 16).reshape(D // 2, COLS)
    other = lax.ppermute(first, "c", SWAP)
    rest = jnp.concatenate([got[:, COLS:], out_cols[6:]], 1)
    other, rest = lax.optimization_barrier((other, rest))
    second = lax.all_gather(rest, G, axis=0, tiled=True)

    core = c.reshape(1)
    a1, kv, q, vec, w_heads = project(core, all_rows, first, other, heads, perm_t)
    kv = exchange(kv, "z").reshape(KEYS // 2, 384)
    other = lax.ppermute(kv, "c", SWAP)
    o, o_t, lse, kvs, kvt, qs = attend(kpos, rank, qpos, q, kv, other)
    o = lax.all_gather(o, "x", axis=0)
    da2_part, act, a2, du, resid, o_perm = feed(x.reshape(1), o, all_rows, perm, second, vec)
    g_feed, mixed_part, g_bfc1, wo_pad = feed_grads(
        all_rows, perm, perm_t, heads, second, act, a2, du
    )

    da2 = exchange(da2_part, "x")
    da2, g_feed = lax.optimization_barrier((da2, g_feed))
    dbr, dresid, sums = norm2(da2, resid, own_rows[TOK:], vec)
    r_feed = lax.psum_scatter(g_feed, G, scatter_dimension=0, tiled=True)
    dbr = lax.all_gather(dbr, "x", axis=0)
    dbr, mixed_part = lax.optimization_barrier((dbr, mixed_part))
    mixed_part = exchange(mixed_part.reshape(TP, TOK, D), "x")
    dkv, dkv_other, dq = attend_back(
        kpos, rank, qpos, qs, kvs, kvt, dbr.reshape(ROWS, D), wo_pad, o_t, lse
    )
    dkv_other, mixed_part = lax.optimization_barrier((dkv_other, mixed_part))
    dkv_other = lax.ppermute(dkv_other, "c", SWAP)
    mixed = jnp.sum(mixed_part.astype(F32), 0)
    mixed = (resid + mixed + vec[BFC2 : BFC2 + 1]).astype(BF)
    mixed = dot_nt(mixed, perm).astype(BF)
    dkv = (dkv.astype(F32) + dkv_other.astype(F32)).astype(BF).reshape(4, ROWS, 384)
    dkv = exchange(dkv, "z")
    dqn, pack = early(dq, heads, a1, perm_t, o_perm, dbr)
    da1_part, pack, pack_other = grads(
        core, dkv, dqn, pack, heads, w_heads, a1, all_rows, perm_t, g_bfc1, sums
    )
    da1_part, r_feed = lax.optimization_barrier((da1_part, r_feed))
    da1 = lax.psum_scatter(da1_part, "x", scatter_dimension=0, tiled=True)
    da1 = da1.astype(F32)
    hat1, rstd1 = standardized(own_rows[:TOK].astype(F32))
    dtok = (dresid + norm_back(da1 * vec[GAIN1 : GAIN1 + 1], hat1, rstd1)).astype(BF)
    dtok = dot_nt(dtok, perm).astype(BF)

    pack_other = lax.ppermute(pack_other, "c", SWAP)
    half = (pack.astype(F32) + pack_other.astype(F32)).astype(BF)
    mine = jnp.sum(exchange(half, ("y", "z")).reshape(16, 24, -1).astype(F32), 0)
    last = jnp.concatenate([mine[:, : COLS + HW], r_feed[:, :D]], 1).astype(BF)
    last, dtok = lax.optimization_barrier((last, dtok))
    last = exchange(last.reshape(TP, 6, -1), "x").astype(F32)
    r_qkv = last[:, :, : 3 * HW].reshape(TP, 6, 3, HW).transpose(1, 2, 0, 3).reshape(6, 3 * D)
    r_out = last[:, :, COLS : COLS + HW].transpose(1, 0, 2).reshape(6, D)
    r_fc1 = last[:, :, COLS + HW :].reshape(TP, 6, 2, 16, 24)
    r_fc1 = r_fc1.transpose(1, 3, 0, 2, 4).reshape(6, FF)
    r_vec = jnp.sum(last[:, :, 3 * HW : 3 * HW + 8], 0)
    return (
        mixed[None],
        dtok[None],
        r_vec[:, GAIN1],
        r_vec[:, BIAS1],
        r_qkv,
        r_vec[:, BQ],
        r_vec[:, BV],
        r_out,
        r_vec[:, BOUT],
        r_vec[:, GAIN2],
        r_vec[:, BIAS2],
        r_fc1,
        mine[:, 3 * HW + BFC1],
        r_feed[:, D:],
        r_vec[:, BFC2],
    )


def solution(mesh):
    fine = Mesh(mesh.devices.reshape(4, 4, 4, 2), ("y", "z", "x", "c"))
    rows = P("y", ("z", "x", "c"), None)
    every = ("y", "z", "x", "c")
    vec, mat = P(every), P(every, None)
    in_specs = (rows, rows, P(), vec, vec, mat, vec, vec, mat, vec, vec, vec, mat, vec, mat, vec)
    out_specs = (rows, rows, vec, vec, mat, vec, vec, mat, vec, vec, vec, mat, vec, mat, vec)
    return jax.shard_map(
        per_device, mesh=fine, in_specs=in_specs, out_specs=out_specs, check_vma=False
    )
```

time: 373 us -> 266 us (0.71)
  waiting for transfers between devices: 136 us -> 55.7 us
  blocking collectives: 41.1 us -> 74.6 us
  matrix products: 38.3 us -> 6.48 us
  Pallas kernels: 36.6 us -> 67.8 us
  local copies, waits for them, and re-layouts: 40.9 us -> 15.5 us
  starting transfers between devices: 41.3 us -> 23.1 us
  other arithmetic: 21.7 us -> 7.06 us
    all_to_all x9 -> x6, waiting for transfers between devices: 121 us -> 44.1 us  [exchange(): return lax.all_to_all(v, axes, 0, 0, tiled=True)]
    pallas_call x2 -> x8, Pallas kernels: 36.6 us -> 67.8 us  [the longest x1 17.5 us: attend_back(): pl.pallas_call(attend_back_kernel, grid_spec=grid_spec, out_shape=[shape(...]
    all_gather x0 -> x2, blocking collectives: none -> 30.5 us  [the longest x1 15.7 us: per_device(): o = lax.all_gather(o, 'x', axis=0)]
    all_to_all x9 -> x6, starting transfers between devices: 41.2 us -> 22.9 us  [exchange(): return lax.all_to_all(v, axes, 0, 0, tiled=True)]
    dot_general x13 -> x2, matrix products: 18.5 us -> 3.09 us  [dot(): lax.dot_general(a, b, (((1,), (0,)), ((), ())), preferred_element_type=F32)]
    all_gather x2 -> x1, waiting for transfers between devices: 15.3 us -> 0.01 us  [per_device(): second = lax.all_gather(rest, G, axis=0, tiled=True)]
    dot_general x5 -> x0, matrix products: 10.5 us -> none  [the longest x4 9.37 us: dot_tn(): lax.dot_general(a, b, (((0,), (0,)), ((), ())), preferred_element_type=F32)]
    ppermute x0 -> x4, waiting for transfers between devices: none -> 7.63 us  [the longest x1 3.61 us: per_device(): dkv_other = lax.ppermute(dkv_other, 'c', SWAP)]
  transfers between devices with their start and end apart: 12 -> 14, of which waited for: 11 -> 11; matrix products, arithmetic and copies ran while one was open for 8% -> 6% of each run, Pallas kernels for 5% -> 22%
where the time goes in v2:
time: 266 us; the launch traced here: 265 us
  blocking collectives  74.6 us (28%)
  Pallas kernels  67.8 us (25%)
  waiting for transfers between devices  55.7 us (21%)
  starting transfers between devices  23.1 us (9%)
  local copies, waits for them, and re-layouts  15.5 us (6%)
  between operations  14.3 us (5%)
  other arithmetic  7.06 us (3%)
  matrix products  6.48 us (2%)
    all_to_all x6, waiting for transfers between devices, exchange(): return lax.all_to_all(v, axes, 0, 0, tiled=True)  44.1 us
    all_to_all x2, blocking collectives, exchange(): return lax.all_to_all(v, axes, 0, 0, tiled=True)  44.1 us
    all_to_all x6, starting transfers between devices, exchange(): return lax.all_to_all(v, axes, 0, 0, tiled=True)  22.9 us
    pallas_call x1, Pallas kernels, attend_back(): pl.pallas_call(attend_back_kernel, grid_spec=grid_spec, out_shape=[shape(...  17.5 us
    all_gather x1, blocking collectives, per_device(): o = lax.all_gather(o, 'x', axis=0)  15.7 us
    all_gather x1, blocking collectives, per_device(): dbr = lax.all_gather(dbr, 'x', axis=0)  14.8 us
    pallas_call x1, Pallas kernels, attend(): pl.pallas_call(attend_kernel, grid_spec=grid_spec, out_shape=[shape((TOK,...  13.5 us
    pallas_call x1, Pallas kernels, feed(): pl.pallas_call(feed_kernel, in_specs=[pl.BlockSpec(memory_space=pltpu.SME...  9.83 us
  transfers between devices with their start and end apart: 14, of which 11 were waited for; matrix products, arithmetic and copies ran while one was open for 6% of the time, Pallas kernels for 22%

profile of v2, /device:TPU:0, one launch (start us, length us, event | category | flops | bytes accessed | tf_op | source)
XLA Modules:
  0.0 264.6 jit_solution(312900127675997780)
XLA Ops:
  7.3 2.8 %convolution_convert_fusion = bf16[256,768]{1,0:T(8,128)(2,1)} fusion(bf16[768,768]{1,0:T(8,128)(2,1)} %constant.40.clone.perm_ref, bf16[128,768]{1,0:T(8,128)(2,1)} %bitcast.64, bf16[128,768]{1,0:T(8,128)(2,1)} %bitcast.65), kind=kOutput, calls=%fused_computation.4 | convolution fusion | flops 302972928 | bytes 1966080 | tf_op jit(solution)/shard_map/dot_general | solution.py:56
  12.5 4.4 %all-to-all-start = ((bf16[4,6,2176]{2,1,0:T(8,128)(2,1)}), bf16[4,6,2176]{2,1,0:T(8,128)(2,1)S(1)}, u32[]{:S(2)}, u32[]{:S(2)}) async-start(bf16[4,6,2176]{2,1,0:T(8,128)(2,1)} %copy.91), calls=%async_computation | async-start | bytes 278528 | tf_op jit(solution)/shard_map/all_to_all | solution.py:601
  16.9 6.0 %all-to-all-done = bf16[4,6,2176]{2,1,0:T(8,128)(2,1)S(1)} async-done(((bf16[4,6,2176]{2,1,0:T(8,128)(2,1)}), bf16[4,6,2176]{2,1,0:T(8,128)(2,1)S(1)}, u32[]{:S(2)}, u32[]{:S(2)}) %all-to-all-start) | async-done | bytes 104480 | tf_op jit(solution)/shard_map/all_to_all | solution.py:601
  23.1 17.8 %all_to_all.44 = bf16[16,24,640]{2,1,0:T(8,128)(2,1)S(1)} all-to-all(bf16[16,24,640]{2,1,0:T(8,128)(2,1)S(1)} %broadcast_in_dim.44), channel_id=1, replica_groups=mesh['y'=4,'z'=4,'x'=4,'c'=2] {'y','z'}, dimensions={0} | all-to-all | bytes 983040 | tf_op jit(solution)/shard_map/all_to_all | solution.py:601
  43.6 5.3 %project.1 = (bf16[512,768]{1,0:T(8,128)(2,1)}, bf16[4,512,384]{2,1,0:T(8,128)(2,1)}, bf16[512,384]{1,0:T(8,128)(2,1)}, f32[16,768]{1,0:T(8,128)}, bf16[768,640]{1,0:T(8,128)(2,1)}) custom-call(s32[1]{0:T(128)} %bitcast.2.c_ref, bf16[4,256,768]{2,1,0:T(8,128)(2,1)} %bitcast.48, bf16[384,640]{1,0:T(8,128)(2,1)} %bitcast.58, bf16[384,640]{1,0:T(8,128)(2,1)} %copy-done.25, ...), custom_call_target="tpu_custom_call" | custom-call | flops 2000000000 | bytes 8000000 | tf_op jit(solution)/shard_map/project/pallas_call | solution.py:307
  49.0 26.3 %all_to_all.45 = bf16[4,512,384]{2,1,0:T(8,128)(2,1)S(1)} all-to-all(bf16[4,512,384]{2,1,0:T(8,128)(2,1)} %get-tuple-element.61), channel_id=1, replica_groups=mesh['y'=4,'z'=4,'x'=4,'c'=2] {'z'}, dimensions={0} | all-to-all | bytes 3145728 | tf_op jit(solution)/shard_map/all_to_all | solution.py:601
  77.0 1.7 collective-permute-done.1.other_ref
  79.9 13.5 %attend.1 = (bf16[128,768]{1,0:T(8,128)(2,1)}, f32[192,512]{1,0:T(8,128)}, f32[3,8,512]{2,1,0:T(8,128)}, bf16[4096,384]{1,0:T(8,128)(2,1)}, bf16[384,4096]{1,0:T(8,128)(2,1)}, /*index=5*/bf16[512,384]{1,0:T(8,128)(2,1)}) custom-call(s32[64]{0:T(128)} %reshape.153.kpos, s32[8]{0:T(128)} %copy-done.27, s32[8,512]{1,0:T(8,128)} %broadcast_in_dim.39.qpos_ref, ...), custom_call_target="tpu_custom_call" | custom-call | flops 5000000000 | bytes 8000000 | tf_op jit(solution)/shard_map/attend/pallas_call | solution.py:230
  93.3 15.7 %all-gather.1 = bf16[512,768]{1,0:T(8,128)(2,1)} all-gather(bf16[128,768]{1,0:T(8,128)(2,1)} %get-tuple-element.62), channel_id=3, replica_groups=mesh['y'=4,'z'=4,'x'=4,'c'=2] {'x'}, dimensions={0}, use_global_device_ids=true | all-gather | bytes 983040 | tf_op jit(solution)/shard_map/all_gather | solution.py:674
  109.1 9.8 %feed.1 = (bf16[4,128,768]{2,1,0:T(8,128)(2,1)}, bf16[512,768]{1,0:T(8,128)(2,1)}, bf16[512,768]{1,0:T(8,128)(2,1)}, bf16[512,768]{1,0:T(8,128)(2,1)}, f32[128,768]{1,0:T(8,128)}, /*index=5*/bf16[512,768]{1,0:T(8,128)(2,1)}) custom-call(s32[1]{0:T(128)} %bitcast.x_ref, bf16[4,128,768]{2,1,0:T(8,128)(2,1)} %bitcast.56, bf16[4,256,768]{2,1,0:T(8,128)(2,1)} %bitcast.49, ...), custom_call_target="tpu_custom_call" | custom-call | flops 4000000000 | bytes 8000000 | tf_op jit(solution)/shard_map/feed/pallas_call | solution.py:382
  118.9 3.5 %all-to-all-start.3 = ((bf16[4,128,768]{2,1,0:T(8,128)(2,1)}), bf16[4,128,768]{2,1,0:T(8,128)(2,1)S(1)}, u32[]{:S(2)}, u32[]{:S(2)}) async-start(bf16[4,128,768]{2,1,0:T(8,128)(2,1)} %get-tuple-element.69), calls=%async_computation.3 | async-start | bytes 1572864 | tf_op jit(solution)/shard_map/all_to_all | solution.py:601
  122.5 9.0 %feed_grads.1 = (f32[768,1536]{1,0:T(8,128)}, bf16[512,768]{1,0:T(8,128)(2,1)}, f32[8,768]{1,0:T(8,128)}, bf16[384,768]{1,0:T(8,128)(2,1)}) custom-call(bf16[4,256,768]{2,1,0:T(8,128)(2,1)} %bitcast.50, bf16[768,768]{1,0:T(8,128)(2,1)} %constant.40.clone.perm_ref, bf16[192,768]{1,0:T(8,128)(2,1)} %constant_dynamic-slice_fusion.perm_t_ref, ...), custom_call_target="tpu_custom_call" | custom-call | flops 3000000000 | bytes 8000000 | tf_op jit(solution)/shard_map/feed_grads/pallas_call | solution.py:433
  131.4 2.0 all-to-all-done.3.da2_ref
  135.4 2.6 norm2.1
  137.9 14.8 %all-gather.2 = bf16[512,768]{1,0:T(8,128)(2,1)} all-gather(bf16[128,768]{1,0:T(8,128)(2,1)} %get-tuple-element.75), channel_id=4, replica_groups=mesh['y'=4,'z'=4,'x'=4,'c'=2] {'x'}, dimensions={0}, use_global_device_ids=true | all-gather | bytes 983040 | tf_op jit(solution)/shard_map/all_gather | solution.py:684
  152.7 3.7 %all-to-all-start.4 = ((bf16[4,128,768]{2,1,0:T(8,128)(2,1)}), bf16[4,128,768]{2,1,0:T(8,128)(2,1)S(1)}, u32[]{:S(2)}, u32[]{:S(2)}) async-start(bf16[4,128,768]{2,1,0:T(8,128)(2,1)} %bitcast.14), calls=%async_computation.4 | async-start | bytes 1572864 | tf_op jit(solution)/shard_map/all_to_all | solution.py:601
  156.4 17.5 %attend_back.1 = (bf16[2048,384]{1,0:T(8,128)(2,1)}, bf16[2048,384]{1,0:T(8,128)(2,1)}, bf16[512,384]{1,0:T(8,128)(2,1)}) custom-call(s32[64]{0:T(128)} %reshape.153.kpos, s32[8]{0:T(128)} %copy-done.27, s32[8,512]{1,0:T(8,128)} %broadcast_in_dim.39.qpos_ref, bf16[512,384]{1,0:T(8,128)(2,1)} %get-tuple-element.66.qs_ref, ...), custom_call_target="tpu_custom_call" | custom-call | flops 15000000512 | bytes 8000000 | tf_op jit(solution)/shard_map/attend_back/pallas_call | solution.py:267
  174.1 3.6 %collective-permute-done.2 = bf16[2048,384]{1,0:T(8,128)(2,1)S(1)} collective-permute-done((bf16[2048,384]{1,0:T(8,128)(2,1)}, bf16[2048,384]{1,0:T(8,128)(2,1)S(1)}, u32[]{:S(2)}, u32[]{:S(2)}) %collective-permute-start.2) | collective-permute-done | bytes 1572896 | tf_op jit(solution)/shard_map/ppermute | solution.py:691
  177.7 3.0 %add_convert_fusion = bf16[2048,384]{1,0:T(8,128)(2,1)} fusion(bf16[2048,384]{1,0:T(8,128)(2,1)S(1)} %collective-permute-done.2, bf16[2048,384]{1,0:T(8,128)(2,1)} %get-tuple-element.84), kind=kLoop, calls=%fused_computation | loop fusion | flops 3145728 | bytes 4718592 | tf_op jit(solution)/shard_map/convert_element_type | solution.py:695
  180.6 3.6 %all-to-all-start.5 = ((bf16[4,512,384]{2,1,0:T(8,128)(2,1)}), bf16[4,512,384]{2,1,0:T(8,128)(2,1)S(1)}, u32[]{:S(2)}, u32[]{:S(2)}) async-start(bf16[4,512,384]{2,1,0:T(8,128)(2,1)} %bitcast.16), calls=%async_computation.5 | async-start | bytes 3145728 | tf_op jit(solution)/shard_map/all_to_all | solution.py:601
  184.3 4.1 %early.1 = (bf16[512,256]{1,0:T(8,128)(2,1)}, bf16[768,512]{1,0:T(8,128)(2,1)}) custom-call(bf16[512,384]{1,0:T(8,128)(2,1)} %get-tuple-element.86.dq_ref, bf16[640,768]{1,0:T(8,128)(2,1)} %constant.41.clone.heads_ref, bf16[512,768]{1,0:T(8,128)(2,1)} %get-tuple-element.87.a1_ref, bf16[192,768]{1,0:T(8,128)(2,1)} %constant_dynamic-slice_fusion.perm_t_ref, ...), custom_call_target="tpu_custom_call" | custom-call | flops 1000000000 | bytes 8000000 | tf_op jit(solution)/shard_map/early/pallas_call | solution.py:499
  188.4 20.3 %all-to-all-done.5.dkv_ref = bf16[4,512,384]{2,1,0:T(8,128)(2,1)S(1)} async-done(((bf16[4,512,384]{2,1,0:T(8,128)(2,1)}), bf16[4,512,384]{2,1,0:T(8,128)(2,1)S(1)}, u32[]{:S(2)}, u32[]{:S(2)}) %all-to-all-start.5) | async-done | bytes 1572896 | tf_op jit(solution)/shard_map/all_to_all | solution.py:601
  209.8 6.0 %grads.1 = (bf16[512,768]{1,0:T(8,128)(2,1)}, bf16[384,896]{1,0:T(8,128)(2,1)}, bf16[384,896]{1,0:T(8,128)(2,1)}) custom-call(s32[1]{0:T(128)} %bitcast.2.c_ref, bf16[4,512,384]{2,1,0:T(8,128)(2,1)} %copy-done.5, bf16[512,256]{1,0:T(8,128)(2,1)} %get-tuple-element.89.dqn_ref, bf16[768,512]{1,0:T(8,128)(2,1)} %get-tuple-element.90.early_ref, ...), custom_call_target="tpu_custom_call" | custom-call | flops 2000000000 | bytes 8000000 | tf_op jit(solution)/shard_map/grads/pallas_call | solution.py:572
  217.0 1.2 collective-permute-done.3
  219.2 4.4 %all-to-all-start.6 = ((bf16[16,24,896]{2,1,0:T(8,128)(2,1)}), bf16[16,24,896]{2,1,0:T(8,128)(2,1)S(1)}, u32[]{:S(2)}, u32[]{:S(2)}) async-start(bf16[16,24,896]{2,1,0:T(8,128)(2,1)} %bitcast.47), calls=%async_computation.6 | async-start | bytes 1376256 | tf_op jit(solution)/shard_map/all_to_all | solution.py:601
  224.7 1.2 fusion
  225.9 11.3 %all-to-all-done.6 = bf16[16,24,896]{2,1,0:T(8,128)(2,1)S(1)} async-done(((bf16[16,24,896]{2,1,0:T(8,128)(2,1)}), bf16[16,24,896]{2,1,0:T(8,128)(2,1)S(1)}, u32[]{:S(2)}, u32[]{:S(2)}) %all-to-all-start.6) | async-done | bytes 688160 | tf_op jit(solution)/shard_map/all_to_all | solution.py:601
  237.5 3.1 %reduce-scatter.5.cloned.1.call-done = bf16[128,768]{1,0:T(8,128)(2,1)} async-done(((bf16[512,768]{1,0:T(8,128)(2,1)}), bf16[128,768]{1,0:T(8,128)(2,1)}) %reduce-scatter.5.cloned.1.call-update) | async-done | bytes 196624 | tf_op jit(solution)/shard_map/reduce_scatter | solution.py:702
  241.7 2.2 convolution_convert_fusion.1
  244.5 3.3 %all-to-all-start.7 = ((bf16[4,6,1600]{2,1,0:T(8,128)(2,1)}), bf16[4,6,1600]{2,1,0:T(8,128)(2,1)S(1)}, u32[]{:S(2)}, u32[]{:S(2)}) async-start(bf16[4,6,1600]{2,1,0:T(8,128)(2,1)} %reshape.166), calls=%async_computation.9 | async-start | bytes 212992 | tf_op jit(solution)/shard_map/all_to_all | solution.py:601
  249.2 4.5 %all-to-all-done.7 = bf16[4,6,1600]{2,1,0:T(8,128)(2,1)S(1)} async-done(((bf16[4,6,1600]{2,1,0:T(8,128)(2,1)}), bf16[4,6,1600]{2,1,0:T(8,128)(2,1)S(1)}, u32[]{:S(2)}, u32[]{:S(2)}) %all-to-all-start.7) | async-done | bytes 76832 | tf_op jit(solution)/shard_map/all_to_all | solution.py:601
  254.4 1.2 reshape.171
  (143 shorter events, 20.8 us)
Async XLA Ops:
  7.2 3.0 %copy-start = (bf16[768,768]{1,0:T(8,128)(2,1)S(1)}, bf16[768,768]{1,0:T(8,128)(2,1)}, u32[]{:S(2)}) copy-start(bf16[768,768]{1,0:T(8,128)(2,1)} %constant.40.clone.perm_ref) | copy-start | bytes 3538948
  7.2 3.0 %copy-start.13 = (bf16[6,768]{1,0:T(8,128)(2,1)S(1)}, bf16[6,768]{1,0:T(8,128)(2,1)}, u32[]{:S(2)}) copy-start(bf16[6,768]{1,0:T(8,128)(2,1)} %param.26) | copy-start | bytes 27652
  7.2 3.0 %copy-start.11 = (bf16[24,768]{1,0:T(8,128)(2,1)S(1)}, bf16[24,768]{1,0:T(8,128)(2,1)}, u32[]{:S(2)}) copy-start(bf16[24,768]{1,0:T(8,128)(2,1)} %param.32) | copy-start | bytes 110596
  7.2 36.4 %all-gather.8.cloned.1.call-start = ((), (), s32[]{:S(2)}) async-start(), calls=%async_computation.13 | async-start | bytes 1966080 | tf_op jit(solution)/shard_map/all_gather | solution.py:642
  7.3 3.2 %copy-start.10 = (bf16[6,3072]{1,0:T(8,128)(2,1)S(1)}, bf16[6,3072]{1,0:T(8,128)(2,1)}, u32[]{:S(2)}) copy-start(bf16[6,3072]{1,0:T(8,128)(2,1)} %param.30) | copy-start | bytes 110596
  10.1 1.3 copy-start.18
  10.1 1.3 copy-start.19
  10.1 1.3 copy-start.20
  10.1 1.3 copy-start.21
  10.2 12.8 %copy-start.15 = (bf16[24]{0:T(256)(128)(2,1)S(1)}, bf16[24]{0:T(256)(128)(2,1)}, u32[]{:S(2)}) copy-start(bf16[24]{0:T(256)(128)(2,1)} %param.31) | copy-start | bytes 148
  12.5 10.4 %all-to-all-start = ((bf16[4,6,2176]{2,1,0:T(8,128)(2,1)}), bf16[4,6,2176]{2,1,0:T(8,128)(2,1)S(1)}, u32[]{:S(2)}, u32[]{:S(2)}) async-start(bf16[4,6,2176]{2,1,0:T(8,128)(2,1)} %copy.91), calls=%async_computation | async-start | bytes 278528 | tf_op jit(solution)/shard_map/all_to_all | solution.py:601
  16.9 92.2 %all-gather.6.cloned.1.call-start = ((), (), s32[]{:S(2)}) async-start(), calls=%async_computation.10 | async-start | bytes 3649536 | tf_op jit(solution)/shard_map/all_gather | solution.py:667
  40.9 2.7 %copy-start.8 = (bf16[16,24,640]{2,1,0:T(8,128)(2,1)}, bf16[16,24,640]{2,1,0:T(8,128)(2,1)S(1)}, u32[]{:S(2)}) copy-start(bf16[16,24,640]{2,1,0:T(8,128)(2,1)S(1)} %all_to_all.44) | copy-start | bytes 1474564
  40.9 1.9 collective-permute-start
  49.0 26.3 %copy-start.14 = (s32[32,2]{0,1:T(2,128)S(1)}, s32[32,2]{0,1:T(2,128)}, u32[]{:S(2)}) copy-start(s32[32,2]{0,1:T(2,128)} %param.20) | copy-start | bytes 772
  75.3 4.0 %copy-start.4 = (bf16[4,512,384]{2,1,0:T(8,128)(2,1)}, bf16[4,512,384]{2,1,0:T(8,128)(2,1)S(1)}, u32[]{:S(2)}) copy-start(bf16[4,512,384]{2,1,0:T(8,128)(2,1)S(1)} %all_to_all.45) | copy-start | bytes 4718596
  75.3 3.4 %collective-permute-start.1 = (bf16[2048,384]{1,0:T(8,128)(2,1)S(1)}, bf16[2048,384]{1,0:T(8,128)(2,1)S(1)}, u32[]{:S(2)}, u32[]{:S(2)}) collective-permute-start(bf16[2048,384]{1,0:T(8,128)(2,1)S(1)} %bitcast.52), channel_id=1, source_target_pairs={{0,1},{1,0},{2,3},{3,2},{4,5},{5,4},{6,7},{7,6},{8,9},{9,8},{10,11... | collective-permute-start | bytes 4718600 | tf_op jit(solution)/shard_map/ppermute | solution.py:672
  76.1 3.2 %copy-start.27 = (s32[8]{0:T(128)}, s32[8]{0:T(128)S(1)}, u32[]{:S(2)}) copy-start(s32[8]{0:T(128)S(1)} %convert_reduce_fusion.3.rank) | copy-start | bytes 100
  118.9 14.5 %all-to-all-start.3 = ((bf16[4,128,768]{2,1,0:T(8,128)(2,1)}), bf16[4,128,768]{2,1,0:T(8,128)(2,1)S(1)}, u32[]{:S(2)}, u32[]{:S(2)}) async-start(bf16[4,128,768]{2,1,0:T(8,128)(2,1)} %get-tuple-element.69), calls=%async_computation.3 | async-start | bytes 1572864 | tf_op jit(solution)/shard_map/all_to_all | solution.py:601
  122.4 94.4 %reduce-scatter.3.cloned.1.call-start = ((), (), s32[]{:S(2)}) async-start(), calls=%async_computation.11 | async-start | bytes 4866048 | tf_op jit(solution)/shard_map/reduce_scatter | solution.py:683
  152.7 21.3 %all-to-all-start.4 = ((bf16[4,128,768]{2,1,0:T(8,128)(2,1)}), bf16[4,128,768]{2,1,0:T(8,128)(2,1)S(1)}, u32[]{:S(2)}, u32[]{:S(2)}) async-start(bf16[4,128,768]{2,1,0:T(8,128)(2,1)} %bitcast.14), calls=%async_computation.4 | async-start | bytes 1572864 | tf_op jit(solution)/shard_map/all_to_all | solution.py:601
  174.0 3.7 %collective-permute-start.2 = (bf16[2048,384]{1,0:T(8,128)(2,1)}, bf16[2048,384]{1,0:T(8,128)(2,1)S(1)}, u32[]{:S(2)}, u32[]{:S(2)}) collective-permute-start(bf16[2048,384]{1,0:T(8,128)(2,1)} %get-tuple-element.85), channel_id=1, source_target_pairs={{0,1},{1,0},{2,3},{3,2},{4,5},{5,4},{6,7},{7,6},{8,9},{9,8},{10,11... | collective-permute-start | bytes 4718600 | tf_op jit(solution)/shard_map/ppermute | solution.py:691
  180.6 28.0 %all-to-all-start.5 = ((bf16[4,512,384]{2,1,0:T(8,128)(2,1)}), bf16[4,512,384]{2,1,0:T(8,128)(2,1)S(1)}, u32[]{:S(2)}, u32[]{:S(2)}) async-start(bf16[4,512,384]{2,1,0:T(8,128)(2,1)} %bitcast.16), calls=%async_computation.5 | async-start | bytes 3145728 | tf_op jit(solution)/shard_map/all_to_all | solution.py:601
  184.2 56.3 %reduce-scatter.5.cloned.1.call-start = ((), (), s32[]{:S(2)}) async-start(), calls=%async_computation.12 | async-start | bytes 983040 | tf_op jit(solution)/shard_map/reduce_scatter | solution.py:702
  215.9 2.4 copy-start.7
  215.9 2.4 collective-permute-start.3
  219.2 5.4 %copy-start.1 = (bf16[768,768]{1,0:T(8,128)(2,1)S(1)}, bf16[768,768]{1,0:T(8,128)(2,1)}, u32[]{:S(2)}) copy-start(bf16[768,768]{1,0:T(8,128)(2,1)} %constant.40.clone.perm_ref) | copy-start | bytes 3538948
  219.2 5.4 %copy-start.6 = (f32[128,768]{1,0:T(8,128)S(1)}, f32[128,768]{1,0:T(8,128)}, u32[]{:S(2)}) copy-start(f32[128,768]{1,0:T(8,128)} %get-tuple-element.65.resid_ref) | copy-start | bytes 1179652
  219.2 18.0 %all-to-all-start.6 = ((bf16[16,24,896]{2,1,0:T(8,128)(2,1)}), bf16[16,24,896]{2,1,0:T(8,128)(2,1)S(1)}, u32[]{:S(2)}, u32[]{:S(2)}) async-start(bf16[16,24,896]{2,1,0:T(8,128)(2,1)} %bitcast.47), calls=%async_computation.6 | async-start | bytes 1376256 | tf_op jit(solution)/shard_map/all_to_all | solution.py:601
  224.6 12.7 %copy-start.9 = (f32[24,1536]{1,0:T(8,128)S(1)}, f32[24,1536]{1,0:T(8,128)}, u32[]{:S(2)}) copy-start(f32[24,1536]{1,0:T(8,128)} %reduce-scatter.3.cloned.1.call-done) | copy-start | bytes 442372
  224.7 17.0 %copy-start.26 = (f32[128,768]{1,0:T(8,128)S(1)}, f32[128,768]{1,0:T(8,128)}, u32[]{:S(2)}) copy-start(f32[128,768]{1,0:T(8,128)} %get-tuple-element.99) | copy-start | bytes 1179652
  244.5 9.1 %all-to-all-start.7 = ((bf16[4,6,1600]{2,1,0:T(8,128)(2,1)}), bf16[4,6,1600]{2,1,0:T(8,128)(2,1)S(1)}, u32[]{:S(2)}, u32[]{:S(2)}) async-start(bf16[4,6,1600]{2,1,0:T(8,128)(2,1)} %reshape.166), calls=%async_computation.9 | async-start | bytes 212992 | tf_op jit(solution)/shard_map/all_to_all | solution.py:601
  (10 other events, 11.6 us)
Sparse Core Ops, SparseCore 0:
  10.3 28.9 all-gather.7
  42.9 47.6 all-gather.5
  133.6 83.1 reduce-scatter.2
  219.2 21.3 reduce-scatter.4

commit v3 on v2

--- a/solution.py
+++ b/solution.py
@@ -49,6 +49,14 @@
             out[HW + h * HD + d, h * 128 + d] = 1
             out[2 * HW + h * HD + d, h * 128 + HD + d] = 1
             out[h * HD + d, 384 + h * 128 + d] = 1
+    return out.astype(jnp.bfloat16)
+
+
+def place_matrix():
+    out = np.zeros((2 * HW, 384), np.float32)
+    for h in range(HL):
+        for d in range(HD):
+            out[HW + h * HD + d, h * 128 + HD + d] = 1
     return out.astype(jnp.bfloat16)
 
 
@@ -150,7 +158,7 @@
     kvs_ref,
     kvt_ref,
     dbr_ref,
-    wo_ref,
+    place_ref,
     o_ref,
     lse_ref,
     own_ref,
@@ -159,7 +167,7 @@
     dos,
     acc,
 ):
-    do_all = dot_nt(dbr_ref[...], wo_ref[...]).astype(BF)
+    do_all = dot(dbr_ref[...], place_ref[...]).astype(BF)
     for b in range(ROWS // BLK):
         at = pl.multiple_of(rank[b] * BLK, BLK)
         dos[pl.ds(at, BLK), :] = do_all[b * BLK : (b + 1) * BLK, :]
@@ -243,7 +251,7 @@
     )(kpos, rank, qpos, q, own, other)
 
 
-def attend_back(kpos, rank, qpos, qs, kvs, kvt, dbr, wo, o, lse):
+def attend_back(kpos, rank, qpos, qs, kvs, kvt, dbr, place, o, lse):
     grid_spec = pltpu.PrefetchScalarGridSpec(
         num_scalar_prefetch=2,
         grid=(HL,),
@@ -252,8 +260,8 @@
             pl.BlockSpec((ROWS, 128), lambda h, *_: (0, h)),
             pl.BlockSpec((KEYS, 128), lambda h, *_: (0, h)),
             pl.BlockSpec((128, KEYS), lambda h, *_: (h, 0)),
-            pl.BlockSpec((ROWS, D), lambda h, *_: (0, 0)),
-            pl.BlockSpec((128, D), lambda h, *_: (h, 0)),
+            pl.BlockSpec((ROWS, 2 * HW), lambda h, *_: (0, 0)),
+            pl.BlockSpec((2 * HW, 128), lambda h, *_: (0, h)),
             pl.BlockSpec((HD, ROWS), lambda h, *_: (h, 0)),
             pl.BlockSpec((1, 8, ROWS), lambda h, *_: (h, 0, 0)),
         ],
@@ -270,7 +278,7 @@
         out_shape=[shape((KEYS // 2, 384)), shape((KEYS // 2, 384)), shape((ROWS, 384))],
         name="attend_back",
         **settings(15_000_000_000),
-    )(kpos, rank, qpos, qs, kvs, kvt, dbr, wo, o, lse)
+    )(kpos, rank, qpos, qs, kvs, kvt, dbr, place, o, lse)
 
 
 GAIN1, BIAS1, BQ, BV, BOUT, GAIN2, BIAS2, BFC2, BFC1 = range(9)
@@ -348,7 +356,14 @@
     resid_ref,
     op_ref,
     resid_s,
+    w_s,
+    sems,
 ):
+    copies = [
+        pltpu.make_async_copy(w_ref.at[:, pl.ds(i * D, D)], w_s.at[i], sems.at[i]) for i in range(3)
+    ]
+    for i in (1, 0, 2):
+        copies[i].start()
     vec = vec_ref[...]
     for i in range(2):
         at = slice(i * 256, (i + 1) * 256)
@@ -362,16 +377,22 @@
         op_ref[at, :] = op
         tok = jnp.concatenate([rows_ref[2 * i, 0:TOK, :], rows_ref[2 * i + 1, 0:TOK, :]], 0)
         dy = jnp.concatenate([rows_ref[2 * i, TOK:, :], rows_ref[2 * i + 1, TOK:, :]], 0)
-        resid = tok.astype(F32) + dot(op, w_ref[:, D : 2 * D]) + vec[BOUT : BOUT + 1]
+        if i == 0:
+            copies[1].wait()
+        resid = tok.astype(F32) + dot(op, w_s[1]) + vec[BOUT : BOUT + 1]
         resid_s[at, :] = resid
         hat, _ = standardized(resid)
         a2 = (hat * vec[GAIN2 : GAIN2 + 1] + vec[BIAS2 : BIAS2 + 1]).astype(BF)
         a2_ref[at, :] = a2
-        act, slope = gelu_pair(dot(a2, w_ref[:, 0:D]) + vec[BFC1 : BFC1 + 1])
-        du = (dot_nt(dy, w_ref[:, 2 * D :]) * slope).astype(BF)
+        if i == 0:
+            copies[0].wait()
+        act, slope = gelu_pair(dot(a2, w_s[0]) + vec[BFC1 : BFC1 + 1])
+        if i == 0:
+            copies[2].wait()
+        du = (dot_nt(dy, w_s[2]) * slope).astype(BF)
         du_ref[at, :] = du
         act_ref[at, :] = act.astype(BF)
-        da2 = dot_nt(du, w_ref[:, 0:D]).astype(BF)
+        da2 = dot_nt(du, w_s[0]).astype(BF)
         da2_ref[2 * i] = da2[:TOK]
         da2_ref[2 * i + 1] = da2[TOK:]
     resid_ref[...] = resid_s[pl.ds(pl.multiple_of(x_ref[0] * TOK, TOK), TOK), :]
@@ -381,7 +402,9 @@
     whole = pl.BlockSpec(memory_space=pltpu.VMEM)
     return pl.pallas_call(
         feed_kernel,
-        in_specs=[pl.BlockSpec(memory_space=pltpu.SMEM)] + [whole] * 5,
+        in_specs=[pl.BlockSpec(memory_space=pltpu.SMEM)]
+        + [whole] * 3
+        + [pl.BlockSpec(memory_space=pl.ANY), whole],
         out_specs=[whole] * 6,
         out_shape=[
             shape((TP, TOK, D)),
@@ -391,7 +414,11 @@
             shape((TOK, D), F32),
             shape((ROWS, D)),
         ],
-        scratch_shapes=[pltpu.VMEM((ROWS, D), F32)],
+        scratch_shapes=[
+            pltpu.VMEM((ROWS, D), F32),
+            pltpu.VMEM((3, D, D), BF),
+            pltpu.SemaphoreType.DMA((3,)),
+        ],
         name="feed",
         **settings(4_000_000_000),
     )(x, o, rows, perm, w, vec)
@@ -400,9 +427,6 @@
 def feed_grads_kernel(
     rows_ref,
     perm_ref,
-    perm_t_ref,
-    heads_ref,
-    wo_ref,
     w2_ref,
     act_ref,
     a2_ref,
@@ -410,25 +434,26 @@
     gw_ref,
     mixed_ref,
     gb_ref,
-    wo_pad_ref,
     dy_s,
 ):
-    wo_t = dot(perm_t_ref[...], wo_ref[...]).astype(BF)
-    wo_pad_ref[...] = dot_tn(heads_ref[...], wo_t).astype(BF)
     for i in range(TP):
         at = slice(i * TOK, (i + 1) * TOK)
         dy_s[at, :] = dot_nt(rows_ref[i, TOK:, :], perm_ref[...]).astype(BF)
-    for i in range(3):
-        at = slice(i * 256, (i + 1) * 256)
-        gw_ref[at, 0:D] = dot_tn(a2_ref[:, at], du_ref[...])
-        gw_ref[at, D:] = dot_tn(act_ref[:, at], dy_s[...])
+    for core in range(2):
+        at = slice(core * 384, (core + 1) * 384)
+        g_fc1 = dot_tn(a2_ref[:, at], du_ref[...]).astype(BF)
+        g_fc2 = dot_tn(act_ref[:, at], dy_s[...]).astype(BF)
+        for y in range(4):
+            to = slice(y * 192 + core * 96, y * 192 + (core + 1) * 96)
+            gw_ref[to, 0:D] = g_fc1[y * 96 : (y + 1) * 96]
+            gw_ref[to, D:] = g_fc2[y * 96 : (y + 1) * 96]
     for i in range(2):
         at = slice(i * 256, (i + 1) * 256)
         mixed_ref[at, :] = dot(act_ref[at, :], w2_ref[...]).astype(BF)
     gb_ref[...] = jnp.broadcast_to(jnp.sum(du_ref[...].astype(F32), 0, keepdims=True), (8, D))
 
 
-def feed_grads(rows, perm, perm_t, heads, w, act, a2, du):
+def feed_grads(rows, perm, w, act, a2, du):
     whole = pl.BlockSpec((ROWS, D), lambda i: (0, 0))
     return pl.pallas_call(
         feed_grads_kernel,
@@ -436,9 +461,6 @@
         in_specs=[
             pl.BlockSpec((TP, 2 * TOK, D), lambda i: (0, 0, 0)),
             pl.BlockSpec((D, D), lambda i: (0, 0)),
-            pl.BlockSpec((HW, D), lambda i: (0, 0)),
-            pl.BlockSpec((HW, 384), lambda i: (2, 0)),
-            pl.BlockSpec((D, D), lambda i: (0, 1)),
             pl.BlockSpec((D, D), lambda i: (0, 2)),
             whole,
             whole,
@@ -448,16 +470,17 @@
             pl.BlockSpec((D, 2 * D), lambda i: (0, 0)),
             whole,
             pl.BlockSpec((8, D), lambda i: (0, 0)),
-            pl.BlockSpec((384, D), lambda i: (0, 0)),
-        ],
-        out_shape=[shape((D, 2 * D), F32), shape((ROWS, D)), shape((8, D), F32), shape((384, D))],
+        ],
+        out_shape=[shape((D, 2 * D)), shape((ROWS, D)), shape((8, D), F32)],
         scratch_shapes=[pltpu.VMEM((ROWS, D), BF)],
         name="feed_grads",
         **settings(3_000_000_000),
-    )(rows, perm, perm_t, heads, w, w, act, a2, du)
-
-
-def norm2_kernel(da2_ref, resid_ref, dy_ref, vec_ref, dbr_ref, dresid_ref, sums_ref):
+    )(rows, perm, w, act, a2, du)
+
+
+def norm2_kernel(
+    da2_ref, resid_ref, dy_ref, vec_ref, wo_ref, perm_ref, send_ref, dresid_ref, sums_ref
+):
     da2 = da2_ref[0].astype(F32)
     for i in range(1, TP):
         da2 = da2 + da2_ref[i].astype(F32)
@@ -466,7 +489,12 @@
     dresid = dy + norm_back(da2 * vec_ref[GAIN2 : GAIN2 + 1, :], hat, rstd)
     dresid_ref[...] = dresid
     dbr = dresid.astype(BF)
-    dbr_ref[...] = dbr
+    do = dot_nt(dbr, wo_ref[...]).astype(BF)
+    dbr_nat = dot_nt(dbr, perm_ref[...]).astype(BF)
+    do_nat = dot_nt(do, perm_ref[...]).astype(BF)
+    for i in range(TP):
+        send_ref[i, :, 0:HW] = dbr_nat[:, i * HW : (i + 1) * HW]
+        send_ref[i, :, HW:] = do_nat[:, i * HW : (i + 1) * HW]
     sums_ref[0:1, :] = jnp.sum(dbr.astype(F32), 0, keepdims=True)
     sums_ref[1:2, :] = jnp.sum(da2 * hat, 0, keepdims=True)
     sums_ref[2:3, :] = jnp.sum(da2, 0, keepdims=True)
@@ -474,20 +502,32 @@
     sums_ref[4:8, :] = jnp.zeros((4, D), F32)
 
 
-def norm2(da2, resid, dy, vec):
+def norm2(da2, resid, dy, vec, w, perm):
+    def whole(*dims):
+        return pl.BlockSpec(dims, lambda i: (0,) * len(dims))
+
     return pl.pallas_call(
         norm2_kernel,
-        out_shape=[shape((TOK, D)), shape((TOK, D), F32), shape((8, D), F32)],
+        grid=(1,),
+        in_specs=[
+            whole(TP, TOK, D),
+            whole(TOK, D),
+            pl.BlockSpec((TOK, D), lambda i: (1, 0)),
+            whole(16, D),
+            pl.BlockSpec((D, D), lambda i: (0, 1)),
+            whole(D, D),
+        ],
+        out_specs=[whole(TP, TOK, 2 * HW), whole(TOK, D), whole(8, D)],
+        out_shape=[shape((TP, TOK, 2 * HW)), shape((TOK, D), F32), shape((8, D), F32)],
         name="norm2",
         **settings(100_000_000),
-    )(da2, resid, dy, vec)
-
-
-def early_kernel(dq_ref, heads_ref, a1_ref, perm_t_ref, op_ref, dbr_ref, dqn_ref, pack_ref):
+    )(da2, resid, dy, vec, w, perm)
+
+
+def early_kernel(dq_ref, heads_ref, a1_ref, op_ref, dbr_ref, dqn_ref, pack_ref):
     dq = dot_nt(dq_ref[...], heads_ref[0:256, 384:]).astype(BF)
     dqn_ref[...] = dq
-    dbr_t = [dot_nt(dbr_ref[i], perm_t_ref[...]).astype(BF) for i in range(TP)]
-    dbr_t = jnp.concatenate(dbr_t, 0)
+    dbr_t = dbr_ref[:, 0:HW]
     for i in range(3):
         at = slice(i * 256, (i + 1) * 256)
         pack_ref[at, 0:256] = dot_tn(a1_ref[:, at], dq).astype(BF)
@@ -495,13 +535,13 @@
         pack_ref[at, 256 + HW :] = jnp.zeros((256, 64), BF)
 
 
-def early(dq, heads, a1, perm_t, op, dbr):
+def early(dq, heads, a1, op, dbr):
     return pl.pallas_call(
         early_kernel,
         out_shape=[shape((ROWS, 256)), shape((D, 512))],
         name="early",
         **settings(1_000_000_000),
-    )(dq, heads, a1, perm_t, op, dbr)
+    )(dq, heads, a1, op, dbr)
 
 
 def grads_kernel(
@@ -638,9 +678,6 @@
     qpos = (ordered[:, None] * BLK + jnp.arange(BLK, dtype=jnp.int32)[None, :]).reshape(1, -1)
     qpos = jnp.broadcast_to(qpos, (8, ROWS))
 
-    own_rows = dot(jnp.concatenate([tokens[0], cotangent[0]], 0), perm).astype(BF)
-    all_rows = lax.all_gather(own_rows, "x", axis=0)
-
     out_cols = dot(jnp.concatenate([w_out, w_fc2], 0), perm).astype(BF)
     vectors = (ln1_gain, ln1_bias, b_query, b_value, b_out, ln2_gain, ln2_bias, b_fc2)
     vectors = sum(jnp.pad(v, (6 * i, 42 - 6 * i)) for i, v in enumerate(vectors))
@@ -656,7 +693,12 @@
         ],
         2,
     )
+    both = jnp.concatenate([tokens[0], cotangent[0]], 0)
+    own_rows = dot(both, perm).astype(BF)
+    all_rows = lax.all_gather(own_rows, "x", axis=0)
+
     got = exchange(sent, "x").reshape(24, -1)
+    got, perm_t = lax.optimization_barrier((got, perm_t))
     first = jnp.where(
         jnp.arange(COLS)[None, :] == 3 * HW + BFC1, b_fc1[:, None], got[:, :COLS]
     )
@@ -673,44 +715,45 @@
     o, o_t, lse, kvs, kvt, qs = attend(kpos, rank, qpos, q, kv, other)
     o = lax.all_gather(o, "x", axis=0)
     da2_part, act, a2, du, resid, o_perm = feed(x.reshape(1), o, all_rows, perm, second, vec)
-    g_feed, mixed_part, g_bfc1, wo_pad = feed_grads(
-        all_rows, perm, perm_t, heads, second, act, a2, du
-    )
+    g_feed, mixed_part, g_bfc1 = feed_grads(all_rows, perm, second, act, a2, du)
 
     da2 = exchange(da2_part, "x")
     da2, g_feed = lax.optimization_barrier((da2, g_feed))
-    dbr, dresid, sums = norm2(da2, resid, own_rows[TOK:], vec)
-    r_feed = lax.psum_scatter(g_feed, G, scatter_dimension=0, tiled=True)
-    dbr = lax.all_gather(dbr, "x", axis=0)
+    dbr, dresid, sums = norm2(da2, resid, own_rows, vec, second, perm)
+    r_feed = lax.psum_scatter(g_feed, "y", scatter_dimension=0, tiled=True)
+    dbr = exchange(dbr, "x").reshape(ROWS, 2 * HW)
     dbr, mixed_part = lax.optimization_barrier((dbr, mixed_part))
     mixed_part = exchange(mixed_part.reshape(TP, TOK, D), "x")
     dkv, dkv_other, dq = attend_back(
-        kpos, rank, qpos, qs, kvs, kvt, dbr.reshape(ROWS, D), wo_pad, o_t, lse
-    )
-    dkv_other, mixed_part = lax.optimization_barrier((dkv_other, mixed_part))
+        kpos, rank, qpos, qs, kvs, kvt, dbr, jnp.asarray(place_matrix()), o_t, lse
+    )
+    dkv_other, mixed_part, r_feed = lax.optimization_barrier((dkv_other, mixed_part, r_feed))
+    r_feed = lax.psum_scatter(r_feed, ("c", "z"), scatter_dimension=0, tiled=True)
     dkv_other = lax.ppermute(dkv_other, "c", SWAP)
     mixed = jnp.sum(mixed_part.astype(F32), 0)
     mixed = (resid + mixed + vec[BFC2 : BFC2 + 1]).astype(BF)
     mixed = dot_nt(mixed, perm).astype(BF)
     dkv = (dkv.astype(F32) + dkv_other.astype(F32)).astype(BF).reshape(4, ROWS, 384)
     dkv = exchange(dkv, "z")
-    dqn, pack = early(dq, heads, a1, perm_t, o_perm, dbr)
+    dkv, r_feed = lax.optimization_barrier((dkv, r_feed))
+    dqn, pack = early(dq, heads, a1, o_perm, dbr)
     da1_part, pack, pack_other = grads(
         core, dkv, dqn, pack, heads, w_heads, a1, all_rows, perm_t, g_bfc1, sums
     )
-    da1_part, r_feed = lax.optimization_barrier((da1_part, r_feed))
     da1 = lax.psum_scatter(da1_part, "x", scatter_dimension=0, tiled=True)
     da1 = da1.astype(F32)
     hat1, rstd1 = standardized(own_rows[:TOK].astype(F32))
     dtok = (dresid + norm_back(da1 * vec[GAIN1 : GAIN1 + 1], hat1, rstd1)).astype(BF)
     dtok = dot_nt(dtok, perm).astype(BF)
 
+    r_feed = r_feed.astype(F32)
     pack_other = lax.ppermute(pack_other, "c", SWAP)
     half = (pack.astype(F32) + pack_other.astype(F32)).astype(BF)
     mine = jnp.sum(exchange(half, ("y", "z")).reshape(16, 24, -1).astype(F32), 0)
     last = jnp.concatenate([mine[:, : COLS + HW], r_feed[:, :D]], 1).astype(BF)
-    last, dtok = lax.optimization_barrier((last, dtok))
-    last = exchange(last.reshape(TP, 6, -1), "x").astype(F32)
+    last = exchange(last.reshape(TP, 6, -1), "x")
+    last, dtok, mixed = lax.optimization_barrier((last, dtok, mixed))
+    last = last.astype(F32)
     r_qkv = last[:, :, : 3 * HW].reshape(TP, 6, 3, HW).transpose(1, 2, 0, 3).reshape(6, 3 * D)
     r_out = last[:, :, COLS : COLS + HW].transpose(1, 0, 2).reshape(6, D)
     r_fc1 = last[:, :, COLS + HW :].reshape(TP, 6, 2, 16, 24)

time: 266 us -> 260 us (0.977)
  waiting for transfers between devices: 55.7 us -> 52.4 us
  blocking collectives: 74.6 us -> 71.4 us
    all_to_all x6, waiting for transfers between devices: 44.1 us -> 22.8 us  [exchange(): return lax.all_to_all(v, axes, 0, 0, tiled=True)]
    reduce_scatter x1 -> x2, waiting for transfers between devices: 0.8 us -> 21.8 us  [the longest x1 21.8 us: per_device(): lax.psum_scatter(r_feed, ('c', 'z'), scatter_dimension=0, tiled=True)]
    all_gather x1 -> x0, blocking collectives: 14.8 us -> none  [per_device(): dbr = lax.all_gather(dbr, 'x', axis=0)]
    all_to_all x2 -> x3, blocking collectives: 44.1 us -> 55.7 us  [exchange(): return lax.all_to_all(v, axes, 0, 0, tiled=True)]
    reduce_scatter x1, waiting for transfers between devices: 3.08 us -> 0.01 us  [per_device(): da1 = lax.psum_scatter(da1_part, 'x', scatter_dimension=0, tiled=True)]
  transfers between devices with their start and end apart: 14 -> 15, of which waited for: 11 -> 9; matrix products, arithmetic and copies ran while one was open for 6% -> 7% of each run, Pallas kernels for 22% -> 20%
where the time goes in v3:
time: 260 us; the launch traced here: 259 us
  blocking collectives  71.4 us (27%)
  Pallas kernels  67.1 us (26%)
  waiting for transfers between devices  52.4 us (20%)
  starting transfers between devices  23.9 us (9%)
  between operations  14.3 us (6%)
  local copies, waits for them, and re-layouts  13.7 us (5%)
  other arithmetic  9.47 us (4%)
  matrix products  6.52 us (3%)
    all_to_all x3, blocking collectives, exchange(): return lax.all_to_all(v, axes, 0, 0, tiled=True)  55.7 us
    all_to_all x6, starting transfers between devices, exchange(): return lax.all_to_all(v, axes, 0, 0, tiled=True)  23.5 us
    all_to_all x6, waiting for transfers between devices, exchange(): return lax.all_to_all(v, axes, 0, 0, tiled=True)  22.8 us
    reduce_scatter x1, waiting for transfers between devices, per_device(): lax.psum_scatter(r_feed, ('c', 'z'), scatter_dimension=0, tiled=True)  21.8 us
    pallas_call x1, Pallas kernels, attend_back(): pl.pallas_call(attend_back_kernel, grid_spec=grid_spec, out_shape=[shape(...  16.6 us
    all_gather x1, blocking collectives, per_device(): o = lax.all_gather(o, 'x', axis=0)  15.7 us
    pallas_call x1, Pallas kernels, attend(): pl.pallas_call(attend_kernel, grid_spec=grid_spec, out_shape=[shape((TOK,...  13.4 us
    pallas_call x1, Pallas kernels, feed(): pl.pallas_call(feed_kernel, in_specs=[pl.BlockSpec(memory_space=pltpu.SME...  9.98 us
  transfers between devices with their start and end apart: 15, of which 9 were waited for; matrix products, arithmetic and copies ran while one was open for 7% of the time, Pallas kernels for 20%

profile of v3, /device:TPU:0, one launch (start us, length us, event | category | flops | bytes accessed | tf_op | source)
XLA Modules:
  0.0 258.9 jit_solution(12658542414000507187)
XLA Ops:
  7.3 2.8 %convolution_convert_fusion.dy_ref = bf16[256,768]{1,0:T(8,128)(2,1)} fusion(bf16[768,768]{1,0:T(8,128)(2,1)} %constant.42.clone.perm_ref, bf16[128,768]{1,0:T(8,128)(2,1)} %bitcast.64, bf16[128,768]{1,0:T(8,128)(2,1)} %bitcast.65), kind=kOutput, calls=%fused_computation.4 | convolution fusion | flops 302972928 | bytes 1966080 | tf_op jit(solution)/shard_map/dot_general | solution.py:64
  12.5 4.4 %all-to-all-start = ((bf16[4,6,2176]{2,1,0:T(8,128)(2,1)}), bf16[4,6,2176]{2,1,0:T(8,128)(2,1)S(1)}, u32[]{:S(2)}, u32[]{:S(2)}) async-start(bf16[4,6,2176]{2,1,0:T(8,128)(2,1)} %copy.90), calls=%async_computation | async-start | bytes 278528 | tf_op jit(solution)/shard_map/all_to_all | solution.py:641
  17.6 5.3 %all-to-all-done = bf16[4,6,2176]{2,1,0:T(8,128)(2,1)S(1)} async-done(((bf16[4,6,2176]{2,1,0:T(8,128)(2,1)}), bf16[4,6,2176]{2,1,0:T(8,128)(2,1)S(1)}, u32[]{:S(2)}, u32[]{:S(2)}) %all-to-all-start) | async-done | bytes 104480 | tf_op jit(solution)/shard_map/all_to_all | solution.py:641
  23.1 17.8 %all_to_all.49 = bf16[16,24,640]{2,1,0:T(8,128)(2,1)S(1)} all-to-all(bf16[16,24,640]{2,1,0:T(8,128)(2,1)S(1)} %broadcast_in_dim.44), channel_id=1, replica_groups=mesh['y'=4,'z'=4,'x'=4,'c'=2] {'y','z'}, dimensions={0} | all-to-all | bytes 983040 | tf_op jit(solution)/shard_map/all_to_all | solution.py:641
  43.5 5.4 %project.1 = (bf16[512,768]{1,0:T(8,128)(2,1)}, bf16[4,512,384]{2,1,0:T(8,128)(2,1)}, bf16[512,384]{1,0:T(8,128)(2,1)}, f32[16,768]{1,0:T(8,128)}, bf16[768,640]{1,0:T(8,128)(2,1)}) custom-call(s32[1]{0:T(128)} %bitcast.c_ref, bf16[4,256,768]{2,1,0:T(8,128)(2,1)} %bitcast.60, bf16[384,640]{1,0:T(8,128)(2,1)} %bitcast.51, bf16[384,640]{1,0:T(8,128)(2,1)} %copy-done.24, ...), custom_call_target="tpu_custom_call" | custom-call | flops 2000000000 | bytes 8000000 | tf_op jit(solution)/shard_map/project/pallas_call | solution.py:315
  48.9 26.4 %all_to_all.50 = bf16[4,512,384]{2,1,0:T(8,128)(2,1)S(1)} all-to-all(bf16[4,512,384]{2,1,0:T(8,128)(2,1)} %get-tuple-element.66), channel_id=1, replica_groups=mesh['y'=4,'z'=4,'x'=4,'c'=2] {'z'}, dimensions={0} | all-to-all | bytes 3145728 | tf_op jit(solution)/shard_map/all_to_all | solution.py:641
  77.0 1.7 collective-permute-done.1.other_ref
  79.8 13.4 %attend.1 = (bf16[128,768]{1,0:T(8,128)(2,1)}, f32[192,512]{1,0:T(8,128)}, f32[3,8,512]{2,1,0:T(8,128)}, bf16[4096,384]{1,0:T(8,128)(2,1)}, bf16[384,4096]{1,0:T(8,128)(2,1)}, /*index=5*/bf16[512,384]{1,0:T(8,128)(2,1)}) custom-call(s32[64]{0:T(128)} %reshape.155.kpos, s32[8]{0:T(128)} %copy-done.26, s32[8,512]{1,0:T(8,128)} %broadcast_in_dim.39.qpos_ref, ...), custom_call_target="tpu_custom_call" | custom-call | flops 5000000000 | bytes 8000000 | tf_op jit(solution)/shard_map/attend/pallas_call | solution.py:238
  93.3 15.7 %all-gather.1 = bf16[512,768]{1,0:T(8,128)(2,1)} all-gather(bf16[128,768]{1,0:T(8,128)(2,1)} %get-tuple-element.70), channel_id=3, replica_groups=mesh['y'=4,'z'=4,'x'=4,'c'=2] {'x'}, dimensions={0}, use_global_device_ids=true | all-gather | bytes 983040 | tf_op jit(solution)/shard_map/all_gather | solution.py:716
  108.9 10.0 %feed.1 = (bf16[4,128,768]{2,1,0:T(8,128)(2,1)}, bf16[512,768]{1,0:T(8,128)(2,1)}, bf16[512,768]{1,0:T(8,128)(2,1)}, bf16[512,768]{1,0:T(8,128)(2,1)}, f32[128,768]{1,0:T(8,128)}, /*index=5*/bf16[512,768]{1,0:T(8,128)(2,1)}) custom-call(s32[1]{0:T(128)} %bitcast.10.x_ref, bf16[4,128,768]{2,1,0:T(8,128)(2,1)} %bitcast.49, bf16[4,256,768]{2,1,0:T(8,128)(2,1)} %bitcast.61, ...), custom_call_target="tpu_custom_call" | custom-call | flops 4000000000 | bytes 8000000 | tf_op jit(solution)/shard_map/feed/pallas_call | solution.py:403
  118.9 3.5 %all-to-all-start.3 = ((bf16[4,128,768]{2,1,0:T(8,128)(2,1)}), bf16[4,128,768]{2,1,0:T(8,128)(2,1)S(1)}, u32[]{:S(2)}, u32[]{:S(2)}) async-start(bf16[4,128,768]{2,1,0:T(8,128)(2,1)} %get-tuple-element.73), calls=%async_computation.3 | async-start | bytes 1572864 | tf_op jit(solution)/shard_map/all_to_all | solution.py:641
  122.5 7.3 %feed_grads.1 = (bf16[768,1536]{1,0:T(8,128)(2,1)}, bf16[512,768]{1,0:T(8,128)(2,1)}, f32[8,768]{1,0:T(8,128)}) custom-call(bf16[4,256,768]{2,1,0:T(8,128)(2,1)} %bitcast.62, bf16[768,768]{1,0:T(8,128)(2,1)} %constant.42.clone.perm_ref, bf16[768,2304]{1,0:T(8,128)(2,1)} %all-gather.5.cloned.1.call-done.w_ref.w2_ref.wo_ref, ...), custom_call_target="tpu_custom_call" | custom-call | flops 3000000000 | bytes 8000000 | tf_op jit(solution)/shard_map/feed_grads/pallas_call | solution.py:458
  129.8 3.7 %all-to-all-done.3.da2_ref = bf16[4,128,768]{2,1,0:T(8,128)(2,1)S(1)} async-done(((bf16[4,128,768]{2,1,0:T(8,128)(2,1)}), bf16[4,128,768]{2,1,0:T(8,128)(2,1)S(1)}, u32[]{:S(2)}, u32[]{:S(2)}) %all-to-all-start.3) | async-done | bytes 786464 | tf_op jit(solution)/shard_map/all_to_all | solution.py:641
  134.5 4.6 %norm2.1 = (bf16[4,128,384]{2,1,0:T(8,128)(2,1)}, f32[128,768]{1,0:T(8,128)}, f32[8,768]{1,0:T(8,128)}) custom-call(bf16[4,128,768]{2,1,0:T(8,128)(2,1)} %copy-done.3, f32[128,768]{1,0:T(8,128)} %get-tuple-element.79.resid_ref, bf16[256,768]{1,0:T(8,128)(2,1)} %convolution_convert_fusion.dy_ref, f32[16,768]{1,0:T(8,128)} %get-tuple-element.72.vec_ref, ...), custom_call_target="tpu_custom_call" | custom-call | flops 100000000 | bytes 8000000 | tf_op jit(solution)/shard_map/norm2/pallas_call | solution.py:509
  139.0 11.6 %all_to_all.51 = bf16[4,128,384]{2,1,0:T(8,128)(2,1)} all-to-all(bf16[4,128,384]{2,1,0:T(8,128)(2,1)} %get-tuple-element.80), channel_id=1, replica_groups=mesh['y'=4,'z'=4,'x'=4,'c'=2] {'x'}, dimensions={0} | all-to-all | bytes 786432 | tf_op jit(solution)/shard_map/all_to_all | solution.py:641
  150.6 3.5 %all-to-all-start.5 = ((bf16[4,128,768]{2,1,0:T(8,128)(2,1)}), bf16[4,128,768]{2,1,0:T(8,128)(2,1)S(1)}, u32[]{:S(2)}, u32[]{:S(2)}) async-start(bf16[4,128,768]{2,1,0:T(8,128)(2,1)} %bitcast.13), calls=%async_computation.5 | async-start | bytes 1572864 | tf_op jit(solution)/shard_map/all_to_all | solution.py:641
  154.4 16.6 %attend_back.1 = (bf16[2048,384]{1,0:T(8,128)(2,1)}, bf16[2048,384]{1,0:T(8,128)(2,1)}, bf16[512,384]{1,0:T(8,128)(2,1)}) custom-call(s32[64]{0:T(128)} %reshape.155.kpos, s32[8]{0:T(128)} %copy-done.26, s32[8,512]{1,0:T(8,128)} %broadcast_in_dim.39.qpos_ref, bf16[512,384]{1,0:T(8,128)(2,1)} %get-tuple-element.67.qs_ref, ...), custom_call_target="tpu_custom_call" | custom-call | flops 15000000512 | bytes 8000000 | tf_op jit(solution)/shard_map/attend_back/pallas_call | solution.py:275
  171.1 3.6 %collective-permute-done.2 = bf16[2048,384]{1,0:T(8,128)(2,1)S(1)} collective-permute-done((bf16[2048,384]{1,0:T(8,128)(2,1)}, bf16[2048,384]{1,0:T(8,128)(2,1)S(1)}, u32[]{:S(2)}, u32[]{:S(2)}) %collective-permute-start.2) | collective-permute-done | bytes 1572896 | tf_op jit(solution)/shard_map/ppermute | solution.py:732
  174.7 3.0 %add_convert_fusion = bf16[2048,384]{1,0:T(8,128)(2,1)} fusion(bf16[2048,384]{1,0:T(8,128)(2,1)S(1)} %collective-permute-done.2, bf16[2048,384]{1,0:T(8,128)(2,1)} %get-tuple-element.85), kind=kLoop, calls=%fused_computation | loop fusion | flops 3145728 | bytes 4718592 | tf_op jit(solution)/shard_map/convert_element_type | solution.py:736
  177.7 3.7 %all-to-all-start.6 = ((bf16[4,512,384]{2,1,0:T(8,128)(2,1)}), bf16[4,512,384]{2,1,0:T(8,128)(2,1)S(1)}, u32[]{:S(2)}, u32[]{:S(2)}) async-start(bf16[4,512,384]{2,1,0:T(8,128)(2,1)} %bitcast.14), calls=%async_computation.7 | async-start | bytes 3145728 | tf_op jit(solution)/shard_map/all_to_all | solution.py:641
  181.6 3.9 %early.1 = (bf16[512,256]{1,0:T(8,128)(2,1)}, bf16[768,512]{1,0:T(8,128)(2,1)}) custom-call(bf16[512,384]{1,0:T(8,128)(2,1)} %get-tuple-element.92.dq_ref, bf16[640,768]{1,0:T(8,128)(2,1)} %constant.43.clone.heads_ref, bf16[512,768]{1,0:T(8,128)(2,1)} %get-tuple-element.93.a1_ref, bf16[512,768]{1,0:T(8,128)(2,1)} %get-tuple-element.94.op_ref, ...), custom_call_target="tpu_custom_call" | custom-call | flops 1000000000 | bytes 8000000 | tf_op jit(solution)/shard_map/early/pallas_call | solution.py:539
  185.4 21.8 %reduce-scatter.6.cloned.1.call-done = bf16[24,1536]{1,0:T(8,128)(2,1)} async-done(((bf16[192,1536]{1,0:T(8,128)(2,1)}), bf16[24,1536]{1,0:T(8,128)(2,1)}) %reduce-scatter.6.cloned.1.call-update) | async-done | bytes 73744 | tf_op jit(solution)/shard_map/reduce_scatter | solution.py:731
  208.4 6.0 %grads.1 = (bf16[512,768]{1,0:T(8,128)(2,1)}, bf16[384,896]{1,0:T(8,128)(2,1)}, bf16[384,896]{1,0:T(8,128)(2,1)}) custom-call(s32[1]{0:T(128)} %bitcast.c_ref, bf16[4,512,384]{2,1,0:T(8,128)(2,1)} %copy-done.5, bf16[512,256]{1,0:T(8,128)(2,1)} %get-tuple-element.95.dqn_ref, bf16[768,512]{1,0:T(8,128)(2,1)} %get-tuple-element.96.early_ref, ...), custom_call_target="tpu_custom_call" | custom-call | flops 2000000000 | bytes 8000000 | tf_op jit(solution)/shard_map/grads/pallas_call | solution.py:612
  215.5 1.3 collective-permute-done.3
  216.7 2.1 add_convert_fusion.1
  218.9 3.7 %all-to-all-start.7 = ((bf16[16,24,896]{2,1,0:T(8,128)(2,1)}), bf16[16,24,896]{2,1,0:T(8,128)(2,1)S(1)}, u32[]{:S(2)}, u32[]{:S(2)}) async-start(bf16[16,24,896]{2,1,0:T(8,128)(2,1)} %bitcast.44), calls=%async_computation.9 | async-start | bytes 1376256 | tf_op jit(solution)/shard_map/all_to_all | solution.py:641
  222.8 1.2 convolution_convert_fusion.1
  224.7 11.9 %all-to-all-done.7 = bf16[16,24,896]{2,1,0:T(8,128)(2,1)S(1)} async-done(((bf16[16,24,896]{2,1,0:T(8,128)(2,1)}), bf16[16,24,896]{2,1,0:T(8,128)(2,1)S(1)}, u32[]{:S(2)}, u32[]{:S(2)}) %all-to-all-start.7) | async-done | bytes 688160 | tf_op jit(solution)/shard_map/all_to_all | solution.py:641
  237.4 4.7 %all-to-all-start.8 = ((bf16[4,6,1600]{2,1,0:T(8,128)(2,1)}), bf16[4,6,1600]{2,1,0:T(8,128)(2,1)S(1)}, u32[]{:S(2)}, u32[]{:S(2)}) async-start(bf16[4,6,1600]{2,1,0:T(8,128)(2,1)} %pad_maximum_fusion.1), calls=%async_computation.10 | async-start | bytes 212992 | tf_op jit(solution)/shard_map/all_to_all | solution.py:641
  244.0 2.2 convolution_convert_fusion.2
  246.1 1.8 all-to-all-done.8
  248.7 1.2 reshape.172
  (143 shorter events, 18.9 us)
Async XLA Ops:
  7.2 3.0 %copy-start = (bf16[768,768]{1,0:T(8,128)(2,1)S(1)}, bf16[768,768]{1,0:T(8,128)(2,1)}, u32[]{:S(2)}) copy-start(bf16[768,768]{1,0:T(8,128)(2,1)} %constant.42.clone.perm_ref) | copy-start | bytes 3538948
  7.2 3.0 %copy-start.12 = (bf16[6,768]{1,0:T(8,128)(2,1)S(1)}, bf16[6,768]{1,0:T(8,128)(2,1)}, u32[]{:S(2)}) copy-start(bf16[6,768]{1,0:T(8,128)(2,1)} %param.27) | copy-start | bytes 27652
  7.2 3.0 %copy-start.10 = (bf16[24,768]{1,0:T(8,128)(2,1)S(1)}, bf16[24,768]{1,0:T(8,128)(2,1)}, u32[]{:S(2)}) copy-start(bf16[24,768]{1,0:T(8,128)(2,1)} %param.33) | copy-start | bytes 110596
  7.2 35.6 %all-gather.7.cloned.1.call-start = ((), (), s32[]{:S(2)}) async-start(), calls=%async_computation.16 | async-start | bytes 1966080 | tf_op jit(solution)/shard_map/all_gather | solution.py:698
  7.3 3.2 %copy-start.9 = (bf16[6,3072]{1,0:T(8,128)(2,1)S(1)}, bf16[6,3072]{1,0:T(8,128)(2,1)}, u32[]{:S(2)}) copy-start(bf16[6,3072]{1,0:T(8,128)(2,1)} %param.31) | copy-start | bytes 110596
  10.1 1.3 copy-start.17
  10.1 1.3 copy-start.18
  10.1 1.3 copy-start.19
  10.5 12.5 %copy-start.14 = (bf16[24]{0:T(256)(128)(2,1)S(1)}, bf16[24]{0:T(256)(128)(2,1)}, u32[]{:S(2)}) copy-start(bf16[24]{0:T(256)(128)(2,1)} %param.32) | copy-start | bytes 148
  12.5 10.4 %all-to-all-start = ((bf16[4,6,2176]{2,1,0:T(8,128)(2,1)}), bf16[4,6,2176]{2,1,0:T(8,128)(2,1)S(1)}, u32[]{:S(2)}, u32[]{:S(2)}) async-start(bf16[4,6,2176]{2,1,0:T(8,128)(2,1)} %copy.90), calls=%async_computation | async-start | bytes 278528 | tf_op jit(solution)/shard_map/all_to_all | solution.py:641
  16.9 92.0 %all-gather.5.cloned.1.call-start = ((), (), s32[]{:S(2)}) async-start(), calls=%async_computation.12 | async-start | bytes 3649536 | tf_op jit(solution)/shard_map/all_gather | solution.py:709
  40.9 1.9 copy-start.7
  40.9 1.9 collective-permute-start
  48.9 26.4 %copy-start.13 = (s32[32,2]{0,1:T(2,128)S(1)}, s32[32,2]{0,1:T(2,128)}, u32[]{:S(2)}) copy-start(s32[32,2]{0,1:T(2,128)} %param.21) | copy-start | bytes 772
  75.3 4.0 %copy-start.4 = (bf16[4,512,384]{2,1,0:T(8,128)(2,1)}, bf16[4,512,384]{2,1,0:T(8,128)(2,1)S(1)}, u32[]{:S(2)}) copy-start(bf16[4,512,384]{2,1,0:T(8,128)(2,1)S(1)} %all_to_all.50) | copy-start | bytes 4718596
  75.3 3.4 %collective-permute-start.1 = (bf16[2048,384]{1,0:T(8,128)(2,1)S(1)}, bf16[2048,384]{1,0:T(8,128)(2,1)S(1)}, u32[]{:S(2)}, u32[]{:S(2)}) collective-permute-start(bf16[2048,384]{1,0:T(8,128)(2,1)S(1)} %bitcast.45), channel_id=1, source_target_pairs={{0,1},{1,0},{2,3},{3,2},{4,5},{5,4},{6,7},{7,6},{8,9},{9,8},{10,11... | collective-permute-start | bytes 4718600 | tf_op jit(solution)/shard_map/ppermute | solution.py:714
  76.1 3.2 %copy-start.26 = (s32[8]{0:T(128)}, s32[8]{0:T(128)S(1)}, u32[]{:S(2)}) copy-start(s32[8]{0:T(128)S(1)} %convert_reduce_fusion.3.rank) | copy-start | bytes 100
  118.9 14.7 %all-to-all-start.3 = ((bf16[4,128,768]{2,1,0:T(8,128)(2,1)}), bf16[4,128,768]{2,1,0:T(8,128)(2,1)S(1)}, u32[]{:S(2)}, u32[]{:S(2)}) async-start(bf16[4,128,768]{2,1,0:T(8,128)(2,1)} %get-tuple-element.73), calls=%async_computation.3 | async-start | bytes 1572864 | tf_op jit(solution)/shard_map/all_to_all | solution.py:641
  122.4 48.6 %reduce-scatter.4.cloned.1.call-start = ((), (), s32[]{:S(2)}) async-start(), calls=%async_computation.13 | async-start | bytes 2949120 | tf_op jit(solution)/shard_map/reduce_scatter | solution.py:723
  150.6 20.4 %all-to-all-start.5 = ((bf16[4,128,768]{2,1,0:T(8,128)(2,1)}), bf16[4,128,768]{2,1,0:T(8,128)(2,1)S(1)}, u32[]{:S(2)}, u32[]{:S(2)}) async-start(bf16[4,128,768]{2,1,0:T(8,128)(2,1)} %bitcast.13), calls=%async_computation.5 | async-start | bytes 1572864 | tf_op jit(solution)/shard_map/all_to_all | solution.py:641
  154.1 53.1 %reduce-scatter.6.cloned.1.call-start = ((), (), s32[]{:S(2)}) async-start(), calls=%async_computation.14 | async-start | bytes 663552 | tf_op jit(solution)/shard_map/reduce_scatter | solution.py:731
  171.0 3.7 %collective-permute-start.2 = (bf16[2048,384]{1,0:T(8,128)(2,1)}, bf16[2048,384]{1,0:T(8,128)(2,1)S(1)}, u32[]{:S(2)}, u32[]{:S(2)}) collective-permute-start(bf16[2048,384]{1,0:T(8,128)(2,1)} %get-tuple-element.89), channel_id=1, source_target_pairs={{0,1},{1,0},{2,3},{3,2},{4,5},{5,4},{6,7},{7,6},{8,9},{9,8},{10,11... | collective-permute-start | bytes 4718600 | tf_op jit(solution)/shard_map/ppermute | solution.py:732
  177.7 3.8 %copy-start.2 = (bf16[256,768]{1,0:T(8,128)(2,1)S(1)}, bf16[256,768]{1,0:T(8,128)(2,1)}, u32[]{:S(2)}) copy-start(bf16[256,768]{1,0:T(8,128)(2,1)} %convolution_convert_fusion.dy_ref) | copy-start | bytes 1179652
  177.7 29.6 %all-to-all-start.6 = ((bf16[4,512,384]{2,1,0:T(8,128)(2,1)}), bf16[4,512,384]{2,1,0:T(8,128)(2,1)S(1)}, u32[]{:S(2)}, u32[]{:S(2)}) async-start(bf16[4,512,384]{2,1,0:T(8,128)(2,1)} %bitcast.14), calls=%async_computation.7 | async-start | bytes 3145728 | tf_op jit(solution)/shard_map/all_to_all | solution.py:641
  181.4 61.4 %reduce-scatter.8.cloned.1.call-start = ((), (), s32[]{:S(2)}) async-start(), calls=%async_computation.15 | async-start | bytes 983040 | tf_op jit(solution)/shard_map/reduce_scatter | solution.py:743
  214.4 2.4 collective-permute-start.3
  218.9 3.9 %copy-start.1 = (bf16[768,768]{1,0:T(8,128)(2,1)S(1)}, bf16[768,768]{1,0:T(8,128)(2,1)}, u32[]{:S(2)}) copy-start(bf16[768,768]{1,0:T(8,128)(2,1)} %constant.42.clone.perm_ref) | copy-start | bytes 3538948
  218.9 3.9 %copy-start.6 = (f32[128,768]{1,0:T(8,128)S(1)}, f32[128,768]{1,0:T(8,128)}, u32[]{:S(2)}) copy-start(f32[128,768]{1,0:T(8,128)} %get-tuple-element.79.resid_ref) | copy-start | bytes 1179652
  218.9 17.7 %all-to-all-start.7 = ((bf16[16,24,896]{2,1,0:T(8,128)(2,1)}), bf16[16,24,896]{2,1,0:T(8,128)(2,1)S(1)}, u32[]{:S(2)}, u32[]{:S(2)}) async-start(bf16[16,24,896]{2,1,0:T(8,128)(2,1)} %bitcast.44), calls=%async_computation.9 | async-start | bytes 1376256 | tf_op jit(solution)/shard_map/all_to_all | solution.py:641
  222.6 1.4 copy-start.8
  224.0 19.9 %copy-start.25 = (f32[128,768]{1,0:T(8,128)S(1)}, f32[128,768]{1,0:T(8,128)}, u32[]{:S(2)}) copy-start(f32[128,768]{1,0:T(8,128)} %get-tuple-element.103) | copy-start | bytes 1179652
  237.4 10.5 %all-to-all-start.8 = ((bf16[4,6,1600]{2,1,0:T(8,128)(2,1)}), bf16[4,6,1600]{2,1,0:T(8,128)(2,1)S(1)}, u32[]{:S(2)}, u32[]{:S(2)}) async-start(bf16[4,6,1600]{2,1,0:T(8,128)(2,1)} %pad_maximum_fusion.1), calls=%async_computation.10 | async-start | bytes 212992 | tf_op jit(solution)/shard_map/all_to_all | solution.py:641
  (10 other events, 11.4 us)
Sparse Core Ops, SparseCore 0:
  10.3 28.9 all-gather.6
  42.9 47.6 all-gather.4
  133.7 26.2 reduce-scatter.3
  171.2 35.9 reduce-scatter.5
  214.7 20.4 reduce-scatter.7

commit v4 on v3

--- a/solution.py
+++ b/solution.py
@@ -18,7 +18,7 @@
 TOK = 128
 ROWS = TOK * TP
 KEYS = 4096
-CHUNK = 1024
+CHUNK = 2048
 BACK = 2048
 EPS = 1e-05
 MASKED = -1e30
@@ -435,18 +435,19 @@
     mixed_ref,
     gb_ref,
     dy_s,
+    g_s,
 ):
     for i in range(TP):
         at = slice(i * TOK, (i + 1) * TOK)
         dy_s[at, :] = dot_nt(rows_ref[i, TOK:, :], perm_ref[...]).astype(BF)
-    for core in range(2):
-        at = slice(core * 384, (core + 1) * 384)
-        g_fc1 = dot_tn(a2_ref[:, at], du_ref[...]).astype(BF)
-        g_fc2 = dot_tn(act_ref[:, at], dy_s[...]).astype(BF)
-        for y in range(4):
-            to = slice(y * 192 + core * 96, y * 192 + (core + 1) * 96)
-            gw_ref[to, 0:D] = g_fc1[y * 96 : (y + 1) * 96]
-            gw_ref[to, D:] = g_fc2[y * 96 : (y + 1) * 96]
+    for lhs, rhs, col in ((a2_ref, du_ref, 0), (act_ref, dy_s, D)):
+        for core in range(2):
+            part = dot_tn(lhs[:, core * 384 : (core + 1) * 384], rhs[...])
+            for y in range(4):
+                for z in range(4):
+                    to = ((core * 4 + z) * 4 + y) * 24
+                    g_s[to : to + 24, :] = part[(y * 4 + z) * 24 : (y * 4 + z + 1) * 24]
+        gw_ref[:, col : col + D] = g_s[...].astype(BF)
     for i in range(2):
         at = slice(i * 256, (i + 1) * 256)
         mixed_ref[at, :] = dot(act_ref[at, :], w2_ref[...]).astype(BF)
@@ -472,7 +473,7 @@
             pl.BlockSpec((8, D), lambda i: (0, 0)),
         ],
         out_shape=[shape((D, 2 * D)), shape((ROWS, D)), shape((8, D), F32)],
-        scratch_shapes=[pltpu.VMEM((ROWS, D), BF)],
+        scratch_shapes=[pltpu.VMEM((ROWS, D), BF), pltpu.VMEM((D, D), F32)],
         name="feed_grads",
         **settings(3_000_000_000),
     )(rows, perm, w, act, a2, du)
@@ -720,7 +721,7 @@
     da2 = exchange(da2_part, "x")
     da2, g_feed = lax.optimization_barrier((da2, g_feed))
     dbr, dresid, sums = norm2(da2, resid, own_rows, vec, second, perm)
-    r_feed = lax.psum_scatter(g_feed, "y", scatter_dimension=0, tiled=True)
+    r_feed = lax.psum_scatter(g_feed, ("c", "z"), scatter_dimension=0, tiled=True)
     dbr = exchange(dbr, "x").reshape(ROWS, 2 * HW)
     dbr, mixed_part = lax.optimization_barrier((dbr, mixed_part))
     mixed_part = exchange(mixed_part.reshape(TP, TOK, D), "x")
@@ -728,7 +729,7 @@
         kpos, rank, qpos, qs, kvs, kvt, dbr, jnp.asarray(place_matrix()), o_t, lse
     )
     dkv_other, mixed_part, r_feed = lax.optimization_barrier((dkv_other, mixed_part, r_feed))
-    r_feed = lax.psum_scatter(r_feed, ("c", "z"), scatter_dimension=0, tiled=True)
+    r_feed = lax.psum_scatter(r_feed, "y", scatter_dimension=0, tiled=True)
     dkv_other = lax.ppermute(dkv_other, "c", SWAP)
     mixed = jnp.sum(mixed_part.astype(F32), 0)
     mixed = (resid + mixed + vec[BFC2 : BFC2 + 1]).astype(BF)
@@ -750,14 +751,14 @@
     pack_other = lax.ppermute(pack_other, "c", SWAP)
     half = (pack.astype(F32) + pack_other.astype(F32)).astype(BF)
     mine = jnp.sum(exchange(half, ("y", "z")).reshape(16, 24, -1).astype(F32), 0)
-    last = jnp.concatenate([mine[:, : COLS + HW], r_feed[:, :D]], 1).astype(BF)
+    r_fc1 = r_feed[:, :D].reshape(24, 2, 16, 24).transpose(0, 2, 1, 3).reshape(24, D)
+    last = jnp.concatenate([mine[:, : COLS + HW], r_fc1], 1).astype(BF)
     last = exchange(last.reshape(TP, 6, -1), "x")
     last, dtok, mixed = lax.optimization_barrier((last, dtok, mixed))
     last = last.astype(F32)
     r_qkv = last[:, :, : 3 * HW].reshape(TP, 6, 3, HW).transpose(1, 2, 0, 3).reshape(6, 3 * D)
     r_out = last[:, :, COLS : COLS + HW].transpose(1, 0, 2).reshape(6, D)
-    r_fc1 = last[:, :, COLS + HW :].reshape(TP, 6, 2, 16, 24)
-    r_fc1 = r_fc1.transpose(1, 3, 0, 2, 4).reshape(6, FF)
+    r_fc1 = last[:, :, COLS + HW :].reshape(TP, 6, 16, 48).transpose(1, 2, 0, 3).reshape(6, FF)
     r_vec = jnp.sum(last[:, :, 3 * HW : 3 * HW + 8], 0)
     return (
         mixed[None],

time: 260 us -> 257 us (0.988)
  waiting for transfers between devices: 52.4 us -> 48.6 us
    reduce_scatter x2, waiting for transfers between devices: 21.8 us -> 18.6 us  [the longest x1 18.6 us: per_device(): r_feed = lax.psum_scatter(r_feed, 'y', scatter_dimension=0, tiled=True)]
where the time goes in v4:
time: 257 us; the launch traced here: 256 us
  blocking collectives  71.4 us (28%)
  Pallas kernels  67 us (26%)
  waiting for transfers between devices  48.6 us (19%)
  starting transfers between devices  25.2 us (10%)
  between operations  14.4 us (6%)
  local copies, waits for them, and re-layouts  13.7 us (5%)
  other arithmetic  9.45 us (4%)
  matrix products  6.5 us (3%)
    all_to_all x3, blocking collectives, exchange(): return lax.all_to_all(v, axes, 0, 0, tiled=True)  55.7 us
    all_to_all x6, starting transfers between devices, exchange(): return lax.all_to_all(v, axes, 0, 0, tiled=True)  25 us
    all_to_all x6, waiting for transfers between devices, exchange(): return lax.all_to_all(v, axes, 0, 0, tiled=True)  21.7 us
    reduce_scatter x1, waiting for transfers between devices, per_device(): r_feed = lax.psum_scatter(r_feed, 'y', scatter_dimension=0, tiled=True)  18.6 us
    pallas_call x1, Pallas kernels, attend_back(): pl.pallas_call(attend_back_kernel, grid_spec=grid_spec, out_shape=[shape(...  16.6 us
    all_gather x1, blocking collectives, per_device(): o = lax.all_gather(o, 'x', axis=0)  15.7 us
    pallas_call x1, Pallas kernels, attend(): pl.pallas_call(attend_kernel, grid_spec=grid_spec, out_shape=[shape((TOK,...  13.3 us
    pallas_call x1, Pallas kernels, feed(): pl.pallas_call(feed_kernel, in_specs=[pl.BlockSpec(memory_space=pltpu.SME...  9.97 us
  transfers between devices with their start and end apart: 15, of which 9 were waited for; matrix products, arithmetic and copies ran while one was open for 7% of the time, Pallas kernels for 20%

profile of v4, /device:TPU:0, one launch (start us, length us, event | category | flops | bytes accessed | tf_op | source)
XLA Modules:
  0.0 256.3 jit_solution(7563901223299647382)
XLA Ops:
  7.3 2.8 %convolution_convert_fusion.dy_ref = bf16[256,768]{1,0:T(8,128)(2,1)} fusion(bf16[768,768]{1,0:T(8,128)(2,1)} %constant.42.clone.perm_ref, bf16[128,768]{1,0:T(8,128)(2,1)} %bitcast.68, bf16[128,768]{1,0:T(8,128)(2,1)} %bitcast.69), kind=kOutput, calls=%fused_computation.4 | convolution fusion | flops 302972928 | bytes 1966080 | tf_op jit(solution)/shard_map/dot_general | solution.py:64
  12.5 4.4 %all-to-all-start = ((bf16[4,6,2176]{2,1,0:T(8,128)(2,1)}), bf16[4,6,2176]{2,1,0:T(8,128)(2,1)S(1)}, u32[]{:S(2)}, u32[]{:S(2)}) async-start(bf16[4,6,2176]{2,1,0:T(8,128)(2,1)} %copy.93), calls=%async_computation | async-start | bytes 278528 | tf_op jit(solution)/shard_map/all_to_all | solution.py:642
  17.6 5.3 %all-to-all-done = bf16[4,6,2176]{2,1,0:T(8,128)(2,1)S(1)} async-done(((bf16[4,6,2176]{2,1,0:T(8,128)(2,1)}), bf16[4,6,2176]{2,1,0:T(8,128)(2,1)S(1)}, u32[]{:S(2)}, u32[]{:S(2)}) %all-to-all-start) | async-done | bytes 104480 | tf_op jit(solution)/shard_map/all_to_all | solution.py:642
  23.1 17.8 %all_to_all.49 = bf16[16,24,640]{2,1,0:T(8,128)(2,1)S(1)} all-to-all(bf16[16,24,640]{2,1,0:T(8,128)(2,1)S(1)} %broadcast_in_dim.44), channel_id=1, replica_groups=mesh['y'=4,'z'=4,'x'=4,'c'=2] {'y','z'}, dimensions={0} | all-to-all | bytes 983040 | tf_op jit(solution)/shard_map/all_to_all | solution.py:642
  43.5 5.4 %project.1 = (bf16[512,768]{1,0:T(8,128)(2,1)}, bf16[4,512,384]{2,1,0:T(8,128)(2,1)}, bf16[512,384]{1,0:T(8,128)(2,1)}, f32[16,768]{1,0:T(8,128)}, bf16[768,640]{1,0:T(8,128)(2,1)}) custom-call(s32[1]{0:T(128)} %bitcast.c_ref, bf16[4,256,768]{2,1,0:T(8,128)(2,1)} %bitcast.64, bf16[384,640]{1,0:T(8,128)(2,1)} %bitcast.55, bf16[384,640]{1,0:T(8,128)(2,1)} %copy-done.24, ...), custom_call_target="tpu_custom_call" | custom-call | flops 2000000000 | bytes 8000000 | tf_op jit(solution)/shard_map/project/pallas_call | solution.py:315
  48.9 26.4 %all_to_all.50 = bf16[4,512,384]{2,1,0:T(8,128)(2,1)S(1)} all-to-all(bf16[4,512,384]{2,1,0:T(8,128)(2,1)} %get-tuple-element.66), channel_id=1, replica_groups=mesh['y'=4,'z'=4,'x'=4,'c'=2] {'z'}, dimensions={0} | all-to-all | bytes 3145728 | tf_op jit(solution)/shard_map/all_to_all | solution.py:642
  77.0 1.7 collective-permute-done.1.other_ref
  79.8 13.3 %attend.1 = (bf16[128,768]{1,0:T(8,128)(2,1)}, f32[192,512]{1,0:T(8,128)}, f32[3,8,512]{2,1,0:T(8,128)}, bf16[4096,384]{1,0:T(8,128)(2,1)}, bf16[384,4096]{1,0:T(8,128)(2,1)}, /*index=5*/bf16[512,384]{1,0:T(8,128)(2,1)}) custom-call(s32[64]{0:T(128)} %reshape.161.kpos, s32[8]{0:T(128)} %copy-done.26, s32[8,512]{1,0:T(8,128)} %broadcast_in_dim.39.qpos_ref, ...), custom_call_target="tpu_custom_call" | custom-call | flops 5000000000 | bytes 8000000 | tf_op jit(solution)/shard_map/attend/pallas_call | solution.py:238
  93.2 15.7 %all-gather.1 = bf16[512,768]{1,0:T(8,128)(2,1)} all-gather(bf16[128,768]{1,0:T(8,128)(2,1)} %get-tuple-element.70), channel_id=3, replica_groups=mesh['y'=4,'z'=4,'x'=4,'c'=2] {'x'}, dimensions={0}, use_global_device_ids=true | all-gather | bytes 983040 | tf_op jit(solution)/shard_map/all_gather | solution.py:717
  108.8 10.0 %feed.1 = (bf16[4,128,768]{2,1,0:T(8,128)(2,1)}, bf16[512,768]{1,0:T(8,128)(2,1)}, bf16[512,768]{1,0:T(8,128)(2,1)}, bf16[512,768]{1,0:T(8,128)(2,1)}, f32[128,768]{1,0:T(8,128)}, /*index=5*/bf16[512,768]{1,0:T(8,128)(2,1)}) custom-call(s32[1]{0:T(128)} %bitcast.10.x_ref, bf16[4,128,768]{2,1,0:T(8,128)(2,1)} %bitcast.53, bf16[4,256,768]{2,1,0:T(8,128)(2,1)} %bitcast.65, ...), custom_call_target="tpu_custom_call" | custom-call | flops 4000000000 | bytes 8000000 | tf_op jit(solution)/shard_map/feed/pallas_call | solution.py:403
  118.8 3.5 %all-to-all-start.3 = ((bf16[4,128,768]{2,1,0:T(8,128)(2,1)}), bf16[4,128,768]{2,1,0:T(8,128)(2,1)S(1)}, u32[]{:S(2)}, u32[]{:S(2)}) async-start(bf16[4,128,768]{2,1,0:T(8,128)(2,1)} %get-tuple-element.73), calls=%async_computation.3 | async-start | bytes 1572864 | tf_op jit(solution)/shard_map/all_to_all | solution.py:642
  122.4 7.3 %feed_grads.1 = (bf16[768,1536]{1,0:T(8,128)(2,1)}, bf16[512,768]{1,0:T(8,128)(2,1)}, f32[8,768]{1,0:T(8,128)}) custom-call(bf16[4,256,768]{2,1,0:T(8,128)(2,1)} %bitcast.66, bf16[768,768]{1,0:T(8,128)(2,1)} %constant.42.clone.perm_ref, bf16[768,2304]{1,0:T(8,128)(2,1)} %all-gather.5.cloned.1.call-done.w_ref.w2_ref.wo_ref, ...), custom_call_target="tpu_custom_call" | custom-call | flops 3000000000 | bytes 8000000 | tf_op jit(solution)/shard_map/feed_grads/pallas_call | solution.py:459
  129.7 3.8 %all-to-all-done.3.da2_ref = bf16[4,128,768]{2,1,0:T(8,128)(2,1)S(1)} async-done(((bf16[4,128,768]{2,1,0:T(8,128)(2,1)}), bf16[4,128,768]{2,1,0:T(8,128)(2,1)S(1)}, u32[]{:S(2)}, u32[]{:S(2)}) %all-to-all-start.3) | async-done | bytes 786464 | tf_op jit(solution)/shard_map/all_to_all | solution.py:642
  134.4 4.6 %norm2.1 = (bf16[4,128,384]{2,1,0:T(8,128)(2,1)}, f32[128,768]{1,0:T(8,128)}, f32[8,768]{1,0:T(8,128)}) custom-call(bf16[4,128,768]{2,1,0:T(8,128)(2,1)} %copy-done.3, f32[128,768]{1,0:T(8,128)} %get-tuple-element.79.resid_ref, bf16[256,768]{1,0:T(8,128)(2,1)} %convolution_convert_fusion.dy_ref, f32[16,768]{1,0:T(8,128)} %get-tuple-element.72.vec_ref, ...), custom_call_target="tpu_custom_call" | custom-call | flops 100000000 | bytes 8000000 | tf_op jit(solution)/shard_map/norm2/pallas_call | solution.py:510
  138.9 11.6 %all_to_all.51 = bf16[4,128,384]{2,1,0:T(8,128)(2,1)} all-to-all(bf16[4,128,384]{2,1,0:T(8,128)(2,1)} %get-tuple-element.80), channel_id=1, replica_groups=mesh['y'=4,'z'=4,'x'=4,'c'=2] {'x'}, dimensions={0} | all-to-all | bytes 786432 | tf_op jit(solution)/shard_map/all_to_all | solution.py:642
  150.5 3.7 %all-to-all-start.5 = ((bf16[4,128,768]{2,1,0:T(8,128)(2,1)}), bf16[4,128,768]{2,1,0:T(8,128)(2,1)S(1)}, u32[]{:S(2)}, u32[]{:S(2)}) async-start(bf16[4,128,768]{2,1,0:T(8,128)(2,1)} %bitcast.13), calls=%async_computation.5 | async-start | bytes 1572864 | tf_op jit(solution)/shard_map/all_to_all | solution.py:642
  154.2 16.6 %attend_back.1 = (bf16[2048,384]{1,0:T(8,128)(2,1)}, bf16[2048,384]{1,0:T(8,128)(2,1)}, bf16[512,384]{1,0:T(8,128)(2,1)}) custom-call(s32[64]{0:T(128)} %reshape.161.kpos, s32[8]{0:T(128)} %copy-done.26, s32[8,512]{1,0:T(8,128)} %broadcast_in_dim.39.qpos_ref, bf16[512,384]{1,0:T(8,128)(2,1)} %get-tuple-element.67.qs_ref, ...), custom_call_target="tpu_custom_call" | custom-call | flops 15000000512 | bytes 8000000 | tf_op jit(solution)/shard_map/attend_back/pallas_call | solution.py:275
  170.9 3.6 %collective-permute-done.2 = bf16[2048,384]{1,0:T(8,128)(2,1)S(1)} collective-permute-done((bf16[2048,384]{1,0:T(8,128)(2,1)}, bf16[2048,384]{1,0:T(8,128)(2,1)S(1)}, u32[]{:S(2)}, u32[]{:S(2)}) %collective-permute-start.2) | collective-permute-done | bytes 1572896 | tf_op jit(solution)/shard_map/ppermute | solution.py:733
  174.6 3.0 %add_convert_fusion = bf16[2048,384]{1,0:T(8,128)(2,1)} fusion(bf16[2048,384]{1,0:T(8,128)(2,1)S(1)} %collective-permute-done.2, bf16[2048,384]{1,0:T(8,128)(2,1)} %get-tuple-element.85), kind=kLoop, calls=%fused_computation | loop fusion | flops 3145728 | bytes 4718592 | tf_op jit(solution)/shard_map/convert_element_type | solution.py:737
  177.5 3.7 %all-to-all-start.6 = ((bf16[4,512,384]{2,1,0:T(8,128)(2,1)}), bf16[4,512,384]{2,1,0:T(8,128)(2,1)S(1)}, u32[]{:S(2)}, u32[]{:S(2)}) async-start(bf16[4,512,384]{2,1,0:T(8,128)(2,1)} %bitcast.14), calls=%async_computation.7 | async-start | bytes 3145728 | tf_op jit(solution)/shard_map/all_to_all | solution.py:642
  182.0 3.9 %early.1 = (bf16[512,256]{1,0:T(8,128)(2,1)}, bf16[768,512]{1,0:T(8,128)(2,1)}) custom-call(bf16[512,384]{1,0:T(8,128)(2,1)} %get-tuple-element.92.dq_ref, bf16[640,768]{1,0:T(8,128)(2,1)} %constant.43.clone.heads_ref, bf16[512,768]{1,0:T(8,128)(2,1)} %get-tuple-element.93.a1_ref, bf16[512,768]{1,0:T(8,128)(2,1)} %get-tuple-element.94.op_ref, ...), custom_call_target="tpu_custom_call" | custom-call | flops 1000000000 | bytes 8000000 | tf_op jit(solution)/shard_map/early/pallas_call | solution.py:540
  185.8 18.6 %reduce-scatter.6.cloned.1.call-done = bf16[24,1536]{1,0:T(8,128)(2,1)} async-done(((bf16[96,1536]{1,0:T(8,128)(2,1)}), bf16[24,1536]{1,0:T(8,128)(2,1)}) %reduce-scatter.6.cloned.1.call-update) | async-done | bytes 73744 | tf_op jit(solution)/shard_map/reduce_scatter | solution.py:732
  204.4 1.2 copy-done.5
  205.6 6.0 %grads.1 = (bf16[512,768]{1,0:T(8,128)(2,1)}, bf16[384,896]{1,0:T(8,128)(2,1)}, bf16[384,896]{1,0:T(8,128)(2,1)}) custom-call(s32[1]{0:T(128)} %bitcast.c_ref, bf16[4,512,384]{2,1,0:T(8,128)(2,1)} %copy-done.5, bf16[512,256]{1,0:T(8,128)(2,1)} %get-tuple-element.95.dqn_ref, bf16[768,512]{1,0:T(8,128)(2,1)} %get-tuple-element.96.early_ref, ...), custom_call_target="tpu_custom_call" | custom-call | flops 2000000000 | bytes 8000000 | tf_op jit(solution)/shard_map/grads/pallas_call | solution.py:613
  212.6 1.3 collective-permute-done.3
  213.9 2.1 add_convert_fusion.1
  216.0 5.5 %all-to-all-start.7 = ((bf16[16,24,896]{2,1,0:T(8,128)(2,1)}), bf16[16,24,896]{2,1,0:T(8,128)(2,1)S(1)}, u32[]{:S(2)}, u32[]{:S(2)}) async-start(bf16[16,24,896]{2,1,0:T(8,128)(2,1)} %bitcast.47), calls=%async_computation.9 | async-start | bytes 1376256 | tf_op jit(solution)/shard_map/all_to_all | solution.py:642
  221.7 1.2 convolution_convert_fusion.1
  224.3 10.8 %all-to-all-done.7 = bf16[16,24,896]{2,1,0:T(8,128)(2,1)S(1)} async-done(((bf16[16,24,896]{2,1,0:T(8,128)(2,1)}), bf16[16,24,896]{2,1,0:T(8,128)(2,1)S(1)}, u32[]{:S(2)}, u32[]{:S(2)}) %all-to-all-start.7) | async-done | bytes 688160 | tf_op jit(solution)/shard_map/all_to_all | solution.py:642
  235.9 4.2 %all-to-all-start.8 = ((bf16[4,6,1600]{2,1,0:T(8,128)(2,1)}), bf16[4,6,1600]{2,1,0:T(8,128)(2,1)S(1)}, u32[]{:S(2)}, u32[]{:S(2)}) async-start(bf16[4,6,1600]{2,1,0:T(8,128)(2,1)} %pad_maximum_fusion.1), calls=%async_computation.10 | async-start | bytes 212992 | tf_op jit(solution)/shard_map/all_to_all | solution.py:642
  242.0 2.2 convolution_convert_fusion.2
  244.2 1.8 all-to-all-done.8
  (145 shorter events, 19.2 us)
Async XLA Ops:
  7.2 3.0 %copy-start = (bf16[768,768]{1,0:T(8,128)(2,1)S(1)}, bf16[768,768]{1,0:T(8,128)(2,1)}, u32[]{:S(2)}) copy-start(bf16[768,768]{1,0:T(8,128)(2,1)} %constant.42.clone.perm_ref) | copy-start | bytes 3538948
  7.2 3.0 %copy-start.12 = (bf16[6,768]{1,0:T(8,128)(2,1)S(1)}, bf16[6,768]{1,0:T(8,128)(2,1)}, u32[]{:S(2)}) copy-start(bf16[6,768]{1,0:T(8,128)(2,1)} %param.27) | copy-start | bytes 27652
  7.2 3.0 %copy-start.10 = (bf16[24,768]{1,0:T(8,128)(2,1)S(1)}, bf16[24,768]{1,0:T(8,128)(2,1)}, u32[]{:S(2)}) copy-start(bf16[24,768]{1,0:T(8,128)(2,1)} %param.33) | copy-start | bytes 110596
  7.2 35.6 %all-gather.7.cloned.1.call-start = ((), (), s32[]{:S(2)}) async-start(), calls=%async_computation.16 | async-start | bytes 1966080 | tf_op jit(solution)/shard_map/all_gather | solution.py:699
  7.3 3.2 %copy-start.9 = (bf16[6,3072]{1,0:T(8,128)(2,1)S(1)}, bf16[6,3072]{1,0:T(8,128)(2,1)}, u32[]{:S(2)}) copy-start(bf16[6,3072]{1,0:T(8,128)(2,1)} %param.31) | copy-start | bytes 110596
  10.1 1.3 copy-start.17
  10.1 1.3 copy-start.18
  10.1 1.3 copy-start.19
  10.5 12.5 %copy-start.14 = (bf16[24]{0:T(256)(128)(2,1)S(1)}, bf16[24]{0:T(256)(128)(2,1)}, u32[]{:S(2)}) copy-start(bf16[24]{0:T(256)(128)(2,1)} %param.32) | copy-start | bytes 148
  12.5 10.4 %all-to-all-start = ((bf16[4,6,2176]{2,1,0:T(8,128)(2,1)}), bf16[4,6,2176]{2,1,0:T(8,128)(2,1)S(1)}, u32[]{:S(2)}, u32[]{:S(2)}) async-start(bf16[4,6,2176]{2,1,0:T(8,128)(2,1)} %copy.93), calls=%async_computation | async-start | bytes 278528 | tf_op jit(solution)/shard_map/all_to_all | solution.py:642
  16.9 91.9 %all-gather.5.cloned.1.call-start = ((), (), s32[]{:S(2)}) async-start(), calls=%async_computation.12 | async-start | bytes 3649536 | tf_op jit(solution)/shard_map/all_gather | solution.py:710
  40.9 1.9 copy-start.7
  40.9 1.9 collective-permute-start
  48.9 26.4 %copy-start.13 = (s32[32,2]{0,1:T(2,128)S(1)}, s32[32,2]{0,1:T(2,128)}, u32[]{:S(2)}) copy-start(s32[32,2]{0,1:T(2,128)} %param.21) | copy-start | bytes 772
  75.3 4.0 %copy-start.4 = (bf16[4,512,384]{2,1,0:T(8,128)(2,1)}, bf16[4,512,384]{2,1,0:T(8,128)(2,1)S(1)}, u32[]{:S(2)}) copy-start(bf16[4,512,384]{2,1,0:T(8,128)(2,1)S(1)} %all_to_all.50) | copy-start | bytes 4718596
  75.3 3.4 %collective-permute-start.1 = (bf16[2048,384]{1,0:T(8,128)(2,1)S(1)}, bf16[2048,384]{1,0:T(8,128)(2,1)S(1)}, u32[]{:S(2)}, u32[]{:S(2)}) collective-permute-start(bf16[2048,384]{1,0:T(8,128)(2,1)S(1)} %bitcast.48), channel_id=1, source_target_pairs={{0,1},{1,0},{2,3},{3,2},{4,5},{5,4},{6,7},{7,6},{8,9},{9,8},{10,11... | collective-permute-start | bytes 4718600 | tf_op jit(solution)/shard_map/ppermute | solution.py:715
  76.1 3.2 %copy-start.26 = (s32[8]{0:T(128)}, s32[8]{0:T(128)S(1)}, u32[]{:S(2)}) copy-start(s32[8]{0:T(128)S(1)} %convert_reduce_fusion.3.rank) | copy-start | bytes 100
  118.8 14.7 %all-to-all-start.3 = ((bf16[4,128,768]{2,1,0:T(8,128)(2,1)}), bf16[4,128,768]{2,1,0:T(8,128)(2,1)S(1)}, u32[]{:S(2)}, u32[]{:S(2)}) async-start(bf16[4,128,768]{2,1,0:T(8,128)(2,1)} %get-tuple-element.73), calls=%async_computation.3 | async-start | bytes 1572864 | tf_op jit(solution)/shard_map/all_to_all | solution.py:642
  122.3 48.5 %reduce-scatter.4.cloned.1.call-start = ((), (), s32[]{:S(2)}) async-start(), calls=%async_computation.13 | async-start | bytes 2654208 | tf_op jit(solution)/shard_map/reduce_scatter | solution.py:724
  150.5 20.3 %all-to-all-start.5 = ((bf16[4,128,768]{2,1,0:T(8,128)(2,1)}), bf16[4,128,768]{2,1,0:T(8,128)(2,1)S(1)}, u32[]{:S(2)}, u32[]{:S(2)}) async-start(bf16[4,128,768]{2,1,0:T(8,128)(2,1)} %bitcast.13), calls=%async_computation.5 | async-start | bytes 1572864 | tf_op jit(solution)/shard_map/all_to_all | solution.py:642
  170.9 3.7 %collective-permute-start.2 = (bf16[2048,384]{1,0:T(8,128)(2,1)}, bf16[2048,384]{1,0:T(8,128)(2,1)S(1)}, u32[]{:S(2)}, u32[]{:S(2)}) collective-permute-start(bf16[2048,384]{1,0:T(8,128)(2,1)} %get-tuple-element.89), channel_id=1, source_target_pairs={{0,1},{1,0},{2,3},{3,2},{4,5},{5,4},{6,7},{7,6},{8,9},{9,8},{10,11... | collective-permute-start | bytes 4718600 | tf_op jit(solution)/shard_map/ppermute | solution.py:733
  177.5 4.3 %copy-start.2 = (bf16[256,768]{1,0:T(8,128)(2,1)S(1)}, bf16[256,768]{1,0:T(8,128)(2,1)}, u32[]{:S(2)}) copy-start(bf16[256,768]{1,0:T(8,128)(2,1)} %convolution_convert_fusion.dy_ref) | copy-start | bytes 1179652
  177.5 26.9 %all-to-all-start.6 = ((bf16[4,512,384]{2,1,0:T(8,128)(2,1)}), bf16[4,512,384]{2,1,0:T(8,128)(2,1)S(1)}, u32[]{:S(2)}, u32[]{:S(2)}) async-start(bf16[4,512,384]{2,1,0:T(8,128)(2,1)} %bitcast.14), calls=%async_computation.7 | async-start | bytes 3145728 | tf_op jit(solution)/shard_map/all_to_all | solution.py:642
  181.2 23.2 %reduce-scatter.6.cloned.1.call-start = ((), (), s32[]{:S(2)}) async-start(), calls=%async_computation.14 | async-start | bytes 368640 | tf_op jit(solution)/shard_map/reduce_scatter | solution.py:732
  181.8 59.0 %reduce-scatter.8.cloned.1.call-start = ((), (), s32[]{:S(2)}) async-start(), calls=%async_computation.15 | async-start | bytes 983040 | tf_op jit(solution)/shard_map/reduce_scatter | solution.py:744
  211.6 2.4 collective-permute-start.3
  216.0 5.6 %copy-start.1 = (bf16[768,768]{1,0:T(8,128)(2,1)S(1)}, bf16[768,768]{1,0:T(8,128)(2,1)}, u32[]{:S(2)}) copy-start(bf16[768,768]{1,0:T(8,128)(2,1)} %constant.42.clone.perm_ref) | copy-start | bytes 3538948
  216.0 5.6 %copy-start.6 = (f32[128,768]{1,0:T(8,128)S(1)}, f32[128,768]{1,0:T(8,128)}, u32[]{:S(2)}) copy-start(f32[128,768]{1,0:T(8,128)} %get-tuple-element.79.resid_ref) | copy-start | bytes 1179652
  216.0 19.0 %all-to-all-start.7 = ((bf16[16,24,896]{2,1,0:T(8,128)(2,1)}), bf16[16,24,896]{2,1,0:T(8,128)(2,1)S(1)}, u32[]{:S(2)}, u32[]{:S(2)}) async-start(bf16[16,24,896]{2,1,0:T(8,128)(2,1)} %bitcast.47), calls=%async_computation.9 | async-start | bytes 1376256 | tf_op jit(solution)/shard_map/all_to_all | solution.py:642
  221.5 1.4 copy-start.8
  222.9 19.1 %copy-start.25 = (f32[128,768]{1,0:T(8,128)S(1)}, f32[128,768]{1,0:T(8,128)}, u32[]{:S(2)}) copy-start(f32[128,768]{1,0:T(8,128)} %get-tuple-element.103) | copy-start | bytes 1179652
  235.9 10.1 %all-to-all-start.8 = ((bf16[4,6,1600]{2,1,0:T(8,128)(2,1)}), bf16[4,6,1600]{2,1,0:T(8,128)(2,1)S(1)}, u32[]{:S(2)}, u32[]{:S(2)}) async-start(bf16[4,6,1600]{2,1,0:T(8,128)(2,1)} %pad_maximum_fusion.1), calls=%async_computation.10 | async-start | bytes 212992 | tf_op jit(solution)/shard_map/all_to_all | solution.py:642
  (10 other events, 11.4 us)
Sparse Core Ops, SparseCore 0:
  10.3 28.9 all-gather.6
  42.9 47.6 all-gather.4
  133.6 32.5 reduce-scatter.3
  184.1 20.2 reduce-scatter.5
  211.9 22.1 reduce-scatter.7
